TPU v7x, 32 devices: a whole 2x2x4 slice. The times are simulated.
32 devices in a mesh: dp: 4 (over x, core), tensor: 8 (over z, y).
Axes of the slice: x: 2, y: 2, z: 4, core: 2. Of those that a mesh axis runs over, the one named last changes fastest.
Arguments:
- tokens: bfloat16 [4096, 2048], P(('dp', 'tensor')), may hold values from -6 to 6
- segments: int32 [4, 1024], P('dp'), may hold values from 0 to 4, as said below
- routes: int32 [4096, 8], P(('dp', 'tensor')), may hold values from 0 to 15, all different within a row; in each aligned block of 128 rows (0 to 127, 128 to 255, ...) at most 80 rows name the same one
- gate_values: bfloat16 [4096, 8], P(('dp', 'tensor')), may hold values from 0.039794922 to 0.25
- cotangent: bfloat16 [4096, 2048], P(('dp', 'tensor')), may hold values from -6 to 6
- query_key_value: bfloat16 [3, 2048, 2048], P(None, 'dp', 'tensor'), may hold values from -0.125 to 0.125
- out_weight: bfloat16 [2048, 2048], P('tensor', 'dp'), may hold values from -1 to 1
- head_gain: bfloat16 [2, 16, 128], P(None, 'tensor', 'dp'), may hold values from 0.25 to 1.75
- layer_gain: bfloat16 [2, 2048], P(None, 'dp'), may hold values from 0.25 to 1.75
- gate_up: bfloat16 [16, 2, 2048, 1024], P(None, None, 'dp', 'tensor'), may hold values from -0.125 to 0.125
- down_weight: bfloat16 [16, 1024, 2048], P(None, 'tensor', 'dp'), may hold values from -0.75 to 0.75
Outputs:
- mixed: bfloat16 [4096, 2048], P(('dp', 'tensor'))
- input_grad: float32 [4096, 2048], P(('dp', 'tensor'))
- gate_grad: float32 [4096, 8], P(('dp', 'tensor'))
- query_key_value_grad: float32 [3, 2048, 2048], P(None, 'dp', 'tensor')
- out_weight_grad: float32 [2048, 2048], P('tensor', 'dp')
- head_gain_grad: float32 [2, 16, 128], P(None, 'tensor', 'dp')
- layer_gain_grad: float32 [2, 2048], P(None, ('dp', 'tensor'))
- gate_up_grad: float32 [16, 2, 2048, 1024], P(None, None, 'dp', 'tensor')
- down_weight_grad: float32 [16, 1024, 2048], P(None, 'tensor', 'dp')
Inputs may be any that keep to these rules, and one draw needn't show every extreme that they name: `segments`: each row never falls; one document of each row begins within its first 128 positions and ends within its last 128. `routes`: within the 128 rows of one aligned block no expert is named more than 80 times, and each row names 8 different experts.
All inputs are finite; a program needn't handle non-finite values.
Results may differ from a plain program's by a relative error of at most 0.014.
Values may be sent and summed in bfloat16 or wider, within the bound.
No kernel may reach another device: no remote copies, remote signals or barrier semaphores. Data moves between devices by JAX's collectives and lax.ppermute only.
A program may use at most 448 MiB of HBM per device.

v0:
```python
import jax
import jax.numpy as jnp
from jax import lax
from jax.sharding import PartitionSpec as P

D = 2048
HD = 128
E = 16


EPSILON = 1e-05
ROPE_BASE = 10000.0
MASKED = -1e30


def turn_half(values_in):
    half_width = values_in.shape[-1] // 2
    return jnp.concatenate([-values_in[..., half_width:], values_in[..., :half_width]], axis=-1)


def rope_tables(length, head_size):
    positions = jnp.arange(length, dtype=jnp.float32)
    inverse_freq = ROPE_BASE ** (-jnp.arange(head_size // 2, dtype=jnp.float32) * 2.0 / head_size)
    phases = positions[:, None] * inverse_freq[None, :]
    phases = jnp.concatenate([phases, phases], axis=-1)
    return (jnp.cos(phases)[:, None, :], jnp.sin(phases)[:, None, :])


def local_slots(routes, experts, capacity):
    flat_routes = routes.reshape(-1)
    chosen = (flat_routes[:, None] == jnp.arange(experts, dtype=jnp.int32)[None, :]).astype(
        jnp.int32
    )
    earlier = jnp.cumsum(chosen, axis=0) - chosen
    within = jnp.sum(earlier * chosen, axis=1)
    return (flat_routes * capacity + within).reshape(routes.shape)


def per_device(
    tokens,
    segments,
    routes,
    gate_values,
    cotangent,
    query_key_value,
    out_weight,
    head_gain,
    layer_gain,
    gate_up,
    down_weight,
):
    groups = lax.axis_size("tensor")
    own_rows = tokens.shape[0]
    seq_len = own_rows * groups
    top_k = routes.shape[1]
    capacity = own_rows * top_k * 5 // (4 * E)
    slot_count = E * capacity
    local_width = query_key_value.shape[2]
    local_heads = local_width // HD
    block_rows = min(512, seq_len)
    blocks_count = seq_len // block_rows
    scale_qk = HD ** (-0.5)
    f32 = jnp.float32
    bf16 = jnp.bfloat16
    qkv_full, out_full, head_full, gain_full, gate_up_full, down_full = (
        lax.all_gather(query_key_value, "dp", axis=1, tiled=True),
        lax.all_gather(out_weight, "dp", axis=1, tiled=True),
        lax.all_gather(head_gain, "dp", axis=2, tiled=True),
        lax.all_gather(layer_gain, "dp", axis=1, tiled=True),
        lax.all_gather(gate_up, "dp", axis=2, tiled=True),
        lax.all_gather(down_weight, "dp", axis=2, tiled=True),
    )
    x_rows = tokens.astype(f32)
    inv_in = lax.rsqrt(jnp.mean(x_rows * x_rows, axis=-1, keepdims=True) + EPSILON)
    x_hat = x_rows * inv_in
    gain_in = gain_full[0].astype(f32)
    gain_mid = gain_full[1].astype(f32)
    normed_in = lax.all_gather((x_hat * gain_in).astype(bf16), "tensor", axis=0, tiled=True)
    projected = jnp.einsum("sd,jdc->jsc", normed_in, qkv_full, preferred_element_type=f32)
    query_raw = projected[0].reshape(seq_len, local_heads, HD)
    key_raw = projected[1].reshape(seq_len, local_heads, HD)
    values_b = projected[2].astype(bf16).reshape(seq_len, local_heads, HD)
    inv_query = lax.rsqrt(jnp.mean(query_raw * query_raw, axis=-1, keepdims=True) + EPSILON)
    inv_key = lax.rsqrt(jnp.mean(key_raw * key_raw, axis=-1, keepdims=True) + EPSILON)
    query_hat = query_raw * inv_query
    key_hat = key_raw * inv_key
    gain_query = head_full[0].astype(f32)
    gain_key = head_full[1].astype(f32)
    cosine_table, sine_table = rope_tables(seq_len, HD)
    query_in = query_hat * gain_query
    key_in = key_hat * gain_key
    queries = (query_in * cosine_table + turn_half(query_in) * sine_table).astype(bf16)
    keys_b = (key_in * cosine_table + turn_half(key_in) * sine_table).astype(bf16)
    seg_ids = segments.reshape(seq_len)
    key_pos = jnp.arange(seq_len, dtype=jnp.int32)

    def block_scores(query_block, first_row):
        raw_scores = (
            jnp.einsum("qhd,khd->hqk", query_block, keys_b, preferred_element_type=f32) * scale_qk
        )
        row_pos = first_row + jnp.arange(query_block.shape[0], dtype=jnp.int32)
        row_segs = lax.dynamic_slice_in_dim(seg_ids, first_row, query_block.shape[0])
        allowed = (row_segs[:, None] == seg_ids[None, :]) & (key_pos[None, :] <= row_pos[:, None])
        return jnp.where(allowed[None], raw_scores, MASKED)

    def attend(block_index):
        first_row = block_index * block_rows
        query_block = lax.dynamic_slice_in_dim(queries, first_row, block_rows, 0)
        scores = block_scores(query_block, first_row)
        row_max = jnp.max(scores, axis=-1, keepdims=True)
        weights_exp = jnp.exp(scores - row_max)
        row_total = jnp.sum(weights_exp, axis=-1, keepdims=True)
        probs_b = (weights_exp / row_total).astype(bf16)
        context_block = jnp.einsum("hqk,khd->qhd", probs_b, values_b, preferred_element_type=f32)
        return (context_block.astype(bf16), (row_max + jnp.log(row_total))[..., 0])

    context_blocks, log_totals = lax.map(attend, jnp.arange(blocks_count))
    context = context_blocks.reshape(seq_len, local_width)
    attention = lax.psum_scatter(
        jnp.dot(context, out_full, preferred_element_type=f32),
        "tensor",
        scatter_dimension=0,
        tiled=True,
    )
    middle = x_rows + attention
    inv_mid = lax.rsqrt(jnp.mean(middle * middle, axis=-1, keepdims=True) + EPSILON)
    mid_hat = middle * inv_mid
    slot_ids = local_slots(routes, E, capacity)
    slot_range = jnp.arange(slot_count, dtype=jnp.int32)
    slot_picks = (slot_ids[:, :, None] == slot_range[None, None, :]).astype(f32)
    dispatch_own = jnp.sum(slot_picks, axis=1).astype(bf16)
    combine_own = jnp.sum(slot_picks * gate_values.astype(f32)[:, :, None], axis=1).astype(bf16)
    normed_mid, dispatch_all, combine_all = (
        lax.all_gather((mid_hat * gain_mid).astype(bf16), "tensor", axis=0, tiled=True),
        lax.all_gather(dispatch_own, "tensor", axis=0, tiled=True),
        lax.all_gather(combine_own, "tensor", axis=0, tiled=True),
    )
    dispatch_four = dispatch_all.reshape(groups, own_rows, E, capacity)
    combine_four = combine_all.reshape(groups, own_rows, E, capacity)
    expert_rows = (
        jnp.einsum(
            "ntec,ntd->encd",
            dispatch_four,
            normed_mid.reshape(groups, own_rows, D),
            preferred_element_type=f32,
        )
        .astype(bf16)
        .reshape(E, groups * capacity, D)
    )
    gate_up_out = jnp.einsum(
        "erd,egdf->gerf", expert_rows, gate_up_full, preferred_element_type=f32
    )
    gate_part = gate_up_out[0]
    up_part = gate_up_out[1]
    gate_sigmoid = jax.nn.sigmoid(gate_part)
    gate_swish = gate_part * gate_sigmoid
    hidden = (gate_swish * up_part).astype(bf16)
    expert_out = jnp.einsum("erf,efd->erd", hidden, down_full, preferred_element_type=f32).astype(
        bf16
    )
    expert_four = expert_out.reshape(E, groups, capacity, D)
    moe_terms = jnp.einsum(
        "ntec,encd->ntd", combine_four, expert_four, preferred_element_type=f32
    ).reshape(seq_len, D)
    moe_rows = lax.psum_scatter(moe_terms, "tensor", scatter_dimension=0, tiled=True)
    layer_out = (middle + moe_rows).astype(bf16)
    d_out = cotangent.astype(f32)
    d_all = lax.all_gather(cotangent, "tensor", axis=0, tiled=True).reshape(groups, own_rows, D)
    qkv_full, out_full, head_full, gain_full, gate_up_full, down_full = (
        lax.all_gather(query_key_value, "dp", axis=1, tiled=True),
        lax.all_gather(out_weight, "dp", axis=1, tiled=True),
        lax.all_gather(head_gain, "dp", axis=2, tiled=True),
        lax.all_gather(layer_gain, "dp", axis=1, tiled=True),
        lax.all_gather(gate_up, "dp", axis=2, tiled=True),
        lax.all_gather(down_weight, "dp", axis=2, tiled=True),
    )
    d_expert = (
        jnp.einsum("ntec,ntd->encd", combine_four, d_all, preferred_element_type=f32)
        .astype(bf16)
        .reshape(E, groups * capacity, D)
    )
    d_combine = jnp.einsum(
        "encd,ntd->ntec", expert_four, d_all, preferred_element_type=f32
    ).reshape(seq_len, slot_count)
    d_hidden = jnp.einsum("erd,efd->erf", d_expert, down_full, preferred_element_type=f32)
    d_gate = (d_hidden * up_part * gate_sigmoid * (1.0 + gate_part * (1.0 - gate_sigmoid))).astype(
        bf16
    )
    d_up = (d_hidden * gate_swish).astype(bf16)
    d_gate_up = jnp.stack([d_gate, d_up])
    down_grad = jnp.einsum("erf,erd->efd", hidden, d_expert, preferred_element_type=f32)
    gate_up_grad = jnp.einsum("erd,gerf->egdf", expert_rows, d_gate_up, preferred_element_type=f32)
    d_rows = (
        jnp.einsum("gerf,egdf->erd", d_gate_up, gate_up_full, preferred_element_type=f32)
        .astype(bf16)
        .reshape(E, groups, capacity, D)
    )
    d_mid_terms = jnp.einsum(
        "ntec,encd->ntd", dispatch_four, d_rows, preferred_element_type=f32
    ).reshape(seq_len, D)
    d_normed_mid, d_combine_own = (
        lax.psum_scatter(d_mid_terms, "tensor", scatter_dimension=0, tiled=True),
        lax.psum_scatter(d_combine, "tensor", scatter_dimension=0, tiled=True),
    )
    gate_grad = jnp.sum(slot_picks * d_combine_own[:, None, :], axis=-1)
    gain_mid_part = jnp.sum(d_normed_mid * mid_hat, axis=0)
    d_mid_hat = d_normed_mid * gain_mid
    d_middle = d_out + inv_mid * (
        d_mid_hat - mid_hat * jnp.mean(d_mid_hat * mid_hat, axis=-1, keepdims=True)
    )
    d_branch = lax.all_gather(d_middle.astype(bf16), "tensor", axis=0, tiled=True)
    out_weight_grad = jnp.einsum("sc,sd->cd", context, d_branch, preferred_element_type=f32)
    d_context = (
        jnp.einsum("sd,cd->sc", d_branch, out_full, preferred_element_type=f32)
        .astype(bf16)
        .reshape(seq_len, local_heads, HD)
    )

    def attend_back(carried, block_index):
        key_acc, value_acc = carried
        first_row = block_index * block_rows
        query_block = lax.dynamic_slice_in_dim(queries, first_row, block_rows, 0)
        d_block = lax.dynamic_slice_in_dim(d_context, first_row, block_rows, 0)
        totals_block = log_totals[block_index]
        prob_block = jnp.exp(block_scores(query_block, first_row) - totals_block[..., None])
        value_acc = value_acc + jnp.einsum(
            "hqk,qhd->khd", prob_block.astype(bf16), d_block, preferred_element_type=f32
        )
        d_probs = jnp.einsum("qhd,khd->hqk", d_block, values_b, preferred_element_type=f32)
        d_scores = (
            prob_block * (d_probs - jnp.sum(prob_block * d_probs, axis=-1, keepdims=True))
        ).astype(bf16)
        d_query_block = (
            jnp.einsum("hqk,khd->qhd", d_scores, keys_b, preferred_element_type=f32) * scale_qk
        )
        key_acc = (
            key_acc
            + jnp.einsum("hqk,qhd->khd", d_scores, query_block, preferred_element_type=f32)
            * scale_qk
        )
        return ((key_acc, value_acc), d_query_block)

    zero_field = jnp.zeros((seq_len, local_heads, HD), f32)
    (d_keys, d_values), d_query_blocks = lax.scan(
        attend_back, (zero_field, zero_field), jnp.arange(blocks_count)
    )
    d_queries = d_query_blocks.reshape(seq_len, local_heads, HD)
    d_query_in = d_queries * cosine_table - turn_half(d_queries) * sine_table
    d_key_in = d_keys * cosine_table - turn_half(d_keys) * sine_table
    head_grad_part = jnp.stack(
        [jnp.sum(d_query_in * query_hat, axis=0), jnp.sum(d_key_in * key_hat, axis=0)]
    )
    d_query_hat = d_query_in * gain_query
    d_key_hat = d_key_in * gain_key
    d_query_raw = inv_query * (
        d_query_hat - query_hat * jnp.mean(d_query_hat * query_hat, axis=-1, keepdims=True)
    )
    d_key_raw = inv_key * (
        d_key_hat - key_hat * jnp.mean(d_key_hat * key_hat, axis=-1, keepdims=True)
    )
    d_projected = jnp.stack(
        [
            d_query_raw.reshape(seq_len, local_width).astype(bf16),
            d_key_raw.reshape(seq_len, local_width).astype(bf16),
            d_values.reshape(seq_len, local_width).astype(bf16),
        ]
    )
    qkv_grad = jnp.einsum("sd,jsc->jdc", normed_in, d_projected, preferred_element_type=f32)
    d_normed_in = lax.psum_scatter(
        jnp.einsum("jsc,jdc->sd", d_projected, qkv_full, preferred_element_type=f32),
        "tensor",
        scatter_dimension=0,
        tiled=True,
    )
    gain_in_part = jnp.sum(d_normed_in * x_hat, axis=0)
    d_x_hat = d_normed_in * gain_in
    input_grad = d_middle + inv_in * (
        d_x_hat - x_hat * jnp.mean(d_x_hat * x_hat, axis=-1, keepdims=True)
    )
    layer_gain_grad = lax.psum_scatter(
        jnp.stack([gain_in_part, gain_mid_part]), ("dp", "tensor"), scatter_dimension=1, tiled=True
    )
    qkv_shard, out_shard, head_shard, gate_up_shard, down_shard = (
        lax.psum_scatter(qkv_grad, "dp", scatter_dimension=1, tiled=True),
        lax.psum_scatter(out_weight_grad, "dp", scatter_dimension=1, tiled=True),
        lax.psum_scatter(head_grad_part, "dp", scatter_dimension=2, tiled=True),
        lax.psum_scatter(gate_up_grad, "dp", scatter_dimension=2, tiled=True),
        lax.psum_scatter(down_grad, "dp", scatter_dimension=2, tiled=True),
    )
    return (
        layer_out,
        input_grad,
        gate_grad,
        qkv_shard,
        out_shard,
        head_shard,
        layer_gain_grad,
        gate_up_shard,
        down_shard,
    )


def solution(mesh):
    return jax.shard_map(
        per_device,
        mesh=mesh,
        in_specs=(
            P(("dp", "tensor"), None),
            P("dp", None),
            P(("dp", "tensor"), None),
            P(("dp", "tensor"), None),
            P(("dp", "tensor"), None),
            P(None, "dp", "tensor"),
            P("tensor", "dp"),
            P(None, "tensor", "dp"),
            P(None, "dp"),
            P(None, None, "dp", "tensor"),
            P(None, "tensor", "dp"),
        ),
        out_specs=(
            P(("dp", "tensor"), None),
            P(("dp", "tensor"), None),
            P(("dp", "tensor"), None),
            P(None, "dp", "tensor"),
            P("tensor", "dp"),
            P(None, "tensor", "dp"),
            P(None, ("dp", "tensor")),
            P(None, None, "dp", "tensor"),
            P(None, "tensor", "dp"),
        ),
        check_vma=False,
    )
```

profile of v0, /device:TPU:0, one launch (start us, length us, event | category | flops | bytes accessed | tf_op | source)
XLA Modules:
  0.0 2197.4 jit_solution(9846350422120196178)
XLA Ops:
  41.8 76.1 %all-gather.11.cloned.1.call-done = bf16[1024,2048]{1,0:T(8,128)(2,1)} async-done(((bf16[128,2048]{1,0:T(8,128)(2,1)}), bf16[1024,2048]{1,0:T(8,128)(2,1)}) %all-gather.11.cloned.1.call-update) | async-done | bytes 4194320 | tf_op jit(solution)/shard_map/all_gather | solution.py:78
  161.6 138.1 %reduce-scatter.16.cloned.1.call-done = f32[128,2048]{1,0:T(8,128)} async-done(((f32[1024,2048]{1,0:T(8,128)}), f32[128,2048]{1,0:T(8,128)}) %reduce-scatter.16.cloned.1.call-update) | async-done | bytes 1048592 | tf_op jit(solution)/shard_map/reduce_scatter | solution.py:119
  305.4 50.8 %all-gather.21.cloned.1.call-done = bf16[1024,1280]{1,0:T(8,128)(2,1)} async-done(((bf16[128,1280]{1,0:T(8,128)(2,1)}), bf16[1024,1280]{1,0:T(8,128)(2,1)}) %all-gather.21.cloned.1.call-update) | async-done | bytes 2621456 | tf_op jit(solution)/shard_map/all_gather | solution.py:135
  370.1 60.9 %all-gather.19.cloned.1.call-done = bf16[1024,2048]{1,0:T(8,128)(2,1)} async-done(((bf16[128,2048]{1,0:T(8,128)(2,1)}), bf16[1024,2048]{1,0:T(8,128)(2,1)}) %all-gather.19.cloned.1.call-update) | async-done | bytes 4194320 | tf_op jit(solution)/shard_map/all_gather | solution.py:134
  431.0 37.9 %fusion.110 = f32[8,2048,1280]{1,2,0} fusion(bf16[8,128,1280]{1,2,0:T(8,128)(2,1)S(1)} %bitcast.267, bf16[8,128,2048]{2,1,0:T(8,128)(2,1)} %bitcast.277), kind=kOutput, calls=%fused_computation.189 | convolution fusion | flops 5368709120 | bytes 90701824
  468.9 40.7 %convert_bitcast_fusion.1 = bf16[16,8,80,2048]{3,2,0,1:T(8,128)(2,1)} fusion(f32[8,2048,16,80]{1,3,2,0:T(8,128)} %bitcast.14), kind=kLoop, calls=%fused_computation.57 | loop fusion | flops 20971520 | bytes 125829120 | tf_op jit(solution)/shard_map/convert_element_type | solution.py:147
  509.7 28.2 %copy.272 = bf16[16,8,80,2048]{3,2,1,0:T(8,128)(2,1)} copy(bf16[16,8,80,2048]{3,2,0,1:T(8,128)(2,1)} %convert_bitcast_fusion.1) | data formatting | bytes 83886080 | tf_op jit(solution)/shard_map/convert_element_type | solution.py:147
  537.8 28.6 %convolution_bitcast_fusion.2 = f32[2,16,640,128]{3,2,0,1:T(8,128)} fusion(bf16[16,640,2048,1]{2,1,3,0:T(8,128)(2,1)} %bitcast.256, bf16[16,2,2048,128]{3,2,1,0:T(8,128)(2,1)} %all-gather.23.cloned.1.call-done), kind=kOutput, calls=%fused_computation.85 | convolution fusion | flops 10737418240 | bytes 69206016 | tf_op jit(solution)/shard_map/erd,egdf->gerf/dot_general | solution.py:150
  571.4 25.4 %all-gather.25.cloned.1.call-done = bf16[16,128,2048]{2,1,0:T(8,128)(2,1)} async-done(((bf16[16,128,512]{2,1,0:T(8,128)(2,1)}), bf16[16,128,2048]{2,1,0:T(8,128)(2,1)}) %all-gather.25.cloned.1.call-update) | async-done | bytes 8388624 | tf_op jit(solution)/shard_map/all_gather | solution.py:71
  596.8 20.6 convolution_convert_fusion
  617.4 55.2 %all-gather.27.cloned.1.call-done = bf16[1024,2048]{1,0:T(8,128)(2,1)} async-done(((bf16[128,2048]{1,0:T(8,128)(2,1)}), bf16[1024,2048]{1,0:T(8,128)(2,1)}) %all-gather.27.cloned.1.call-update) | async-done | bytes 4194320 | tf_op jit(solution)/shard_map/all_gather | solution.py:168
  672.6 18.6 fusion.63
  698.7 100.8 %reduce-scatter.24.cloned.1.call-done = f32[128,1280]{0,1:T(8,128)} async-done(((f32[1024,1280]{0,1:T(8,128)}), f32[128,1280]{0,1:T(8,128)}) %reduce-scatter.24.cloned.1.call-update) | async-done | bytes 655376 | tf_op jit(solution)/shard_map/reduce_scatter | solution.py:203
  804.0 54.5 %all-gather.17.cloned.1.call-done = bf16[1024,1280]{1,0:T(8,128)(2,1)} async-done(((bf16[128,1280]{1,0:T(8,128)(2,1)}), bf16[1024,1280]{1,0:T(8,128)(2,1)}) %all-gather.17.cloned.1.call-update) | async-done | bytes 2621456 | tf_op jit(solution)/shard_map/all_gather | solution.py:136
  872.6 20.3 convert_bitcast_fusion
  892.8 28.1 %copy.277 = bf16[16,8,80,2048]{3,2,1,0:T(8,128)(2,1)} copy(bf16[16,8,80,2048]{3,2,0,1:T(8,128)(2,1)} %convert_bitcast_fusion) | data formatting | bytes 83886080 | tf_op jit(solution)/shard_map/convert_element_type | solution.py:179
  921.0 23.9 %fusion.62 = (bf16[1,16,640,128]{3,2,1,0:T(8,128)(2,1)S(1)}, bf16[1,16,640,128]{3,2,1,0:T(8,128)(2,1)}) fusion(f32[2,16,640,128]{3,2,0,1:T(8,128)} %convolution_bitcast_fusion.2, bf16[16,640,2048]{2,1,0:T(8,128)(2,1)} %bitcast.258, bf16[16,128,2048]{2,1,0:T(8,128)(2,1)} %all-gather.25.cloned.1.call-done), kind=kOutput, calls=%fused_computation.87 | convolution fusion | flops 5385748480 | bytes 66060288 | tf_op jit(solution)/shard_map/erd,efd->erf/dot_general | solution.py:185
  944.8 24.1 %bitcast_convert_fusion = bf16[16,640,2048]{2,1,0:T(8,128)(2,1)} fusion(bf16[16,2,2048,128]{3,2,1,0:T(8,128)(2,1)} %all-gather.23.cloned.1.call-done, bf16[1,16,640,128]{3,2,1,0:T(8,128)(2,1)} %get-tuple-element.437, bf16[1,16,640,128]{3,2,1,0:T(8,128)(2,1)S(1)} %get-tuple-element.436), kind=kOutput, calls=%fused_computation.53 | convolution fusion | flops 10761011200 | bytes 63963136 | tf_op jit(solution)/shard_map/gerf,egdf->erd/dot_general | solution.py:194
  969.0 18.7 fusion.45
  987.8 147.7 %reduce-scatter.20.cloned.1.call-done = f32[128,2048]{1,0:T(8,128)} async-done(((f32[1024,2048]{1,0:T(8,128)}), f32[128,2048]{1,0:T(8,128)}) %reduce-scatter.20.cloned.1.call-update) | async-done | bytes 1048592 | tf_op jit(solution)/shard_map/reduce_scatter | solution.py:202
  1152.6 60.0 %all-gather.29.cloned.1.call-done = bf16[1024,2048]{1,0:T(8,128)(2,1)} async-done(((bf16[128,2048]{1,0:T(8,128)(2,1)}), bf16[1024,2048]{1,0:T(8,128)(2,1)}) %all-gather.29.cloned.1.call-update) | async-done | bytes 4194320 | tf_op jit(solution)/shard_map/all_gather | solution.py:211
  1216.4 25.0 %while.29 = (s32[]{:T(128)}, f32[1024,2,128]{0,2,1:T(8,128)S(1)}, f32[1024,2,128]{0,2,1:T(8,128)}, f32[2,512,2,128]{3,1,2,0:T(8,128)}, s32[2]{0:T(128)S(1)}, /*i...) while((s32[]{:T(128)}, f32[1024,2,128]{0,2,1:T(8,128)S(1)}, ...), condition=%wide.region_19.20_spmd.clone, body=%wide.region_17.19_spmd.clone.sunk | while | flops 1360920064 | bytes 57715096 | solution.py:244
  1283.5 19.6 fusion.49
  1303.2 117.5 %reduce-scatter.22.cloned.1.call-done = f32[128,2048]{1,0:T(8,128)} async-done(((f32[1024,2048]{1,0:T(8,128)}), f32[128,2048]{1,0:T(8,128)}) %reduce-scatter.22.cloned.1.call-update) | async-done | bytes 1048592 | tf_op jit(solution)/shard_map/reduce_scatter | solution.py:269
  1423.7 29.9 %convolution_bitcast_fusion = f32[16,2,2048,128]{2,3,1,0:T(8,128)} fusion(bf16[16,640,2048,1]{2,1,3,0:T(8,128)(2,1)} %bitcast.257, bf16[1,16,640,128]{3,2,1,0:T(8,128)(2,1)} %get-tuple-element.437, bf16[1,16,640,128]{3,2,1,0:T(8,128)(2,1)S(1)} %copy-done.18), kind=kOutput, calls=%fused_computation.63 | convolution fusion | flops 10740039680 | bytes 80740352 | tf_op jit(solution)/shard_map/erd,gerf->egdf/dot_general | solution.py:192
  1459.6 23.6 %fusion.109 = f32[16,128,2048]{2,1,0:T(8,128)} fusion(bf16[16,640,128]{2,1,0:T(8,128)(2,1)S(1)} %copy-done.5, bf16[16,640,2048]{2,1,0:T(8,128)(2,1)} %bitcast.259), kind=kOutput, calls=%fused_computation.188 | convolution fusion | flops 5368709120 | bytes 61341696 | tf_op jit(solution)/shard_map/erf,erd->efd/dot_general | solution.py:191
  1486.2 16.6 reduce-scatter.26.cloned.1.call-done
  1505.8 149.9 %reduce-scatter.18.cloned.1.call-done = f32[128,2048]{1,0:T(8,128)} async-done(((f32[1024,2048]{1,0:T(8,128)}), f32[128,2048]{1,0:T(8,128)}) %reduce-scatter.18.cloned.1.call-update) | async-done | bytes 1048592 | tf_op jit(solution)/shard_map/reduce_scatter | solution.py:165
  1658.9 133.6 %reduce-scatter.36.cloned.1.call-done = f32[64,2]{1,0:T(8,128)} async-done(((f32[2048,2]{1,0:T(8,128)}), f32[64,2]{1,0:T(8,128)}) %reduce-scatter.36.cloned.1.call-update) | async-done | bytes 528
  1793.9 232.5 %reduce-scatter.30.cloned.1.call-done = f32[16,2,512,128]{2,3,1,0:T(8,128)} async-done(((f32[16,2,2048,128]{2,3,1,0:T(8,128)}), f32[16,2,512,128]{2,3,1,0:T(8,128)}) %reduce-scatter.30.cloned.1.call-update) | async-done | bytes 8388624 | tf_op jit(solution)/shard_map/reduce_scatter | solution.py:287
  2035.7 25.3 %reduce-scatter.28.cloned.1.call-done = f32[256,512]{1,0:T(8,128)} async-done(((f32[256,2048]{1,0:T(8,128)}), f32[256,512]{1,0:T(8,128)}) %reduce-scatter.28.cloned.1.call-update) | async-done | bytes 524304 | tf_op jit(solution)/shard_map/reduce_scatter | solution.py:285
  2061.0 129.3 %reduce-scatter.32.cloned.1.call-done = f32[16,128,512]{2,1,0:T(8,128)} async-done(((f32[16,128,2048]{2,1,0:T(8,128)}), f32[16,128,512]{2,1,0:T(8,128)}) %reduce-scatter.32.cloned.1.call-update) | async-done | bytes 4194320 | tf_op jit(solution)/shard_map/reduce_scatter | solution.py:288
  (367 shorter events, 250.0 us)
Async XLA Ops:
  7.2 34.6 %all-gather.13.cloned.1.call-start = ((), (), s32[]{:S(2)}) async-start(), calls=%async_computation.12 | async-start | bytes 3932160 | tf_op jit(solution)/shard_map/all_gather | solution.py:66
  9.5 108.4 %all-gather.11.cloned.1.call-start = ((), (), s32[]{:S(2)}) async-start(), calls=%async_computation.11 | async-start | bytes 4718592 | tf_op jit(solution)/shard_map/all_gather | solution.py:78
  17.1 284.0 %copy-start.53 = (f32[1,2048]{1,0:T(1,128)}, f32[1,2048]{1,0:T(1,128)S(1)}, u32[]{:S(2)}) copy-start(f32[1,2048]{1,0:T(1,128)S(1)} %get-tuple-element.459) | copy-start | bytes 24580
  19.8 126.5 %all-gather.15.cloned.1.call-start = ((), (), s32[]{:S(2)}) async-start(), calls=%async_computation.13 | async-start | bytes 1310720 | tf_op jit(solution)/shard_map/all_gather | solution.py:67
  20.6 279.1 %reduce-scatter.16.cloned.1.call-start = ((), (), s32[]{:S(2)}) async-start(), calls=%async_computation.14 | async-start | bytes 9437184 | tf_op jit(solution)/shard_map/reduce_scatter | solution.py:119
  153.0 203.2 %all-gather.21.cloned.1.call-start = ((), (), s32[]{:S(2)}) async-start(), calls=%async_computation.17 | async-start | bytes 2949120 | tf_op jit(solution)/shard_map/all_gather | solution.py:135
  161.6 269.4 %all-gather.19.cloned.1.call-start = ((), (), s32[]{:S(2)}) async-start(), calls=%async_computation.16 | async-start | bytes 4718592 | tf_op jit(solution)/shard_map/all_gather | solution.py:134
  303.1 234.7 %all-gather.23.cloned.1.call-start = ((), (), s32[]{:S(2)}) async-start(), calls=%async_computation.18 | async-start | bytes 20971520 | tf_op jit(solution)/shard_map/all_gather | solution.py:70
  303.9 292.9 %all-gather.25.cloned.1.call-start = ((), (), s32[]{:S(2)}) async-start(), calls=%async_computation.19 | async-start | bytes 10485760 | tf_op jit(solution)/shard_map/all_gather | solution.py:71
  304.6 368.0 %all-gather.27.cloned.1.call-start = ((), (), s32[]{:S(2)}) async-start(), calls=%async_computation.21 | async-start | bytes 4718592 | tf_op jit(solution)/shard_map/all_gather | solution.py:168
  305.3 494.1 %reduce-scatter.24.cloned.1.call-start = ((), (), s32[]{:S(2)}) async-start(), calls=%async_computation.25 | async-start | bytes 5898240 | tf_op jit(solution)/shard_map/reduce_scatter | solution.py:203
  697.9 160.6 %all-gather.17.cloned.1.call-start = ((), (), s32[]{:S(2)}) async-start(), calls=%async_computation.15 | async-start | bytes 2949120 | tf_op jit(solution)/shard_map/all_gather | solution.py:136
  804.0 331.5 %reduce-scatter.20.cloned.1.call-start = ((), (), s32[]{:S(2)}) async-start(), calls=%async_computation.22 | async-start | bytes 9437184 | tf_op jit(solution)/shard_map/reduce_scatter | solution.py:202
  987.7 152.4 %copy-start.28 = (f32[1024,128]{1,0:T(8,128)S(1)}, f32[1024,128]{1,0:T(8,128)}, u32[]{:S(2)}) copy-start(f32[1024,128]{1,0:T(8,128)} %get-tuple-element.453) | copy-start | bytes 1572868
  987.7 153.5 %copy-start.75 = (f32[64]{0:T(128)S(1)}, f32[64]{0:T(128)}, u32[]{:S(2)}) copy-start(f32[64]{0:T(128)} %copy-done.74) | copy-start | bytes 772
  987.7 162.9 %copy-start.57 = (f32[1024,2]{0,1:T(2,128)S(1)}, f32[1024,2]{0,1:T(2,128)}, u32[]{:S(2)}) copy-start(f32[1024,2]{0,1:T(2,128)} %copy-done.56) | copy-start | bytes 24580
  987.7 162.9 %copy-start.14 = (f32[1,1024,256]{1,2,0:T(8,128)S(1)}, f32[1,1024,256]{1,2,0:T(8,128)}, u32[]{:S(2)}) copy-start(f32[1,1024,256]{1,2,0:T(8,128)} %copy-done.13) | copy-start | bytes 3145732
  987.8 224.8 %all-gather.29.cloned.1.call-start = ((), (), s32[]{:S(2)}) async-start(), calls=%async_computation.23 | async-start | bytes 4718592 | tf_op jit(solution)/shard_map/all_gather | solution.py:211
  1140.0 280.6 %reduce-scatter.22.cloned.1.call-start = ((), (), s32[]{:S(2)}) async-start(), calls=%async_computation.24 | async-start | bytes 9437184 | tf_op jit(solution)/shard_map/reduce_scatter | solution.py:269
  1273.2 211.5 %reduce-scatter.34.cloned.1.call-start = ((), (), s32[]{:S(2)}) async-start(), calls=%async_computation.30 | async-start | bytes 81920
  1274.2 228.6 %reduce-scatter.26.cloned.1.call-start = ((), (), s32[]{:S(2)}) async-start(), calls=%async_computation.26 | async-start | bytes 7864320 | tf_op jit(solution)/shard_map/reduce_scatter | solution.py:284
  1281.8 374.0 %reduce-scatter.18.cloned.1.call-start = ((), (), s32[]{:S(2)}) async-start(), calls=%async_computation.20 | async-start | bytes 9437184 | tf_op jit(solution)/shard_map/reduce_scatter | solution.py:165
  1303.1 489.4 %reduce-scatter.36.cloned.1.call-start = ((), (), s32[]{:S(2)}) async-start(), calls=%async_computation.31 | async-start | bytes 1081344
  1423.6 602.8 %reduce-scatter.30.cloned.1.call-start = ((), (), s32[]{:S(2)}) async-start(), calls=%async_computation.28 | async-start | bytes 41943040 | tf_op jit(solution)/shard_map/reduce_scatter | solution.py:287
  1453.7 607.4 %reduce-scatter.28.cloned.1.call-start = ((), (), s32[]{:S(2)}) async-start(), calls=%async_computation.27 | async-start | bytes 2621440 | tf_op jit(solution)/shard_map/reduce_scatter | solution.py:285
  1459.5 730.8 %reduce-scatter.32.cloned.1.call-start = ((), (), s32[]{:S(2)}) async-start(), calls=%async_computation.29 | async-start | bytes 20971520 | tf_op jit(solution)/shard_map/reduce_scatter | solution.py:288
  1483.2 172.5 %copy-start.8 = (f32[128,2048]{1,0:T(8,128)S(1)}, f32[128,2048]{1,0:T(8,128)}, u32[]{:S(2)}) copy-start(f32[128,2048]{1,0:T(8,128)} %copy-done.6) | copy-start | bytes 3145732
  1483.2 172.5 %copy-start.22 = (f32[128,2048]{1,0:T(8,128)S(1)}, f32[128,2048]{1,0:T(8,128)}, u32[]{:S(2)}) copy-start(f32[128,2048]{1,0:T(8,128)} %reduce-scatter.20.cloned.1.call-done) | copy-start | bytes 3145732
  1483.2 172.5 %copy-start.31 = (bf16[128,2048]{1,0:T(8,128)(2,1)S(1)}, bf16[128,2048]{1,0:T(8,128)(2,1)}, u32[]{:S(2)}) copy-start(bf16[128,2048]{1,0:T(8,128)(2,1)} %param.19) | copy-start | bytes 1572868
  1483.2 172.5 %copy-start.55 = (f32[1,2048]{1,0:T(1,128)S(1)}, f32[1,2048]{1,0:T(1,128)}, u32[]{:S(2)}) copy-start(f32[1,2048]{1,0:T(1,128)} %copy-done.53) | copy-start | bytes 24580
  1483.2 172.5 %copy-start.71 = (f32[128]{0:T(128)S(1)}, f32[128]{0:T(128)}, u32[]{:S(2)}) copy-start(f32[128]{0:T(128)} %copy-done.69) | copy-start | bytes 1540
  1483.2 172.5 %copy-start.77 = (f32[128]{0:T(128)S(1)}, f32[128]{0:T(128)}, u32[]{:S(2)}) copy-start(f32[128]{0:T(128)} %copy-done.76) | copy-start | bytes 1540
  (73 other events, 2691.8 us)
Sparse Core Ops, SparseCore 0:
  10.2 31.5 all-gather.12
  44.5 73.3 all-gather.10
  119.5 14.9 all-gather.14
  153.1 146.5 reduce-scatter.15
  302.5 53.6 all-gather.20
  359.0 71.9 all-gather.18
  432.6 104.1 all-gather.22
  538.5 58.2 all-gather.24
  599.2 73.3 all-gather.26
  698.0 101.3 reduce-scatter.23
  804.1 54.4 all-gather.16
  987.8 147.6 reduce-scatter.19
  1140.1 72.3 all-gather.28
  1273.3 147.2 reduce-scatter.21
  1423.6 18.3 reduce-scatter.33
  1444.4 58.3 reduce-scatter.25
  1506.7 148.9 reduce-scatter.17
  1658.4 134.0 reduce-scatter.35
  1795.3 231.1 reduce-scatter.29
  2029.6 31.3 reduce-scatter.27
  2064.2 126.1 reduce-scatter.31
where the time goes:
time: 2210 us; the launch traced here: 2200 us
  waiting for transfers between devices  1590 us (72%)
  matrix products  318 us (14%)
  local copies, waits for them, and re-layouts  146 us (7%)
  other arithmetic  108 us (5%)
    reduce_scatter x1, waiting for transfers between devices, per_device(): lax.psum_scatter(gate_up_grad, 'dp', scatter_dimension=2, tiled=True)  233 us
    reduce_scatter x1, waiting for transfers between devices, per_device(): lax.psum_scatter(moe_terms, 'tensor', scatter_dimension=0, tiled=True)  150 us
    reduce_scatter x1, waiting for transfers between devices, per_device(): lax.psum_scatter(d_mid_terms, 'tensor', scatter_dimension=0, tiled=True)  148 us
    reduce_scatter x1, waiting for transfers between devices, per_device(): lax.psum_scatter(jnp.dot(context, out_full, preferred_element_type=f32),...  138 us
    unnamed x23, waiting for transfers between devices  137 us
    reduce_scatter x1, waiting for transfers between devices, per_device(): lax.psum_scatter(down_grad, 'dp', scatter_dimension=2, tiled=True)  129 us
    reduce_scatter x1, waiting for transfers between devices, per_device(): lax.psum_scatter(jnp.einsum('jsc,jdc->sd', d_projected, qkv_full, preferr...  117 us
    reduce_scatter x1, waiting for transfers between devices, per_device(): lax.psum_scatter(d_combine, 'tensor', scatter_dimension=0, tiled=True)  101 us
  transfers between devices with their start and end apart: 21, of which 18 were waited for; matrix products, arithmetic and copies ran while one was open for 15% of the time, Pallas kernels for 0%

commit v1 on v0

v1 whole, which is shorter than its diff:
```python
import functools

import jax
import jax.numpy as jnp
from jax import lax
from jax.experimental import pallas as pl
from jax.experimental.pallas import tpu as pltpu
from jax.sharding import PartitionSpec as P

HD = 128
E = 16
EPSILON = 1e-05
ROPE_BASE = 10000.0
MASKED = -1e30
LANES = 128
CHUNKS = 2

f32 = jnp.float32
bf16 = jnp.bfloat16
NT = (((1,), (1,)), ((), ()))
TN = (((0,), (0,)), ((), ()))
ANY = pl.BlockSpec(memory_space=pl.ANY)
SMEM = pl.BlockSpec(memory_space=pltpu.SMEM)
VMEM = pl.BlockSpec(memory_space=pltpu.VMEM)


def dot(a, b):
    return jnp.dot(a, b, preferred_element_type=f32)


def dot_nt(a, b):
    return lax.dot_general(a, b, NT, preferred_element_type=f32)


def dot_tn(a, b):
    return lax.dot_general(a, b, TN, preferred_element_type=f32)


def shape(dims, dtype):
    return jax.ShapeDtypeStruct(dims, dtype)


def ring_of(groups):
    return list(range(0, groups, 2)) + list(range(groups - 1, 0, -2))


def ring_step(value, groups, sign):
    ring = ring_of(groups)
    pairs = [(ring[p], ring[(p + sign) % groups]) for p in range(groups)]
    return lax.ppermute(value, "tensor", pairs)


def ring_gather(own, groups):
    half = own.shape[0] // 2
    steps = groups // 2
    below, above = [own], [own]
    for _ in range(steps - 1):
        below.append(ring_step(below[-1], groups, 1))
        above.append(ring_step(above[-1], groups, -1))
    far_low = ring_step(below[-1][:half], groups, 1)
    far_high = ring_step(above[-1][half:], groups, -1)
    return [far_low, far_high, own] + above[1:] + below[:0:-1]


def ring_scatter(far_low, far_high, rest, groups):
    steps = groups // 2
    rows = rest.shape[0] // (groups - 1)

    def block(distance):
        at = (distance % groups if distance >= 0 else groups - 1 + distance) * rows
        return rest[at : at + rows].astype(f32)

    half = rows // 2
    rise = ring_step(far_low, groups, 1).astype(f32)
    fall = ring_step(far_high, groups, -1).astype(f32)
    rise = jnp.pad(rise, ((0, half), (0, 0)))
    fall = jnp.pad(fall, ((half, 0), (0, 0)))
    for distance in range(steps - 1, 0, -1):
        rise = ring_step((block(distance) + rise).astype(bf16), groups, 1).astype(f32)
        fall = ring_step((block(-distance) + fall).astype(bf16), groups, -1).astype(f32)
    return block(0) + rise + fall


def bits_of(count):
    return [1 << b for b in range(count.bit_length() - 1)]


def flip_step(value, axis, count, bit):
    return lax.ppermute(value, axis, [(s, s ^ bit) for s in range(count)])


def relative(parts, axis):
    count = len(parts)
    index = lax.axis_index(axis)
    for bit in bits_of(count):
        turned = (index & bit) != 0
        parts = [jnp.where(turned, parts[k ^ bit], parts[k]) for k in range(count)]
    return parts


def split_last(value, count):
    width = value.shape[-1] // count
    return [value[..., k * width : (k + 1) * width] for k in range(count)]


def relative_columns(value, axis, count):
    return jnp.concatenate(relative(split_last(value, count), axis), axis=-1)


def flip_gather(own, axis, count):
    parts = {0: own}
    for bit in reversed(bits_of(count)):
        for k in list(parts):
            parts[k ^ bit] = flip_step(parts[k], axis, count, bit)
    return [parts[k] for k in range(count)]


def flip_reduce(parts, axis, count):
    parts = list(parts)
    for bit in bits_of(count):
        for k in range(0, count, 2 * bit):
            sent = parts[k + bit]
            parts[k] = parts[k].astype(f32) + flip_step(sent, axis, count, bit).astype(f32)
            if k % (4 * bit) and 2 * bit < count:
                parts[k] = parts[k].astype(bf16)
    return parts[0]


def flip_reduce_rows(value, axis, count):
    for bit in bits_of(count):
        pairs = value.reshape((value.shape[0] // 2, 2) + value.shape[1:])
        value = pairs[:, 0] + flip_step(pairs[:, 1], axis, count, bit)
    return value[0]


def fetch(sources, target, sems, first, rows_at):
    copies = []
    for number, source in enumerate(sources):
        copy = pltpu.make_async_copy(
            source, target.at[pl.ds(rows_at[number], source.shape[0])], sems.at[first + number]
        )
        copy.start()
        copies.append(copy)
    return copies


def piece_rows(order, half, pieces):
    rows = 2 * half
    starts = [pl.multiple_of(order[0] * rows, rows)]
    starts.append(pl.multiple_of(order[0] * rows + half, half))
    for number in range(2, pieces):
        starts.append(pl.multiple_of(order[number - 1] * rows, rows))
    return starts


def send_out(staged, outs, sems, first, starts):
    low, high, rest = outs
    half = low.shape[0]
    copies = []
    targets = [low, high] + [
        rest.at[pl.ds(at, 2 * half)] for at in range(0, rest.shape[0], 2 * half)
    ]
    for number, target in enumerate(targets):
        copy = pltpu.make_async_copy(
            staged.at[pl.ds(starts[number], target.shape[0])], target, sems.at[first + number]
        )
        copy.start()
        copies.append(copy)
    return copies


def allowed_pairs(seg_col, seg_row, first, rows, width):
    row_pos = first + lax.broadcasted_iota(jnp.int32, (rows, width), 0)
    key_pos = lax.broadcasted_iota(jnp.int32, (rows, width), 1)
    return (seg_col[pl.ds(first, rows), :] == seg_row[:, pl.ds(0, width)]) & (key_pos <= row_pos)


def attn_fwd_body(n, count, block, *refs):
    it = iter(refs)
    order = next(it)
    pieces = [next(it) for _ in range(count)]
    wq = [next(it) for _ in range(n)]
    wo = [next(it) for _ in range(n)]
    gains, cosine, sine, seg_row, seg_col = (next(it) for _ in range(5))
    q_o, k_o, v_o, qr_o, kr_o, ctx_o, lse_o, x_o = (next(it) for _ in range(8))
    outs = [next(it) for _ in range(3)]
    xs, wqs, wos, stage, sems = (next(it) for _ in range(5))
    length, width = ctx_o.shape
    depth = wq[0].shape[1]
    heads = width // HD
    starts = piece_rows(order, pieces[0].shape[0], count)
    copies = []
    for k in range(n):
        for j in range(3):
            copies.append(
                pltpu.make_async_copy(
                    wq[k].at[j],
                    wqs.at[pl.ds(k * depth, depth), pl.ds(j * width, width)],
                    sems.at[2 * count + 4 * k + j],
                )
            )
        copies.append(
            pltpu.make_async_copy(
                wo[k], wos.at[:, pl.ds(k * depth, depth)], sems.at[2 * count + 4 * k + 3]
            )
        )
    for copy in copies:
        copy.start()
    for copy in copies + fetch(pieces, xs, sems, 0, starts):
        copy.wait()
    keep = pltpu.make_async_copy(xs, x_o, sems.at[0])
    keep.start()
    scale = HD ** (-0.5)

    def project(r, _):
        rows = pl.ds(pl.multiple_of(r * block, block), block)
        out = dot(xs[rows, :], wqs[...])
        v_o[rows, :] = out[:, 2 * width :].astype(bf16)
        for j, (raw_o, hat_o) in enumerate(((qr_o, q_o), (kr_o, k_o))):
            raw = out[:, j * width : (j + 1) * width]
            raw_o[rows, :] = raw
            for h in range(heads):
                cols = slice(h * HD, (h + 1) * HD)
                u = raw[:, cols]
                inv = lax.rsqrt(jnp.mean(u * u, axis=-1, keepdims=True) + EPSILON)
                u = u * inv * gains[j : j + 1, cols]
                u = u * cosine[rows, :] + pltpu.roll(u, HD // 2, 1) * sine[rows, :]
                hat_o[rows, cols] = u.astype(bf16)
        return 0

    lax.fori_loop(0, length // block, project, 0)
    for b in range(length // block):
        rows = pl.ds(b * block, block)
        hi = (b + 1) * block
        allowed = allowed_pairs(seg_col, seg_row, b * block, block, hi)
        for h in range(heads):
            cols = slice(h * HD, (h + 1) * HD)
            s = dot_nt(q_o[rows, cols], k_o[pl.ds(0, hi), cols]) * scale
            s = jnp.where(allowed, s, MASKED)
            top = jnp.max(s, axis=-1, keepdims=True)
            e = jnp.exp(s - top)
            total = jnp.sum(e, axis=-1, keepdims=True)
            probs = (e * (1.0 / total)).astype(bf16)
            ctx_o[rows, cols] = dot(probs, v_o[pl.ds(0, hi), cols]).astype(bf16)
            lse_o[h, rows, :] = top + jnp.log(total)
        stage[rows, :] = dot(ctx_o[rows, :], wos[...]).astype(bf16)
    for copy in send_out(stage, outs, sems, count, starts):
        copy.wait()
    keep.wait()


def attn_fwd(order, pieces, wq, wo, gains, cosine, sine, seg_row, seg_col):
    n, count = len(wq), len(pieces)
    half, d = pieces[0].shape
    length = cosine.shape[0]
    width = wo[0].shape[0]
    heads = width // HD
    block = min(256, length)
    scratch = [
        pltpu.VMEM((length, d), bf16),
        pltpu.VMEM((d, 3 * width), bf16),
        pltpu.VMEM((width, d), bf16),
        pltpu.VMEM((length, d), bf16),
        pltpu.SemaphoreType.DMA((2 * count + 4 * n,)),
    ]
    return pl.pallas_call(
        functools.partial(attn_fwd_body, n, count, block),
        in_specs=[SMEM] + [ANY] * (count + 2 * n) + [VMEM] * 5,
        out_specs=[VMEM] * 7 + [ANY] * 4,
        out_shape=[shape((length, width), bf16)] * 3
        + [shape((length, width), f32)] * 2
        + [shape((length, width), bf16), shape((heads, length, 1), f32), shape((length, d), bf16)]
        + [shape((half, d), bf16)] * 2
        + [shape((length - 2 * half, d), bf16)],
        scratch_shapes=scratch,
        compiler_params=pltpu.CompilerParams(vmem_limit_bytes=48 << 20),
        cost_estimate=pl.CostEstimate(
            flops=20 * length * d * width, bytes_accessed=40 << 20, transcendentals=0
        ),
        name="attn_fwd",
    )(order, *pieces, *wq, *wo, gains, cosine, sine, seg_row, seg_col)


def attn_bwd_body(n, count, block, *refs):
    it = iter(refs)
    order = next(it)
    pieces = [next(it) for _ in range(count)]
    wq = [next(it) for _ in range(n)]
    wo = [next(it) for _ in range(n)]
    q, k_, v, qr, kr, lse = (next(it) for _ in range(6))
    gains, cosine, sine, seg_row, seg_col, x = (next(it) for _ in range(6))
    outs = [next(it) for _ in range(3)]
    dp_o, hg_o, gs_o, db_o = (next(it) for _ in range(4))
    db, wqs, wos, stage, dctx, dq, dk, dv, sems = (next(it) for _ in range(9))
    length, width = q.shape
    depth = wq[0].shape[1]
    heads = width // HD
    starts = piece_rows(order, pieces[0].shape[0], count)
    copies = []
    for k in range(n):
        for j in range(3):
            copies.append(
                pltpu.make_async_copy(
                    wq[k].at[j],
                    wqs.at[pl.ds(k * depth, depth), pl.ds(j * width, width)],
                    sems.at[2 * count + 4 * k + j],
                )
            )
        copies.append(
            pltpu.make_async_copy(
                wo[k], wos.at[:, pl.ds(k * depth, depth)], sems.at[2 * count + 4 * k + 3]
            )
        )
    for copy in copies:
        copy.start()
    for copy in copies + fetch(pieces, db, sems, 0, starts):
        copy.wait()
    keep = pltpu.make_async_copy(db, db_o, sems.at[0])
    keep.start()
    scale = HD ** (-0.5)

    def branch(r, _):
        rows = pl.ds(pl.multiple_of(r * block, block), block)
        dctx[rows, :] = dot_nt(db[rows, :], wos[...]).astype(bf16)
        dk[rows, :] = jnp.zeros((block, width), f32)
        dv[rows, :] = jnp.zeros((block, width), f32)
        return 0

    lax.fori_loop(0, length // block, branch, 0)
    for b in range(length // block):
        rows = pl.ds(b * block, block)
        hi = (b + 1) * block
        low = pl.ds(0, hi)
        allowed = allowed_pairs(seg_col, seg_row, b * block, block, hi)
        for h in range(heads):
            cols = slice(h * HD, (h + 1) * HD)
            s = dot_nt(q[rows, cols], k_[low, cols]) * scale
            p = jnp.where(allowed, jnp.exp(s - lse[h, rows, :]), 0.0)
            g = dot_nt(dctx[rows, cols], v[low, cols])
            pg = p * g
            ds = (pg - p * jnp.sum(pg, axis=-1, keepdims=True)).astype(bf16)
            dq[rows, cols] = dot(ds, k_[low, cols]) * scale
            dk[low, cols] += dot_tn(ds, q[rows, cols]) * scale
            dv[low, cols] += dot_tn(p.astype(bf16), dctx[rows, cols])
    hg_o[...] = jnp.zeros_like(hg_o)
    gs_o[...] = jnp.zeros_like(gs_o)

    def finish(r, _):
        rows = pl.ds(pl.multiple_of(r * block, block), block)
        dp_o[rows, 2 * width :] = dv[rows, :].astype(bf16)
        for j, (raw, grad) in enumerate(((qr, dq), (kr, dk))):
            for h in range(heads):
                cols = slice(h * HD, (h + 1) * HD)
                u = raw[rows, cols]
                inv = lax.rsqrt(jnp.mean(u * u, axis=-1, keepdims=True) + EPSILON)
                hat = u * inv
                t = grad[rows, cols]
                t = t * cosine[rows, :] - pltpu.roll(t, HD // 2, 1) * sine[rows, :]
                hg_o[j : j + 1, cols] += jnp.sum(t * hat, axis=0, keepdims=True)
                w = t * gains[j : j + 1, cols]
                w = inv * (w - hat * jnp.mean(w * hat, axis=-1, keepdims=True))
                dp_o[rows, j * width + h * HD : j * width + (h + 1) * HD] = w.astype(bf16)
        out = dot_nt(dp_o[rows, :], wqs[...])
        gs_o[...] += jnp.sum(out * x[rows, :].astype(f32), axis=0, keepdims=True)
        stage[rows, :] = out.astype(bf16)
        return 0

    lax.fori_loop(0, length // block, finish, 0)
    for copy in send_out(stage, outs, sems, count, starts):
        copy.wait()
    keep.wait()


def attn_bwd(order, pieces, wq, wo, q, k, v, qr, kr, lse, gains, cosine, sine, seg_row, seg_col, x):
    n, count = len(wq), len(pieces)
    half, d = pieces[0].shape
    length, width = q.shape
    block = min(256, length)
    scratch = [
        pltpu.VMEM((length, d), bf16),
        pltpu.VMEM((d, 3 * width), bf16),
        pltpu.VMEM((width, d), bf16),
        pltpu.VMEM((length, d), bf16),
        pltpu.VMEM((length, width), bf16),
        pltpu.VMEM((length, width), f32),
        pltpu.VMEM((length, width), f32),
        pltpu.VMEM((length, width), f32),
        pltpu.SemaphoreType.DMA((2 * count + 4 * n,)),
    ]
    return pl.pallas_call(
        functools.partial(attn_bwd_body, n, count, block),
        in_specs=[SMEM] + [ANY] * (count + 2 * n) + [VMEM] * 12,
        out_specs=[ANY] * 3 + [VMEM] * 3 + [ANY],
        out_shape=[shape((half, d), bf16)] * 2
        + [shape((length - 2 * half, d), bf16)]
        + [
            shape((length, 3 * width), bf16),
            shape((2, width), f32),
            shape((1, d), f32),
            shape((length, d), bf16),
        ],
        scratch_shapes=scratch,
        compiler_params=pltpu.CompilerParams(vmem_limit_bytes=48 << 20),
        cost_estimate=pl.CostEstimate(
            flops=40 * length * d * width, bytes_accessed=40 << 20, transcendentals=0
        ),
        name="attn_bwd",
    )(order, *pieces, *wq, *wo, q, k, v, qr, kr, lse, gains, cosine, sine, seg_row, seg_col, x)


def attn_grad_body(x, dp, ctx, db, qkv_o, out_o):
    width = ctx.shape[1]
    grad = dot_tn(x[...], dp[...])
    for j in range(3):
        qkv_o[0, j] = grad[:, j * width : (j + 1) * width].astype(bf16)
    out_o[0] = dot_tn(ctx[...], db[...]).astype(bf16)


def attn_grad(x, dp, ctx, db, n):
    length, d = x.shape
    width = ctx.shape[1]
    depth = d // n
    return pl.pallas_call(
        attn_grad_body,
        grid=(n,),
        in_specs=[
            pl.BlockSpec((length, depth), lambda k: (0, k)),
            pl.BlockSpec((length, 3 * width), lambda k: (0, 0)),
            pl.BlockSpec((length, width), lambda k: (0, 0)),
            pl.BlockSpec((length, depth), lambda k: (0, k)),
        ],
        out_specs=[
            pl.BlockSpec((1, 3, depth, width), lambda k: (k, 0, 0, 0)),
            pl.BlockSpec((1, width, depth), lambda k: (k, 0, 0)),
        ],
        out_shape=[shape((n, 3, depth, width), bf16), shape((n, width, depth), bf16)],
        compiler_params=pltpu.CompilerParams(vmem_limit_bytes=32 << 20),
        cost_estimate=pl.CostEstimate(
            flops=8 * length * d * width, bytes_accessed=16 << 20, transcendentals=0
        ),
        name="attn_grad",
    )(x, dp, ctx, db)


def moe_body(n, group, block, steps, count, *refs):
    it = iter(refs)
    xp = [next(it) for _ in range(count)]
    cp = [next(it) for _ in range(count)]
    gu = [next(it) for _ in range(n)]
    dn = [next(it) for _ in range(n)]
    moe_o = [next(it) for _ in range(3)]
    dm_o = [next(it) for _ in range(3)]
    hw_o, dgu_o = next(it), next(it)
    xs, cs, wgu, wd, macc, dacc, gg, sems = (next(it) for _ in range(8))
    length, d = xs.shape
    fw, depth = dn[0].shape[1], dn[0].shape[2]
    step = pl.program_id(0)
    half = xp[0].shape[0]
    starts = [0, half] + [2 * half * (i - 1) for i in range(2, count)]

    @pl.when(step == 0)
    def _():
        copies = fetch(xp, xs, sems, 0, starts) + fetch(cp, cs, sems, count, starts)
        macc[...] = jnp.zeros_like(macc)
        dacc[...] = jnp.zeros_like(dacc)
        gg[...] = jnp.zeros_like(gg)
        for copy in copies:
            copy.wait()

    for k in range(n):
        for i in range(group):
            for g in range(2):
                wgu[pl.ds(k * depth, depth), pl.ds((2 * i + g) * fw, fw)] = gu[k][i, g]
            wd[pl.ds(i * fw, fw), pl.ds(k * depth, depth)] = dn[k][i]

    def rows_of(r, _):
        rows = pl.ds(pl.multiple_of(r * block, block), block)
        gate_up = dot(xs[rows, :], wgu[...])
        d_hid = dot_nt(cs[rows, pl.ds(0, d)], wd[...])
        gates = cs[rows, pl.ds(d, LANES)].astype(f32)
        lane = lax.broadcasted_iota(jnp.int32, gates.shape, 1)
        total = jnp.zeros(gates.shape, f32)
        hidden, grads = [], []
        for i in range(group):
            pick = lane == step * group + i
            w = jnp.sum(jnp.where(pick, gates, 0.0), axis=1, keepdims=True)
            g = gate_up[:, 2 * i * fw : (2 * i + 1) * fw]
            u = gate_up[:, (2 * i + 1) * fw : (2 * i + 2) * fw]
            dh = d_hid[:, i * fw : (i + 1) * fw]
            z = jax.nn.sigmoid(g)
            swish = g * z
            h = swish * u
            total = total + jnp.where(pick, jnp.sum(h * dh, axis=1, keepdims=True), 0.0)
            dw = dh * w
            hidden.append((h * w).astype(bf16))
            grads.append((dw * u * z * (1.0 + g * (1.0 - z))).astype(bf16))
            grads.append((dw * swish).astype(bf16))
        hid = jnp.concatenate(hidden, axis=1)
        grad = jnp.concatenate(grads, axis=1)
        hw_o[rows, :] = hid
        dgu_o[rows, :] = grad
        gg[rows, :] += total
        macc[rows, :] += dot(hid, wd[...])
        dacc[rows, :] += dot_nt(grad, wgu[...])
        return 0

    lax.fori_loop(0, length // block, rows_of, 0)

    @pl.when(step == steps - 1)
    def _():
        xs[...] = dacc[...].astype(bf16)
        copies = send_out(xs, dm_o, sems, 0, starts)
        cs[:, pl.ds(0, d)] = macc[...].astype(bf16)
        cs[:, pl.ds(d, LANES)] = gg[...].astype(bf16)
        copies = copies + send_out(cs, moe_o, sems, count, starts)
        for copy in copies:
            copy.wait()


def moe(xp, cp, gate_up, down, group=2):
    n, count = len(gate_up), len(xp)
    experts, _, depth, fw = gate_up[0].shape
    d = n * depth
    wide = d + LANES
    half = xp[0].shape[0]
    length = sum(p.shape[0] for p in xp)
    steps = experts // group

    def outs(columns):
        return [shape((half, columns), bf16)] * 2 + [shape((length - 2 * half, columns), bf16)]

    return pl.pallas_call(
        functools.partial(moe_body, n, group, min(512, length), steps, count),
        grid=(steps,),
        in_specs=[ANY] * (2 * count)
        + [pl.BlockSpec((group, 2, depth, fw), lambda s: (s, 0, 0, 0))] * n
        + [pl.BlockSpec((group, fw, depth), lambda s: (s, 0, 0))] * n,
        out_specs=[ANY] * 6
        + [
            pl.BlockSpec((length, group * fw), lambda s: (0, s)),
            pl.BlockSpec((length, 2 * group * fw), lambda s: (0, s)),
        ],
        out_shape=outs(wide)
        + outs(d)
        + [shape((length, experts * fw), bf16), shape((length, 2 * experts * fw), bf16)],
        scratch_shapes=[
            pltpu.VMEM((length, d), bf16),
            pltpu.VMEM((length, wide), bf16),
            pltpu.VMEM((d, 2 * group * fw), bf16),
            pltpu.VMEM((group * fw, d), bf16),
            pltpu.VMEM((length, d), f32),
            pltpu.VMEM((length, d), f32),
            pltpu.VMEM((length, LANES), f32),
            pltpu.SemaphoreType.DMA((2 * count,)),
        ],
        compiler_params=pltpu.CompilerParams(vmem_limit_bytes=60 << 20),
        cost_estimate=pl.CostEstimate(
            flops=18 * length * d * experts * fw, bytes_accessed=60 << 20, transcendentals=0
        ),
        name="moe",
    )(*xp, *cp, *gate_up, *down)


def turn_body(count, *refs):
    pieces, out, xs, sems = refs[:count], refs[count], refs[count + 1], refs[count + 2]
    half = pieces[0].shape[0]
    starts = [0, half] + [2 * half * (i - 1) for i in range(2, count)]
    for copy in fetch(pieces, xs, sems, 0, starts):
        copy.wait()
    length, d = xs.shape
    size = 256
    eye = (
        lax.broadcasted_iota(jnp.int32, (size, size), 0)
        == lax.broadcasted_iota(jnp.int32, (size, size), 1)
    ).astype(bf16)
    for at in range(0, d, size):
        out[pl.ds(at, size), :] = dot_nt(eye, xs[:, pl.ds(at, size)]).astype(bf16)


def turn_rows(pieces):
    count = len(pieces)
    length = sum(p.shape[0] for p in pieces)
    d = pieces[0].shape[1]
    return pl.pallas_call(
        functools.partial(turn_body, count),
        in_specs=[ANY] * count,
        out_specs=VMEM,
        out_shape=shape((d, length), bf16),
        scratch_shapes=[pltpu.VMEM((length, d), bf16), pltpu.SemaphoreType.DMA((count,))],
        compiler_params=pltpu.CompilerParams(vmem_limit_bytes=32 << 20),
        cost_estimate=pl.CostEstimate(
            flops=2 * length * d * 256, bytes_accessed=8 << 20, transcendentals=0
        ),
        name="turn_rows",
    )(*pieces)


def moe_grad_body(n, group, count, xt, dgu, hw, *refs):
    pieces = refs[:count]
    gu_o = refs[count : count + n]
    dn_o = refs[count + n : count + 2 * n]
    cs, sems = refs[count + 2 * n :]
    fw, depth = dn_o[0].shape[1], dn_o[0].shape[2]
    half = pieces[0].shape[0]
    d = n * depth
    starts = [0, half] + [2 * half * (i - 1) for i in range(2, count)]

    @pl.when(pl.program_id(0) == 0)
    def _():
        for copy in fetch([p.at[:, pl.ds(0, d)] for p in pieces], cs, sems, 0, starts):
            copy.wait()

    for k in range(n):
        grad = dot(xt[pl.ds(k * depth, depth), :], dgu[...])
        for i in range(group):
            for g in range(2):
                at = (2 * i + g) * fw
                gu_o[k][i, g] = grad[:, at : at + fw].astype(bf16)
    turned = hw[...].T
    for k in range(n):
        grad = dot(turned, cs[:, pl.ds(k * depth, depth)])
        for i in range(group):
            dn_o[k][i] = grad[i * fw : (i + 1) * fw].astype(bf16)


def moe_grad(xt, dgu, hw, cp, n, experts, first, number, group=2):
    d, length = xt.shape
    count = len(cp)
    depth = d // n
    fw = hw.shape[1] // experts
    start = first // group
    return pl.pallas_call(
        functools.partial(moe_grad_body, n, group, count),
        grid=(number // group,),
        in_specs=[
            pl.BlockSpec((d, length), lambda s: (0, 0)),
            pl.BlockSpec((length, 2 * group * fw), lambda s: (0, s + start)),
            pl.BlockSpec((length, group * fw), lambda s: (0, s + start)),
        ]
        + [ANY] * count,
        out_specs=[pl.BlockSpec((group, 2, depth, fw), lambda s: (s, 0, 0, 0))] * n
        + [pl.BlockSpec((group, fw, depth), lambda s: (s, 0, 0))] * n,
        out_shape=[shape((number, 2, depth, fw), bf16)] * n + [shape((number, fw, depth), bf16)] * n,
        scratch_shapes=[pltpu.VMEM((length, d), bf16), pltpu.SemaphoreType.DMA((count,))],
        compiler_params=pltpu.CompilerParams(vmem_limit_bytes=48 << 20),
        cost_estimate=pl.CostEstimate(
            flops=6 * length * d * number * fw, bytes_accessed=30 << 20, transcendentals=0
        ),
        name="moe_grad",
    )(xt, dgu, hw, *cp)


def rope_tables(length):
    positions = jnp.arange(length, dtype=f32)
    inverse_freq = ROPE_BASE ** (-jnp.arange(HD // 2, dtype=f32) * 2.0 / HD)
    phases = positions[:, None] * inverse_freq[None, :]
    cosine, sine = jnp.cos(phases), jnp.sin(phases)
    return jnp.concatenate([cosine, cosine], axis=-1), jnp.concatenate([-sine, sine], axis=-1)


def per_device(
    tokens,
    segments,
    routes,
    gate_values,
    cotangent,
    query_key_value,
    out_weight,
    head_gain,
    layer_gain,
    gate_up,
    down_weight,
):
    groups = lax.axis_size("tensor")
    n = lax.axis_size("dp")
    own_rows, d = tokens.shape
    seq_len = own_rows * groups
    heads = query_key_value.shape[2] // HD
    depth = d // n

    small = jnp.concatenate([layer_gain.reshape(-1), head_gain.reshape(-1)])
    small = flip_gather(small, "dp", n)
    cut = 2 * depth
    gain_rel = jnp.concatenate([s[:cut].reshape(2, depth) for s in small], axis=1).astype(f32)
    gain_in, gain_mid = gain_rel[0], gain_rel[1]
    head_parts = relative([s[cut:].reshape(2, heads, HD // n) for s in small], "dp")
    gain_head = jnp.concatenate(head_parts, axis=2).reshape(2, heads * HD).astype(f32)

    ring = jnp.array(ring_of(groups), jnp.int32)
    place = jnp.argmax(ring == lax.axis_index("tensor")).astype(jnp.int32)
    steps = groups // 2
    distances = [steps] + list(range(steps)) + list(range(1 - steps, 0))
    order = ring[(place + jnp.array(distances, jnp.int32)) % groups]
    cosine, sine = rope_tables(seq_len)
    seg_row = segments.reshape(1, seq_len)
    seg_col = segments.reshape(seq_len, 1)
    chosen = routes[:, :, None] == jnp.arange(E, dtype=jnp.int32)
    gates = jnp.sum(jnp.where(chosen, gate_values.astype(f32)[:, :, None], 0.0), axis=1)

    x = relative_columns(tokens, "dp", n).astype(f32)
    inv_in = lax.rsqrt(jnp.mean(x * x, axis=-1, keepdims=True) + EPSILON)
    x_hat = x * inv_in
    normed_in = ring_gather((x_hat * gain_in).astype(bf16), groups)
    wq = flip_gather(query_key_value, "dp", n)
    wo = flip_gather(out_weight, "dp", n)
    d_out = relative_columns(cotangent, "dp", n)
    q, k, v, q_raw, k_raw, context, lse, normed_all, *attn = attn_fwd(
        order, normed_in, wq, wo, gain_head, cosine, sine, seg_row, seg_col
    )
    with_gates = jnp.concatenate(
        [d_out, jnp.pad(gates, ((0, 0), (0, LANES - E))).astype(bf16)], axis=1
    )
    d_pieces = ring_gather(with_gates, groups)
    middle = x + ring_scatter(*attn, groups)
    inv_mid = lax.rsqrt(jnp.mean(middle * middle, axis=-1, keepdims=True) + EPSILON)
    mid_hat = middle * inv_mid
    normed_mid = ring_gather((mid_hat * gain_mid).astype(bf16), groups)

    gu = flip_gather(gate_up, "dp", n)
    dn = flip_gather(down_weight, "dp", n)
    *both, hidden, d_gate_up = moe(normed_mid, d_pieces, gu, dn)
    d_normed_mid = ring_scatter(*both[3:], groups)
    d_mid_hat = d_normed_mid * gain_mid
    d_middle = d_out.astype(f32) + inv_mid * (
        d_mid_hat - mid_hat * jnp.mean(d_mid_hat * mid_hat, axis=-1, keepdims=True)
    )
    d_branch = ring_gather(d_middle.astype(bf16), groups)
    mixed_rel = ring_scatter(*both[:3], groups)
    layer_out = relative_columns((middle + mixed_rel[:, :d]).astype(bf16), "dp", n)
    gate_grad = jnp.sum(jnp.where(chosen, mixed_rel[:, None, d : d + E], 0.0), axis=-1)

    mid_turned = turn_rows(normed_mid)
    number = E // CHUNKS
    gu_parts, dn_parts = [], []
    for c in range(CHUNKS):
        grads = moe_grad(mid_turned, d_gate_up, hidden, d_pieces, n, E, c * number, number)
        gu_parts.append(flip_reduce(grads[:n], "dp", n))
        dn_parts.append(flip_reduce(grads[n:], "dp", n))

    *to_rows, d_projected, head_part, in_part, d_branch_all = attn_bwd(
        order, d_branch, wq, wo, q, k, v, q_raw, k_raw, lse, gain_head, cosine, sine,
        seg_row, seg_col, normed_all,
    )
    d_normed_in = ring_scatter(*to_rows, groups)
    qkv_grad, out_grad = attn_grad(normed_all, d_projected, context, d_branch_all, n)
    qkv_grad = flip_reduce([qkv_grad[k] for k in range(n)], "dp", n)
    out_grad = flip_reduce([out_grad[k] for k in range(n)], "dp", n)

    d_x_hat = d_normed_in * gain_in
    input_grad = d_middle + inv_in * (
        d_x_hat - x_hat * jnp.mean(d_x_hat * x_hat, axis=-1, keepdims=True)
    )
    input_grad = relative_columns(input_grad, "dp", n)

    mid_part = jnp.sum(d_normed_mid * mid_hat, axis=0)
    layer_part = jnp.stack([in_part[0] / gain_in, mid_part])
    head_rel = relative(split_last(head_part.reshape(2, heads, HD), n), "dp")
    rows = [
        jnp.concatenate([a.reshape(-1), b.reshape(-1)])
        for a, b in zip(split_last(layer_part, n), head_rel)
    ]
    summed = flip_reduce_rows(jnp.stack(rows), "dp", n)
    head_grad = summed[cut:].reshape(2, heads, HD // n)
    layer_parts = relative(split_last(summed[:cut].reshape(2, depth), groups), "tensor")
    layer_grad = flip_reduce_rows(jnp.stack(layer_parts), "tensor", groups)

    return (
        layer_out,
        input_grad,
        gate_grad,
        qkv_grad,
        out_grad,
        head_grad,
        layer_grad,
        jnp.concatenate(gu_parts, axis=0),
        jnp.concatenate(dn_parts, axis=0),
    )


def solution(mesh):
    return jax.shard_map(
        per_device,
        mesh=mesh,
        in_specs=(
            P(("dp", "tensor"), None),
            P("dp", None),
            P(("dp", "tensor"), None),
            P(("dp", "tensor"), None),
            P(("dp", "tensor"), None),
            P(None, "dp", "tensor"),
            P("tensor", "dp"),
            P(None, "tensor", "dp"),
            P(None, "dp"),
            P(None, None, "dp", "tensor"),
            P(None, "tensor", "dp"),
        ),
        out_specs=(
            P(("dp", "tensor"), None),
            P(("dp", "tensor"), None),
            P(("dp", "tensor"), None),
            P(None, "dp", "tensor"),
            P("tensor", "dp"),
            P(None, "tensor", "dp"),
            P(None, ("dp", "tensor")),
            P(None, None, "dp", "tensor"),
            P(None, "tensor", "dp"),
        ),
        check_vma=False,
    )
```

time: 2210 us -> 761 us (0.34)
  waiting for transfers between devices: 1590 us -> 391 us
  matrix products: 318 us -> 0 us
  Pallas kernels: 0 us -> 166 us
  local copies, waits for them, and re-layouts: 146 us -> 24.5 us
  starting transfers between devices: 1.04 us -> 96 us
  other arithmetic: 108 us -> 72 us
    reduce_scatter x9 -> x0, waiting for transfers between devices: 1060 us -> none  [the longest x1 233 us: per_device(): lax.psum_scatter(gate_up_grad, 'dp', scatter_dimension=2, tiled=True)]
    all_gather x10 -> x0, waiting for transfers between devices: 395 us -> none  [the longest x1 76.1 us: per_device(): lax.all_gather((x_hat * gain_in).astype(bf16), 'tensor', axis=0, tiled=True)]
    ppermute x0 -> x102, waiting for transfers between devices: none -> 391 us  [the longest x64 248 us: ring_step(): return lax.ppermute(value, 'tensor', pairs)]
    dot_general x30 -> x0, matrix products: 280 us -> none  [the longest x1 29.9 us: per_device(): jnp.einsum('erd,gerf->egdf', expert_rows, d_gate_up, preferred_element_ty...]
    pallas_call x0 -> x7, Pallas kernels: none -> 166 us  [the longest x1 76.1 us: moe(): pl.pallas_call(functools.partial(moe_body, n, group, min(512, length), st...]
    unnamed x23 -> x0, waiting for transfers between devices: 137 us -> none
    ppermute x0 -> x102, starting transfers between devices: none -> 96 us  [the longest x64 71.2 us: ring_step(): return lax.ppermute(value, 'tensor', pairs)]
    convert_element_type x5 -> x0, local copies, waits for them, and re-layouts: 57.5 us -> none  [the longest x1 28.2 us: per_device(): expert_rows = jnp.einsum('ntec,ntd->encd', dispatch_four, normed_mid.resh...]
  transfers between devices with their start and end apart: 21 -> 102, of which waited for: 18 -> 46; matrix products, arithmetic and copies ran while one was open for 15% -> 10% of each run, Pallas kernels for 0% -> 6%
where the time goes in v1:
time: 761 us; the launch traced here: 751 us
  waiting for transfers between devices  391 us (51%)
  Pallas kernels  166 us (22%)
  starting transfers between devices  96 us (13%)
  other arithmetic  72 us (9%)
  local copies, waits for them, and re-layouts  24.5 us (3%)
    ppermute x64, waiting for transfers between devices, ring_step(): return lax.ppermute(value, 'tensor', pairs)  248 us
    ppermute x38, waiting for transfers between devices, flip_step(): return lax.ppermute(value, axis, [(s, s ^ bit) for s in range(count)])  143 us
    pallas_call x1, Pallas kernels, moe(): pl.pallas_call(functools.partial(moe_body, n, group, min(512, length), st...  76.1 us
    ppermute x64, starting transfers between devices, ring_step(): return lax.ppermute(value, 'tensor', pairs)  71.2 us
    pallas_call x2, Pallas kernels, moe_grad(): pl.pallas_call(functools.partial(moe_grad_body, n, group, count), grid=(n...  38 us
    pallas_call x1, Pallas kernels, attn_bwd(): pl.pallas_call(functools.partial(attn_bwd_body, n, count, block), in_spec...  26 us
    ppermute x38, starting transfers between devices, flip_step(): return lax.ppermute(value, axis, [(s, s ^ bit) for s in range(count)])  24.8 us
    pallas_call x1, Pallas kernels, attn_fwd(): pl.pallas_call(functools.partial(attn_fwd_body, n, count, block), in_spec...  18.2 us
  transfers between devices with their start and end apart: 102, of which 46 were waited for; matrix products, arithmetic and copies ran while one was open for 10% of the time, Pallas kernels for 6%

profile of v1, /device:TPU:0, one launch (start us, length us, event | category | flops | bytes accessed | tf_op | source)
XLA Modules:
  0.0 751.3 jit_solution(15948352275999118624)
XLA Ops:
  14.2 10.3 %collective-permute-done.3.refs_9_ = bf16[128,2048]{1,0:T(8,128)(2,1)} collective-permute-done((bf16[128,2048]{1,0:T(8,128)(2,1)S(1)}, bf16[128,2048]{1,0:T(8,128)(2,1)}, u32[]{:S(2)}, u32[]{:S(2)}) %collective-permute-start.3) | collective-permute-done | bytes 524320 | tf_op jit(solution)/shard_map/ppermute | solution.py:50
  30.3 8.0 %collective-permute-done.4.refs_8_ = bf16[128,2048]{1,0:T(8,128)(2,1)} collective-permute-done((bf16[128,2048]{1,0:T(8,128)(2,1)}, bf16[128,2048]{1,0:T(8,128)(2,1)}, u32[]{:S(2)}, u32[]{:S(2)}) %collective-permute-start.4) | collective-permute-done | bytes 524320 | tf_op jit(solution)/shard_map/ppermute | solution.py:50
  62.8 18.2 %attn_fwd.1 = (bf16[1024,256]{1,0:T(8,128)(2,1)S(1)}, bf16[1024,256]{1,0:T(8,128)(2,1)S(1)}, bf16[1024,256]{1,0:T(8,128)(2,1)S(1)}, f32[1024,256]{1,0:T(8,128)},...) custom-call(s32[8]{0:T(128)S(1)} %gather_fusion, ...), custom_call_target="tpu_custom_call" | custom-call | flops 10737418240 | bytes 41943040 | tf_op jit(solution)/shard_map/attn_fwd/pallas_call | solution.py:266
  96.4 9.2 %collective-permute-done.18 = bf16[128,2048]{1,0:T(8,128)(2,1)S(1)} collective-permute-done((bf16[128,2048]{1,0:T(8,128)(2,1)S(1)}, bf16[128,2048]{1,0:T(8,128)(2,1)S(1)}, u32[]{:S(2)}, u32[]{:S(2)}) %collective-permute-start.18) | collective-permute-done | bytes 524320 | tf_op jit(solution)/shard_map/ppermute | solution.py:50
  138.1 10.7 %collective-permute-done.37.refs_12_.refs_3_ = bf16[128,2176]{1,0:T(8,128)(2,1)S(1)} collective-permute-done((bf16[128,2176]{1,0:T(8,128)(2,1)S(1)}, bf16[128,2176]{1,0:T(8,128)(2,1)S(1)}, u32[]{:S(2)}, u32[]{:S(2)}) %collective-permute-start.37) | collective-permute-done | bytes 557088 | tf_op jit(solution)/shard_map/ppermute | solution.py:50
  161.3 8.8 %collective-permute-done.38.refs_13_.refs_4_ = bf16[128,2176]{1,0:T(8,128)(2,1)S(1)} collective-permute-done((bf16[128,2176]{1,0:T(8,128)(2,1)S(1)}, bf16[128,2176]{1,0:T(8,128)(2,1)S(1)}, u32[]{:S(2)}, u32[]{:S(2)}) %collective-permute-start.38) | collective-permute-done | bytes 557088 | tf_op jit(solution)/shard_map/ppermute | solution.py:50
  171.7 8.0 %collective-permute-done.42.refs_20_ = bf16[16,2,512,128]{3,2,1,0:T(8,128)(2,1)} collective-permute-done((bf16[16,2,512,128]{3,2,1,0:T(8,128)(2,1)}, bf16[16,2,512,128]{3,2,1,0:T(8,128)(2,1)}, u32[]{:S(2)}, u32[]{:S(2)}) %collective-permute-start.42) | collective-permute-done | bytes 4194336 | tf_op jit(solution)/shard_map/ppermute | solution.py:89
  183.3 11.6 %collective-permute-done.39.refs_14_.refs_5_ = bf16[128,2176]{1,0:T(8,128)(2,1)S(1)} collective-permute-done((bf16[128,2176]{1,0:T(8,128)(2,1)S(1)}, bf16[128,2176]{1,0:T(8,128)(2,1)S(1)}, u32[]{:S(2)}, u32[]{:S(2)}) %collective-permute-start.39) | collective-permute-done | bytes 557088 | tf_op jit(solution)/shard_map/ppermute | solution.py:50
  196.9 11.6 %collective-permute-done.25.refs_8_ = bf16[128,2048]{1,0:T(8,128)(2,1)S(1)} collective-permute-done((bf16[128,2048]{1,0:T(8,128)(2,1)S(1)}, bf16[128,2048]{1,0:T(8,128)(2,1)S(1)}, u32[]{:S(2)}, u32[]{:S(2)}) %collective-permute-start.25) | collective-permute-done | bytes 524320 | tf_op jit(solution)/shard_map/ppermute | solution.py:50
  210.6 12.1 %collective-permute-done.45.refs_24_ = bf16[16,128,512]{2,1,0:T(8,128)(2,1)} collective-permute-done((bf16[16,128,512]{2,1,0:T(8,128)(2,1)}, bf16[16,128,512]{2,1,0:T(8,128)(2,1)}, u32[]{:S(2)}, u32[]{:S(2)}) %collective-permute-start.45) | collective-permute-done | bytes 2097184 | tf_op jit(solution)/shard_map/ppermute | solution.py:89
  224.8 12.2 %collective-permute-done.27.refs_6_ = bf16[128,2048]{1,0:T(8,128)(2,1)S(1)} collective-permute-done((bf16[128,2048]{1,0:T(8,128)(2,1)S(1)}, bf16[128,2048]{1,0:T(8,128)(2,1)S(1)}, u32[]{:S(2)}, u32[]{:S(2)}) %collective-permute-start.27) | collective-permute-done | bytes 524320 | tf_op jit(solution)/shard_map/ppermute | solution.py:50
  238.3 11.8 %collective-permute-done.31.refs_5_ = bf16[128,2048]{1,0:T(8,128)(2,1)S(1)} collective-permute-done((bf16[128,2048]{1,0:T(8,128)(2,1)S(1)}, bf16[128,2048]{1,0:T(8,128)(2,1)S(1)}, u32[]{:S(2)}, u32[]{:S(2)}) %collective-permute-start.31) | collective-permute-done | bytes 524320 | tf_op jit(solution)/shard_map/ppermute | solution.py:50
  270.9 76.1 %moe.1 = (bf16[64,2176]{1,0:T(8,128)(2,1)}, bf16[64,2176]{1,0:T(8,128)(2,1)}, bf16[896,2176]{1,0:T(8,128)(2,1)}, bf16[64,2048]{1,0:T(8,128)(2,1)}, bf16[64,2048]...) custom-call(bf16[64,2048]{1,0:T(8,128)(2,1)} %copy-done.12, ...), custom_call_target="tpu_custom_call" | custom-call | flops 77309411328 | bytes 62914560 | tf_op jit(solution)/shard_map/moe/pallas_call | solution.py:532
  352.5 19.4 %moe_grad.3 = (bf16[8,2,512,128]{3,2,1,0:T(8,128)(2,1)}, bf16[8,2,512,128]{3,2,1,0:T(8,128)(2,1)}, bf16[8,2,512,128]{3,2,1,0:T(8,128)(2,1)}, bf16[8,2,512,128]{3...) custom-call(bf16[2048,1024]{1,0:T(8,128)(2,1)} %copy-done, ...), custom_call_target="tpu_custom_call" | custom-call | flops 12884901888 | bytes 31457280 | tf_op jit(solution)/shard_map/moe_grad/pallas_call | solution.py:632
  376.3 18.5 %moe_grad.2 = (bf16[8,2,512,128]{3,2,1,0:T(8,128)(2,1)}, bf16[8,2,512,128]{3,2,1,0:T(8,128)(2,1)}, bf16[8,2,512,128]{3,2,1,0:T(8,128)(2,1)}, bf16[8,2,512,128]{3...) custom-call(bf16[2048,1024]{1,0:T(8,128)(2,1)} %copy-done, ...), custom_call_target="tpu_custom_call" | custom-call | flops 12884901888 | bytes 31457280 | tf_op jit(solution)/shard_map/moe_grad/pallas_call | solution.py:632
  402.3 11.0 %collective-permute-done.57 = bf16[128,2048]{1,0:T(8,128)(2,1)S(1)} collective-permute-done((bf16[128,2048]{1,0:T(8,128)(2,1)S(1)}, bf16[128,2048]{1,0:T(8,128)(2,1)S(1)}, u32[]{:S(2)}, u32[]{:S(2)}) %collective-permute-start.57) | collective-permute-done | bytes 524320 | tf_op jit(solution)/shard_map/ppermute | solution.py:50
  415.1 8.8 %collective-permute-done.49 = bf16[128,2176]{1,0:T(8,128)(2,1)S(1)} collective-permute-done((bf16[128,2176]{1,0:T(8,128)(2,1)S(1)}, bf16[128,2176]{1,0:T(8,128)(2,1)S(1)}, u32[]{:S(2)}, u32[]{:S(2)}) %collective-permute-start.49) | collective-permute-done | bytes 557088 | tf_op jit(solution)/shard_map/ppermute | solution.py:50
  427.1 11.7 %collective-permute-done.60 = bf16[128,2048]{1,0:T(8,128)(2,1)S(1)} collective-permute-done((bf16[128,2048]{1,0:T(8,128)(2,1)S(1)}, bf16[128,2048]{1,0:T(8,128)(2,1)S(1)}, u32[]{:S(2)}, u32[]{:S(2)}) %collective-permute-start.60) | collective-permute-done | bytes 524320 | tf_op jit(solution)/shard_map/ppermute | solution.py:50
  440.6 7.9 %collective-permute-done.52 = bf16[128,2176]{1,0:T(8,128)(2,1)S(1)} collective-permute-done((bf16[128,2176]{1,0:T(8,128)(2,1)S(1)}, bf16[128,2176]{1,0:T(8,128)(2,1)S(1)}, u32[]{:S(2)}, u32[]{:S(2)}) %collective-permute-start.52) | collective-permute-done | bytes 557088 | tf_op jit(solution)/shard_map/ppermute | solution.py:50
  453.9 9.5 %collective-permute-done.61 = bf16[128,2048]{1,0:T(8,128)(2,1)S(1)} collective-permute-done((bf16[128,2048]{1,0:T(8,128)(2,1)S(1)}, bf16[128,2048]{1,0:T(8,128)(2,1)S(1)}, u32[]{:S(2)}, u32[]{:S(2)}) %collective-permute-start.61) | collective-permute-done | bytes 524320 | tf_op jit(solution)/shard_map/ppermute | solution.py:50
  476.8 10.6 %collective-permute-done.62 = bf16[128,2048]{1,0:T(8,128)(2,1)S(1)} collective-permute-done((bf16[128,2048]{1,0:T(8,128)(2,1)S(1)}, bf16[128,2048]{1,0:T(8,128)(2,1)S(1)}, u32[]{:S(2)}, u32[]{:S(2)}) %collective-permute-start.62) | collective-permute-done | bytes 524320 | tf_op jit(solution)/shard_map/ppermute | solution.py:50
  497.7 15.8 %collective-permute-done.101 = bf16[8,128,512]{2,1,0:T(8,128)(2,1)S(1)} collective-permute-done((bf16[8,128,512]{2,1,0:T(8,128)(2,1)S(1)}, bf16[8,128,512]{2,1,0:T(8,128)(2,1)S(1)}, u32[]{:S(2)}, u32[]{:S(2)}) %collective-permute-start.101) | collective-permute-done | bytes 1048608 | tf_op jit(solution)/shard_map/ppermute | solution.py:89
  516.6 19.4 %collective-permute-done.98 = bf16[8,128,512]{2,1,0:T(8,128)(2,1)S(1)} collective-permute-done((bf16[8,128,512]{2,1,0:T(8,128)(2,1)S(1)}, bf16[8,128,512]{2,1,0:T(8,128)(2,1)S(1)}, u32[]{:S(2)}, u32[]{:S(2)}) %collective-permute-start.98) | collective-permute-done | bytes 1048608 | tf_op jit(solution)/shard_map/ppermute | solution.py:89
  539.4 9.3 %collective-permute-done.63.refs_9_ = bf16[128,2048]{1,0:T(8,128)(2,1)S(1)} collective-permute-done((bf16[128,2048]{1,0:T(8,128)(2,1)S(1)}, bf16[128,2048]{1,0:T(8,128)(2,1)S(1)}, u32[]{:S(2)}, u32[]{:S(2)}) %collective-permute-start.63) | collective-permute-done | bytes 524320 | tf_op jit(solution)/shard_map/ppermute | solution.py:50
  560.5 20.5 %collective-permute-done.95 = bf16[8,2,512,128]{3,2,1,0:T(8,128)(2,1)} collective-permute-done((bf16[8,2,512,128]{3,2,1,0:T(8,128)(2,1)}, bf16[8,2,512,128]{3,2,1,0:T(8,128)(2,1)}, u32[]{:S(2)}, u32[]{:S(2)}) %collective-permute-start.95) | collective-permute-done | bytes 2097184 | tf_op jit(solution)/shard_map/ppermute | solution.py:89
  588.6 28.4 %collective-permute-done.92 = bf16[8,2,512,128]{3,2,1,0:T(8,128)(2,1)} collective-permute-done((bf16[8,2,512,128]{3,2,1,0:T(8,128)(2,1)}, bf16[8,2,512,128]{3,2,1,0:T(8,128)(2,1)}, u32[]{:S(2)}, u32[]{:S(2)}) %collective-permute-start.92) | collective-permute-done | bytes 2097184 | tf_op jit(solution)/shard_map/ppermute | solution.py:89
  622.4 26.0 %attn_bwd.1 = (bf16[64,2048]{1,0:T(8,128)(2,1)}, bf16[64,2048]{1,0:T(8,128)(2,1)S(1)}, bf16[896,2048]{1,0:T(8,128)(2,1)}, bf16[1024,768]{1,0:T(8,128)(2,1)}, f32...) custom-call(s32[8]{0:T(128)S(1)} %gather_fusion, ...), custom_call_target="tpu_custom_call" | custom-call | flops 21474836480 | bytes 41943040 | tf_op jit(solution)/shard_map/attn_bwd/pallas_call | solution.py:390
  649.2 8.3 %pad_maximum_fusion = f32[16,2,512,128]{3,2,1,0:T(8,128)} fusion(f32[8,2,512,128]{3,2,1,0:T(8,128)} %convert_add_fusion, f32[8,2,512,128]{3,2,1,0:T(8,128)} %convert_add_fusion.1), kind=kLoop, calls=%fused_computation.1 | loop fusion | flops 2097152 | bytes 16777216 | tf_op jit(solution)/shard_map/concatenate | solution.py:775
  673.4 9.2 %collective-permute-done.87 = f32[4,2,64]{2,1,0:T(2,128)S(1)} collective-permute-done((f32[4,2,64]{2,1,0:T(2,128)S(1)}, f32[4,2,64]{2,1,0:T(2,128)S(1)}, u32[]{:S(2)}, u32[]{:S(2)}) %collective-permute-start.87) | collective-permute-done | bytes 2080 | tf_op jit(solution)/shard_map/ppermute | solution.py:89
  702.3 11.9 %collective-permute-done.89 = f32[1,2,64]{2,1,0:T(2,128)S(1)} collective-permute-done((f32[1,2,64]{2,1,0:T(2,128)S(1)}, f32[1,2,64]{2,1,0:T(2,128)S(1)}, u32[]{:S(2)}, u32[]{:S(2)}) %collective-permute-start.89) | collective-permute-done | bytes 544 | tf_op jit(solution)/shard_map/ppermute | solution.py:89
  720.7 9.8 %collective-permute-done.77 = bf16[128,2048]{1,0:T(8,128)(2,1)S(1)} collective-permute-done((bf16[128,2048]{1,0:T(8,128)(2,1)S(1)}, bf16[128,2048]{1,0:T(8,128)(2,1)S(1)}, u32[]{:S(2)}, u32[]{:S(2)}) %collective-permute-start.77) | collective-permute-done | bytes 524320 | tf_op jit(solution)/shard_map/ppermute | solution.py:50
  733.8 9.3 %collective-permute-done.84 = bf16[256,512]{1,0:T(8,128)(2,1)S(1)} collective-permute-done((bf16[256,512]{1,0:T(8,128)(2,1)S(1)}, bf16[256,512]{1,0:T(8,128)(2,1)S(1)}, u32[]{:S(2)}, u32[]{:S(2)}) %collective-permute-start.84) | collective-permute-done | bytes 262176 | tf_op jit(solution)/shard_map/ppermute | solution.py:89
  (519 shorter events, 274.9 us)
Async XLA Ops:
  12.2 43.2 %collective-permute-start.11 = (bf16[3,512,256]{2,1,0:T(8,128)(2,1)}, bf16[3,512,256]{2,1,0:T(8,128)(2,1)}, u32[]{:S(2)}, u32[]{:S(2)}) collective-permute-start(bf16[3,512,256]{2,1,0:T(8,128)(2,1)} %refs_10_.3), channel_id=1, source_target_pairs={{0,8},{8,0},{16,24},{24,16},{1,9},{9,1},{17,25},{25,17},{2,10},{10... | collective-permute-start | bytes 2359304 | tf_op jit(solution)/shard_map/ppermute | solution.py:89
  12.2 29.4 %collective-permute-start.12 = (bf16[3,512,256]{2,1,0:T(8,128)(2,1)}, bf16[3,512,256]{2,1,0:T(8,128)(2,1)}, u32[]{:S(2)}, u32[]{:S(2)}) collective-permute-start(bf16[3,512,256]{2,1,0:T(8,128)(2,1)} %refs_10_.3), channel_id=1, source_target_pairs={{0,16},{8,24},{16,0},{24,8},{1,17},{9,25},{17,1},{25,9},{2,18},{10... | collective-permute-start | bytes 2359304 | tf_op jit(solution)/shard_map/ppermute | solution.py:89
  14.1 28.9 %collective-permute-start.15 = (bf16[256,512]{1,0:T(8,128)(2,1)S(1)}, bf16[256,512]{1,0:T(8,128)(2,1)S(1)}, u32[]{:S(2)}, u32[]{:S(2)}) collective-permute-start(bf16[256,512]{1,0:T(8,128)(2,1)S(1)} %copy-done.32), channel_id=1, source_target_pairs={{0,16},{8,24},{16,0},{24,8},{1,17},{9,25},{17,1},{25,9},{2,18},{10... | collective-permute-start | bytes 786440 | tf_op jit(solution)/shard_map/ppermute | solution.py:89
  85.9 93.8 %collective-permute-start.42 = (bf16[16,2,512,128]{3,2,1,0:T(8,128)(2,1)}, bf16[16,2,512,128]{3,2,1,0:T(8,128)(2,1)}, u32[]{:S(2)}, u32[]{:S(2)}) collective-permute-start(bf16[16,2,512,128]{3,2,1,0:T(8,128)(2,1)} %refs_18_.1), channel_id=1, source_target_pairs={{0,16},{8,24},{16,0},{24,8},{1,17},{9,25},{17,1},{25,9},{2,18},{10... | collective-permute-start | bytes 12582920 | tf_op jit(solution)/shard_map/ppermute | solution.py:89
  123.1 25.8 %collective-permute-start.37 = (bf16[128,2176]{1,0:T(8,128)(2,1)S(1)}, bf16[128,2176]{1,0:T(8,128)(2,1)S(1)}, u32[]{:S(2)}, u32[]{:S(2)}) collective-permute-start(bf16[128,2176]{1,0:T(8,128)(2,1)S(1)} %pad_dynamic-update-slice_fusion.refs_11_.refs_2_), channel_id=1, source_target_pairs={{0,1},{2,0},{4,2},{6,4},{7,6},{5,7},{3,5},{1,3},{8,9},{10,8},{12,1... | collective-permute-start | bytes 1671176 | tf_op jit(solution)/shard_map/ppermute | solution.py:50
  150.9 28.9 %collective-permute-start.20 = (bf16[128,2048]{1,0:T(8,128)(2,1)S(1)}, bf16[128,2048]{1,0:T(8,128)(2,1)S(1)}, u32[]{:S(2)}, u32[]{:S(2)}) collective-permute-start(bf16[128,2048]{1,0:T(8,128)(2,1)S(1)} %get-tuple-element.129), channel_id=1, source_target_pairs={{0,2},{2,4},{4,6},{6,7},{7,5},{5,3},{3,1},{1,0},{8,10},{10,12},{12... | collective-permute-start | bytes 1572872 | tf_op jit(solution)/shard_map/ppermute | solution.py:50
  170.1 52.5 %collective-permute-start.45 = (bf16[16,128,512]{2,1,0:T(8,128)(2,1)}, bf16[16,128,512]{2,1,0:T(8,128)(2,1)}, u32[]{:S(2)}, u32[]{:S(2)}) collective-permute-start(bf16[16,128,512]{2,1,0:T(8,128)(2,1)} %refs_22_.1), channel_id=1, source_target_pairs={{0,16},{8,24},{16,0},{24,8},{1,17},{9,25},{17,1},{25,9},{2,18},{10... | collective-permute-start | bytes 6291464 | tf_op jit(solution)/shard_map/ppermute | solution.py:89
  171.7 99.1 %collective-permute-start.41 = (bf16[16,2,512,128]{3,2,1,0:T(8,128)(2,1)}, bf16[16,2,512,128]{3,2,1,0:T(8,128)(2,1)}, u32[]{:S(2)}, u32[]{:S(2)}) collective-permute-start(bf16[16,2,512,128]{3,2,1,0:T(8,128)(2,1)} %refs_18_.1), channel_id=1, source_target_pairs={{0,8},{8,0},{16,24},{24,16},{1,9},{9,1},{17,25},{25,17},{2,10},{10... | collective-permute-start | bytes 12582920 | tf_op jit(solution)/shard_map/ppermute | solution.py:89
  179.7 91.2 %collective-permute-start.43 = (bf16[16,2,512,128]{3,2,1,0:T(8,128)(2,1)}, bf16[16,2,512,128]{3,2,1,0:T(8,128)(2,1)}, u32[]{:S(2)}, u32[]{:S(2)}) collective-permute-start(bf16[16,2,512,128]{3,2,1,0:T(8,128)(2,1)} %collective-permute-done.42.refs_20_), channel_id=1, source_target_pairs={{0,8},{8,0},{16,24},{24,16},{1,9},{9,1},{17,25},{25,17},{2,10},{10... | collective-permute-start | bytes 12582920 | tf_op jit(solution)/shard_map/ppermute | solution.py:89
  222.7 48.2 %collective-permute-start.44 = (bf16[16,128,512]{2,1,0:T(8,128)(2,1)}, bf16[16,128,512]{2,1,0:T(8,128)(2,1)}, u32[]{:S(2)}, u32[]{:S(2)}) collective-permute-start(bf16[16,128,512]{2,1,0:T(8,128)(2,1)} %refs_22_.1), channel_id=1, source_target_pairs={{0,8},{8,0},{16,24},{24,16},{1,9},{9,1},{17,25},{25,17},{2,10},{10... | collective-permute-start | bytes 6291464 | tf_op jit(solution)/shard_map/ppermute | solution.py:89
  222.7 48.2 %collective-permute-start.46 = (bf16[16,128,512]{2,1,0:T(8,128)(2,1)}, bf16[16,128,512]{2,1,0:T(8,128)(2,1)}, u32[]{:S(2)}, u32[]{:S(2)}) collective-permute-start(bf16[16,128,512]{2,1,0:T(8,128)(2,1)} %collective-permute-done.45.refs_24_), channel_id=1, source_target_pairs={{0,8},{8,0},{16,24},{24,16},{1,9},{9,1},{17,25},{25,17},{2,10},{10... | collective-permute-start | bytes 6291464 | tf_op jit(solution)/shard_map/ppermute | solution.py:89
  347.0 25.1 %collective-permute-start.55 = (bf16[64,2048]{1,0:T(8,128)(2,1)}, bf16[64,2048]{1,0:T(8,128)(2,1)S(1)}, u32[]{:S(2)}, u32[]{:S(2)}) collective-permute-start(bf16[64,2048]{1,0:T(8,128)(2,1)} %get-tuple-element.62), channel_id=1, source_target_pairs={{0,2},{2,4},{4,6},{6,7},{7,5},{5,3},{3,1},{1,0},{8,10},{10,12},{12... | collective-permute-start | bytes 786440 | tf_op jit(solution)/shard_map/ppermute | solution.py:50
  348.7 53.5 %collective-permute-start.59 = (bf16[64,2048]{1,0:T(8,128)(2,1)}, bf16[64,2048]{1,0:T(8,128)(2,1)}, u32[]{:S(2)}, u32[]{:S(2)}) collective-permute-start(bf16[64,2048]{1,0:T(8,128)(2,1)} %get-tuple-element.63), channel_id=1, source_target_pairs={{0,1},{2,0},{4,2},{6,4},{7,6},{5,7},{3,5},{1,3},{8,9},{10,8},{12,1... | collective-permute-start | bytes 786440 | tf_op jit(solution)/shard_map/ppermute | solution.py:50
  349.1 24.8 %collective-permute-start.47 = (bf16[64,2176]{1,0:T(8,128)(2,1)}, bf16[64,2176]{1,0:T(8,128)(2,1)S(1)}, u32[]{:S(2)}, u32[]{:S(2)}) collective-permute-start(bf16[64,2176]{1,0:T(8,128)(2,1)} %get-tuple-element.59), channel_id=1, source_target_pairs={{0,2},{2,4},{4,6},{6,7},{7,5},{5,3},{3,1},{1,0},{8,10},{10,12},{12... | collective-permute-start | bytes 835592 | tf_op jit(solution)/shard_map/ppermute | solution.py:50
  350.7 63.8 %collective-permute-start.51 = (bf16[64,2176]{1,0:T(8,128)(2,1)}, bf16[64,2176]{1,0:T(8,128)(2,1)}, u32[]{:S(2)}, u32[]{:S(2)}) collective-permute-start(bf16[64,2176]{1,0:T(8,128)(2,1)} %get-tuple-element.60), channel_id=1, source_target_pairs={{0,1},{2,0},{4,2},{6,4},{7,6},{5,7},{3,5},{1,3},{8,9},{10,8},{12,1... | collective-permute-start | bytes 835592 | tf_op jit(solution)/shard_map/ppermute | solution.py:50
  372.0 77.1 %collective-permute-start.94 = (bf16[8,2,512,128]{3,2,1,0:T(8,128)(2,1)}, bf16[8,2,512,128]{3,2,1,0:T(8,128)(2,1)}, u32[]{:S(2)}, u32[]{:S(2)}) collective-permute-start(bf16[8,2,512,128]{3,2,1,0:T(8,128)(2,1)} %get-tuple-element.90), channel_id=1, source_target_pairs={{0,8},{8,0},{16,24},{24,16},{1,9},{9,1},{17,25},{25,17},{2,10},{10... | collective-permute-start | bytes 6291464 | tf_op jit(solution)/shard_map/ppermute | solution.py:89
  402.2 135.4 %collective-permute-start.93 = (bf16[8,2,512,128]{3,2,1,0:T(8,128)(2,1)S(1)}, bf16[8,2,512,128]{3,2,1,0:T(8,128)(2,1)S(1)}, u32[]{:S(2)}, u32[]{:S(2)}) collective-permute-start(bf16[8,2,512,128]{3,2,1,0:T(8,128)(2,1)S(1)} %copy-done.92), channel_id=1, source_target_pairs={{0,8},{8,0},{16,24},{24,16},{1,9},{9,1},{17,25},{25,17},{2,10},{10... | collective-permute-start | bytes 6291464 | tf_op jit(solution)/shard_map/ppermute | solution.py:89
  414.6 58.6 %collective-permute-start.91 = (bf16[8,2,512,128]{3,2,1,0:T(8,128)(2,1)S(1)}, bf16[8,2,512,128]{3,2,1,0:T(8,128)(2,1)S(1)}, u32[]{:S(2)}, u32[]{:S(2)}) collective-permute-start(bf16[8,2,512,128]{3,2,1,0:T(8,128)(2,1)S(1)} %copy-done.93), channel_id=1, source_target_pairs={{0,8},{8,0},{16,24},{24,16},{1,9},{9,1},{17,25},{25,17},{2,10},{10... | collective-permute-start | bytes 6291464 | tf_op jit(solution)/shard_map/ppermute | solution.py:89
  438.8 37.4 %collective-permute-start.58 = (bf16[128,2048]{1,0:T(8,128)(2,1)S(1)}, bf16[128,2048]{1,0:T(8,128)(2,1)S(1)}, u32[]{:S(2)}, u32[]{:S(2)}) collective-permute-start(bf16[128,2048]{1,0:T(8,128)(2,1)S(1)} %get-tuple-element.127), channel_id=1, source_target_pairs={{0,2},{2,4},{4,6},{6,7},{7,5},{5,3},{3,1},{1,0},{8,10},{10,12},{12... | collective-permute-start | bytes 1572872 | tf_op jit(solution)/shard_map/ppermute | solution.py:50
  487.4 26.1 %collective-permute-start.101 = (bf16[8,128,512]{2,1,0:T(8,128)(2,1)S(1)}, bf16[8,128,512]{2,1,0:T(8,128)(2,1)S(1)}, u32[]{:S(2)}, u32[]{:S(2)}) collective-permute-start(bf16[8,128,512]{2,1,0:T(8,128)(2,1)S(1)} %add_convert_fusion.2), channel_id=1, source_target_pairs={{0,16},{8,24},{16,0},{24,8},{1,17},{9,25},{17,1},{25,9},{2,18},{10... | collective-permute-start | bytes 3145736 | tf_op jit(solution)/shard_map/ppermute | solution.py:89
  495.3 40.6 %collective-permute-start.98 = (bf16[8,128,512]{2,1,0:T(8,128)(2,1)S(1)}, bf16[8,128,512]{2,1,0:T(8,128)(2,1)S(1)}, u32[]{:S(2)}, u32[]{:S(2)}) collective-permute-start(bf16[8,128,512]{2,1,0:T(8,128)(2,1)S(1)} %add_convert_fusion.3), channel_id=1, source_target_pairs={{0,16},{8,24},{16,0},{24,8},{1,17},{9,25},{17,1},{25,9},{2,18},{10... | collective-permute-start | bytes 3145736 | tf_op jit(solution)/shard_map/ppermute | solution.py:89
  497.0 91.6 %collective-permute-start.90 = (bf16[8,2,512,128]{3,2,1,0:T(8,128)(2,1)}, bf16[8,2,512,128]{3,2,1,0:T(8,128)(2,1)}, u32[]{:S(2)}, u32[]{:S(2)}) collective-permute-start(bf16[8,2,512,128]{3,2,1,0:T(8,128)(2,1)} %get-tuple-element.84), channel_id=1, source_target_pairs={{0,8},{8,0},{16,24},{24,16},{1,9},{9,1},{17,25},{25,17},{2,10},{10... | collective-permute-start | bytes 6291464 | tf_op jit(solution)/shard_map/ppermute | solution.py:89
  497.1 83.9 %collective-permute-start.95 = (bf16[8,2,512,128]{3,2,1,0:T(8,128)(2,1)}, bf16[8,2,512,128]{3,2,1,0:T(8,128)(2,1)}, u32[]{:S(2)}, u32[]{:S(2)}) collective-permute-start(bf16[8,2,512,128]{3,2,1,0:T(8,128)(2,1)} %add_convert_fusion), channel_id=1, source_target_pairs={{0,16},{8,24},{16,0},{24,8},{1,17},{9,25},{17,1},{25,9},{2,18},{10... | collective-permute-start | bytes 6291464 | tf_op jit(solution)/shard_map/ppermute | solution.py:89
  513.5 103.5 %collective-permute-start.92 = (bf16[8,2,512,128]{3,2,1,0:T(8,128)(2,1)}, bf16[8,2,512,128]{3,2,1,0:T(8,128)(2,1)}, u32[]{:S(2)}, u32[]{:S(2)}) collective-permute-start(bf16[8,2,512,128]{3,2,1,0:T(8,128)(2,1)} %add_convert_fusion.1), channel_id=1, source_target_pairs={{0,16},{8,24},{16,0},{24,8},{1,17},{9,25},{17,1},{25,9},{2,18},{10... | collective-permute-start | bytes 6291464 | tf_op jit(solution)/shard_map/ppermute | solution.py:89
  557.9 28.6 %collective-permute-start.65 = (bf16[128,2048]{1,0:T(8,128)(2,1)S(1)}, bf16[128,2048]{1,0:T(8,128)(2,1)S(1)}, u32[]{:S(2)}, u32[]{:S(2)}) collective-permute-start(bf16[128,2048]{1,0:T(8,128)(2,1)S(1)} %collective-permute-done.64.refs_8_), channel_id=1, source_target_pairs={{0,2},{2,4},{4,6},{6,7},{7,5},{5,3},{3,1},{1,0},{8,10},{10,12},{12... | collective-permute-start | bytes 1572872 | tf_op jit(solution)/shard_map/ppermute | solution.py:50
  559.5 28.7 %collective-permute-start.69 = (bf16[128,2048]{1,0:T(8,128)(2,1)S(1)}, bf16[128,2048]{1,0:T(8,128)(2,1)S(1)}, u32[]{:S(2)}, u32[]{:S(2)}) collective-permute-start(bf16[128,2048]{1,0:T(8,128)(2,1)S(1)} %collective-permute-done.68.refs_5_), channel_id=1, source_target_pairs={{0,1},{2,0},{4,2},{6,4},{7,6},{5,7},{3,5},{1,3},{8,9},{10,8},{12,1... | collective-permute-start | bytes 1572872 | tf_op jit(solution)/shard_map/ppermute | solution.py:50
  586.5 35.9 %collective-permute-start.66 = (bf16[64,2048]{1,0:T(8,128)(2,1)S(1)}, bf16[64,2048]{1,0:T(8,128)(2,1)S(1)}, u32[]{:S(2)}, u32[]{:S(2)}) collective-permute-start(bf16[64,2048]{1,0:T(8,128)(2,1)S(1)} %slice.439), channel_id=1, source_target_pairs={{0,2},{2,4},{4,6},{6,7},{7,5},{5,3},{3,1},{1,0},{8,10},{10,12},{12... | collective-permute-start | bytes 786440 | tf_op jit(solution)/shard_map/ppermute | solution.py:50
  588.2 34.2 %collective-permute-start.70 = (bf16[64,2048]{1,0:T(8,128)(2,1)S(1)}, bf16[64,2048]{1,0:T(8,128)(2,1)S(1)}, u32[]{:S(2)}, u32[]{:S(2)}) collective-permute-start(bf16[64,2048]{1,0:T(8,128)(2,1)S(1)} %slice.440), channel_id=1, source_target_pairs={{0,1},{2,0},{4,2},{6,4},{7,6},{5,7},{3,5},{1,3},{8,9},{10,8},{12,1... | collective-permute-start | bytes 786440 | tf_op jit(solution)/shard_map/ppermute | solution.py:50
  659.2 35.9 %collective-permute-start.75 = (bf16[64,2048]{1,0:T(8,128)(2,1)S(1)}, bf16[64,2048]{1,0:T(8,128)(2,1)}, u32[]{:S(2)}, u32[]{:S(2)}) collective-permute-start(bf16[64,2048]{1,0:T(8,128)(2,1)S(1)} %get-tuple-element.73), channel_id=1, source_target_pairs={{0,1},{2,0},{4,2},{6,4},{7,6},{5,7},{3,5},{1,3},{8,9},{10,8},{12,1... | collective-permute-start | bytes 786440 | tf_op jit(solution)/shard_map/ppermute | solution.py:50
  672.8 43.4 %collective-permute-start.80 = (bf16[3,512,256]{2,1,0:T(8,128)(2,1)}, bf16[3,512,256]{2,1,0:T(8,128)(2,1)}, u32[]{:S(2)}, u32[]{:S(2)}) collective-permute-start(bf16[3,512,256]{2,1,0:T(8,128)(2,1)} %get-tuple-element.132), channel_id=1, source_target_pairs={{0,8},{8,0},{16,24},{24,16},{1,9},{9,1},{17,25},{25,17},{2,10},{10... | collective-permute-start | bytes 2359304 | tf_op jit(solution)/shard_map/ppermute | solution.py:89
  672.9 71.3 %collective-permute-start.79 = (bf16[3,512,256]{2,1,0:T(8,128)(2,1)}, bf16[3,512,256]{2,1,0:T(8,128)(2,1)}, u32[]{:S(2)}, u32[]{:S(2)}) collective-permute-start(bf16[3,512,256]{2,1,0:T(8,128)(2,1)} %get-tuple-element.131), channel_id=1, source_target_pairs={{0,8},{8,0},{16,24},{24,16},{1,9},{9,1},{17,25},{25,17},{2,10},{10... | collective-permute-start | bytes 2359304 | tf_op jit(solution)/shard_map/ppermute | solution.py:89
  717.6 26.6 %collective-permute-start.81 = (bf16[3,512,256]{2,1,0:T(8,128)(2,1)S(1)}, bf16[3,512,256]{2,1,0:T(8,128)(2,1)S(1)}, u32[]{:S(2)}, u32[]{:S(2)}) collective-permute-start(bf16[3,512,256]{2,1,0:T(8,128)(2,1)S(1)} %fusion), channel_id=1, source_target_pairs={{0,16},{8,24},{16,0},{24,8},{1,17},{9,25},{17,1},{25,9},{2,18},{10... | collective-permute-start | bytes 2359304 | tf_op jit(solution)/shard_map/ppermute | solution.py:89
  (167 other events, 3646.3 us)

commit v2 on v1

v2 whole, which is shorter than its diff:
```python
import functools

import jax
import jax.numpy as jnp
import numpy as np
from jax import lax
from jax.experimental import pallas as pl
from jax.experimental.pallas import tpu as pltpu
from jax.sharding import PartitionSpec as P

HD = 128
E = 16
EPSILON = 1e-05
ROPE_BASE = 10000.0
MASKED = -1e30
LANES = 128
CHUNKS = 4
VMEM_BYTES = 60 << 20

f32 = jnp.float32
bf16 = jnp.bfloat16
NT = (((1,), (1,)), ((), ()))
TN = (((0,), (0,)), ((), ()))
ANY = pl.BlockSpec(memory_space=pl.ANY)
SMEM = pl.BlockSpec(memory_space=pltpu.SMEM)
VMEM = pl.BlockSpec(memory_space=pltpu.VMEM)


def dot(a, b):
    return jnp.dot(a, b, preferred_element_type=f32)


def dot_nt(a, b):
    return lax.dot_general(a, b, NT, preferred_element_type=f32)


def dot_tn(a, b):
    return lax.dot_general(a, b, TN, preferred_element_type=f32)


def shape(dims, dtype):
    return jax.ShapeDtypeStruct(dims, dtype)


def ring_of(groups):
    return list(range(0, groups, 2)) + list(range(groups - 1, 0, -2))


def distances_of(groups):
    steps = groups // 2
    near = [s * k for k in range(steps - 1, 0, -1) for s in (1, -1)]
    return [steps] + near + [0]


def ring_step(value, groups, sign):
    ring = ring_of(groups)
    pairs = [(ring[p], ring[(p + sign) % groups]) for p in range(groups)]
    return lax.ppermute(value, "tensor", pairs)


def tie(values, after):
    values, after = tuple(values), tuple(after)
    return lax.optimization_barrier(values + after)[: len(values)]


class Gather:
    def __init__(self, own, groups):
        self.groups, self.steps = groups, groups // 2
        self.below, self.above = [own], [own]

    def step(self, after=()):
        low, high = self.below[-1], self.above[-1]
        if len(self.below) == self.steps:
            half = low.shape[0] // 2
            low, high = low[:half], high[half:]
        if after:
            low, high = tie((low, high), after)
        self.below.append(ring_step(low, self.groups, 1))
        self.above.append(ring_step(high, self.groups, -1))
        return [self.below[-1], self.above[-1]]

    def run(self):
        while len(self.below) <= self.steps:
            self.step()
        return self

    def at(self, distance):
        return self.above[distance] if distance >= 0 else self.below[-distance]

    def far(self):
        return [self.below[self.steps], self.above[self.steps]]

    def pieces(self):
        return self.far() + [self.at(k) for k in distances_of(self.groups)[1:]]


class Scatter:
    def __init__(self, pieces, groups):
        self.groups, self.steps, self.done = groups, groups // 2, 0
        self.far = pieces[:2]
        self.block = dict(zip(distances_of(groups)[1:], pieces[2:]))

    def step(self, after=(), riders=None):
        if self.done == 0:
            sent = self.far
        else:
            distance = self.steps - self.done
            low, high = (v.astype(f32) for v in self.moved)
            if self.done == 1:
                half = low.shape[0]
                low = jnp.pad(low, ((0, half), (0, 0)))
                high = jnp.pad(high, ((half, 0), (0, 0)))
            dtype = self.far[0].dtype
            low = (self.block[distance].astype(f32) + low).astype(dtype)
            high = (self.block[-distance].astype(f32) + high).astype(dtype)
            sent = [low, high]
        rows, columns = sent[0].shape
        if riders:
            riders = [jnp.pad(r, ((0, 0), (0, columns - r.shape[1]))) for r in riders]
            sent = [jnp.concatenate(pair, axis=0) for pair in zip(sent, riders)]
        if after:
            sent = tie(sent, after)
        self.moved = [ring_step(sent[0], self.groups, 1), ring_step(sent[1], self.groups, -1)]
        self.done += 1
        if riders:
            self.ridden = [m[rows:] for m in self.moved]
            self.moved = [m[:rows] for m in self.moved]
        return self.moved

    def run(self):
        while self.done < self.steps:
            self.step()
        return self

    def result(self):
        low, high = self.moved
        return self.block[0].astype(f32) + low.astype(f32) + high.astype(f32)


def bits_of(count):
    return [1 << b for b in range(count.bit_length() - 1)]


def flip_step(value, axis, count, bit):
    return lax.ppermute(value, axis, [(s, s ^ bit) for s in range(count)])


def relative(parts, axis):
    count = len(parts)
    index = lax.axis_index(axis)
    for bit in bits_of(count):
        turned = (index & bit) != 0
        parts = [jnp.where(turned, parts[k ^ bit], parts[k]) for k in range(count)]
    return parts


def split_last(value, count):
    width = value.shape[-1] // count
    return [value[..., k * width : (k + 1) * width] for k in range(count)]


def flip_reduce(keep, sent, axis, count):
    return flip_rest(keep, flip_step(sent, axis, count, 1), axis, count)


def flip_rest(keep, got, axis, count):
    for bit in bits_of(count)[1:]:
        odd = (keep[1::2].astype(f32) + got[1::2].astype(f32)).astype(bf16)
        more = flip_step(odd, axis, count, bit)
        if 2 * bit < count:
            keep = (keep[0::2].astype(f32) + got[0::2].astype(f32)).astype(bf16)
            got = more
    return [keep, got, more, odd]


def flip_reduce_rows(value, axis, count):
    for bit in bits_of(count):
        pairs = value.reshape((value.shape[0] // 2, 2) + value.shape[1:])
        value = pairs[:, 0] + flip_step(pairs[:, 1], axis, count, bit)
    return value[0]


def fetch(sources, target, sems, first, rows_at):
    copies = []
    for number, source in enumerate(sources):
        if source.shape[1] > target.shape[1]:
            source = source.at[:, pl.ds(0, target.shape[1])]
        copy = pltpu.make_async_copy(
            source, target.at[pl.ds(rows_at[number], source.shape[0])], sems.at[first + number]
        )
        copy.start()
        copies.append(copy)
    return copies


def load_projections(weights, wqs, sems, first):
    copies = []
    n, _, width = weights.shape
    depth = wqs.shape[0] // n
    for k in range(n):
        for j in range(3):
            source = weights.at[k, pl.ds(j * depth, depth)]
            target = wqs.at[pl.ds(k * depth, depth), pl.ds(j * width, width)]
            copies.append(pltpu.make_async_copy(source, target, sems.at[first + 3 * k + j]))
    return copies


def load_outputs(weights, wos, sems, first):
    copies = []
    n, _, width = weights.shape
    depth = wos.shape[1] // n
    cuts = max(1, depth // width)
    columns = depth // cuts
    for k in range(n):
        for c in range(cuts):
            source = weights.at[k, pl.ds(3 * depth + c * width, width), pl.ds(0, columns)]
            target = wos.at[:, pl.ds(k * depth + c * columns, columns)]
            copies.append(pltpu.make_async_copy(source, target, sems.at[first + cuts * k + c]))
    return copies


def output_copies(n, depth, width):
    return n * max(1, depth // width)


def piece_shapes(own_rows, columns, count):
    half = shape((own_rows // 2, columns), bf16)
    return [half, half] + [shape((own_rows, columns), bf16)] * (count - 2)


def cost(micros):
    return pl.CostEstimate(flops=int(micros * 6e8), bytes_accessed=1 << 20, transcendentals=0)


def piece_rows(order, half, pieces):
    rows = 2 * half
    starts = [pl.multiple_of(order[0] * rows, rows)]
    starts.append(pl.multiple_of(order[0] * rows + half, half))
    for number in range(2, pieces):
        starts.append(pl.multiple_of(order[number - 1] * rows, rows))
    return starts


def send_out(staged, targets, sems, first, starts):
    copies = []
    for number, target in enumerate(targets):
        copy = pltpu.make_async_copy(
            staged.at[pl.ds(starts[number], target.shape[0])], target, sems.at[first + number]
        )
        copy.start()
        copies.append(copy)
    return copies


def allowed_pairs(seg_col, seg_row, first, rows, width):
    row_pos = first + lax.broadcasted_iota(jnp.int32, (rows, width), 0)
    key_pos = lax.broadcasted_iota(jnp.int32, (rows, width), 1)
    return (seg_col[pl.ds(first, rows), :] == seg_row[:, pl.ds(0, width)]) & (key_pos <= row_pos)


def attn_proj_body(count, block, *refs):
    it = iter(refs)
    order = next(it)
    pieces = [next(it) for _ in range(count)]
    wq = next(it)
    gain, gains, cosine, sine = (next(it) for _ in range(4))
    q_o, k_o, v_o, qr_o, kr_o, x_o = (next(it) for _ in range(6))
    xs, xn, wqs, sems = (next(it) for _ in range(4))
    length, width = q_o.shape
    heads = width // HD
    starts = piece_rows(order, pieces[0].shape[0], count)
    copies = load_projections(wq, wqs, sems, count)
    for copy in copies:
        copy.start()
    for copy in fetch(pieces, xs, sems, 0, starts) + copies:
        copy.wait()

    def project(r, _):
        rows = pl.ds(pl.multiple_of(r * block, block), block)
        wide = xs[rows, :].astype(f32)
        inv = lax.rsqrt(jnp.mean(wide * wide, axis=-1, keepdims=True) + EPSILON)
        xn[rows, :] = (wide * inv * gain[...]).astype(bf16)
        out = dot(xn[rows, :], wqs[...])
        v_o[rows, :] = out[:, 2 * width :].astype(bf16)
        for j, (raw_o, hat_o) in enumerate(((qr_o, q_o), (kr_o, k_o))):
            raw = out[:, j * width : (j + 1) * width]
            raw_o[rows, :] = raw
            for h in range(heads):
                cols = slice(h * HD, (h + 1) * HD)
                u = raw[:, cols]
                inv = lax.rsqrt(jnp.mean(u * u, axis=-1, keepdims=True) + EPSILON)
                u = u * inv * gains[j : j + 1, cols]
                u = u * cosine[rows, :] + pltpu.roll(u, HD // 2, 1) * sine[rows, :]
                hat_o[rows, cols] = u.astype(bf16)
        return 0

    lax.fori_loop(0, length // block, project, 0)
    keep = pltpu.make_async_copy(xn, x_o, sems.at[0])
    keep.start()
    keep.wait()


def attn_proj(order, pieces, wq, gain, gains, cosine, sine):
    n, count = wq.shape[0], len(pieces)
    d = gain.shape[1]
    length = cosine.shape[0]
    width = wq.shape[2]
    return pl.pallas_call(
        functools.partial(attn_proj_body, count, min(256, length)),
        in_specs=[SMEM] + [ANY] * (count + 1) + [VMEM] * 4,
        out_specs=[VMEM] * 5 + [ANY],
        out_shape=[shape((length, width), bf16)] * 3
        + [shape((length, width), f32)] * 2
        + [shape((length, d), bf16)],
        scratch_shapes=[
            pltpu.VMEM((length, d), bf16),
            pltpu.VMEM((length, d), bf16),
            pltpu.VMEM((d, 3 * width), bf16),
            pltpu.SemaphoreType.DMA((count + 3 * n,)),
        ],
        compiler_params=pltpu.CompilerParams(vmem_limit_bytes=VMEM_BYTES),
        cost_estimate=cost(10),
        name="attn_proj",
    )(order, *pieces, wq, gain, gains, cosine, sine)


def attn_core_body(count, block, *refs):
    it = iter(refs)
    order = next(it)
    wo = next(it)
    q, k_, v, seg_row, seg_col = (next(it) for _ in range(5))
    ctx_o, lse_o = next(it), next(it)
    outs = [next(it) for _ in range(count)]
    wos, stage, sems = (next(it) for _ in range(3))
    length, width = ctx_o.shape
    heads = width // HD
    starts = piece_rows(order, outs[0].shape[0], count)
    copies = load_outputs(wo, wos, sems, count)
    for copy in copies:
        copy.start()
    scale = HD ** (-0.5)
    for b in range(length // block):
        rows = pl.ds(b * block, block)
        hi = (b + 1) * block
        allowed = allowed_pairs(seg_col, seg_row, b * block, block, hi)
        for h in range(heads):
            cols = slice(h * HD, (h + 1) * HD)
            s = dot_nt(q[rows, cols], k_[pl.ds(0, hi), cols]) * scale
            s = jnp.where(allowed, s, MASKED)
            top = jnp.max(s, axis=-1, keepdims=True)
            e = jnp.exp(s - top)
            total = jnp.sum(e, axis=-1, keepdims=True)
            probs = (e * (1.0 / total)).astype(bf16)
            ctx_o[rows, cols] = dot(probs, v[pl.ds(0, hi), cols]).astype(bf16)
            lse_o[h, rows, :] = top + jnp.log(total)
    for copy in copies:
        copy.wait()
    stage[...] = dot(ctx_o[...], wos[...]).astype(bf16)
    for copy in send_out(stage, outs, sems, 0, starts):
        copy.wait()


def attn_core(order, wo, q, k, v, seg_row, seg_col, own_rows, d):
    n = wo.shape[0]
    length, width = q.shape
    count = length // own_rows + 1
    return pl.pallas_call(
        functools.partial(attn_core_body, count, min(256, length)),
        in_specs=[SMEM] + [ANY] + [VMEM] * 5,
        out_specs=[VMEM] * 2 + [ANY] * count,
        out_shape=[shape((length, width), bf16), shape((width // HD, length, 1), f32)]
        + piece_shapes(own_rows, d, count),
        scratch_shapes=[
            pltpu.VMEM((width, d), bf16),
            pltpu.VMEM((length, d), bf16),
            pltpu.SemaphoreType.DMA((count + output_copies(n, d // n, width),)),
        ],
        compiler_params=pltpu.CompilerParams(vmem_limit_bytes=36 << 20),
        cost_estimate=cost(10),
        name="attn_core",
    )(order, wo, q, k, v, seg_row, seg_col)


def attn_back_body(count, block, *refs):
    it = iter(refs)
    order = next(it)
    pieces = [next(it) for _ in range(count)]
    wo = next(it)
    q, k_, v, lse, seg_row, seg_col = (next(it) for _ in range(6))
    dq_o, dk_o, dv_o, db_o = (next(it) for _ in range(4))
    db, wos, dctx, sems = (next(it) for _ in range(4))
    length, width = q.shape
    heads = width // HD
    starts = piece_rows(order, pieces[0].shape[0], count)
    copies = load_outputs(wo, wos, sems, count)
    for copy in copies:
        copy.start()
    for copy in copies + fetch(pieces, db, sems, 0, starts):
        copy.wait()
    keep = pltpu.make_async_copy(db, db_o, sems.at[0])
    keep.start()
    scale = HD ** (-0.5)
    dctx[...] = dot_nt(db[...], wos[...]).astype(bf16)
    dk_o[...] = jnp.zeros_like(dk_o)
    dv_o[...] = jnp.zeros_like(dv_o)
    for b in range(length // block):
        rows = pl.ds(b * block, block)
        hi = (b + 1) * block
        low = pl.ds(0, hi)
        allowed = allowed_pairs(seg_col, seg_row, b * block, block, hi)
        for h in range(heads):
            cols = slice(h * HD, (h + 1) * HD)
            s = dot_nt(q[rows, cols], k_[low, cols]) * scale
            p = jnp.where(allowed, jnp.exp(s - lse[h, rows, :]), 0.0)
            g = dot_nt(dctx[rows, cols], v[low, cols])
            pg = p * g
            ds = (pg - p * jnp.sum(pg, axis=-1, keepdims=True)).astype(bf16)
            dq_o[rows, cols] = dot(ds, k_[low, cols]) * scale
            dk_o[low, cols] += dot_tn(ds, q[rows, cols]) * scale
            dv_o[low, cols] += dot_tn(p.astype(bf16), dctx[rows, cols])
    keep.wait()


def attn_back(order, pieces, wo, q, k, v, lse, seg_row, seg_col):
    n, count = wo.shape[0], len(pieces)
    d = pieces[0].shape[1]
    length, width = q.shape
    return pl.pallas_call(
        functools.partial(attn_back_body, count, min(256, length)),
        in_specs=[SMEM] + [ANY] * (count + 1) + [VMEM] * 6,
        out_specs=[VMEM] * 3 + [ANY],
        out_shape=[shape((length, width), f32)] * 3 + [shape((length, d), bf16)],
        scratch_shapes=[
            pltpu.VMEM((length, d), bf16),
            pltpu.VMEM((width, d), bf16),
            pltpu.VMEM((length, width), bf16),
            pltpu.SemaphoreType.DMA((count + output_copies(n, d // n, width),)),
        ],
        compiler_params=pltpu.CompilerParams(vmem_limit_bytes=VMEM_BYTES),
        cost_estimate=cost(14),
        name="attn_back",
    )(order, *pieces, wo, q, k, v, lse, seg_row, seg_col)


def proj_back_body(count, block, *refs):
    it = iter(refs)
    order = next(it)
    wq = next(it)
    qr, kr, dq, dk, dv = (next(it) for _ in range(5))
    gains, cosine, sine, x = (next(it) for _ in range(4))
    dp_o, hg_o, gs_o = (next(it) for _ in range(3))
    outs = [next(it) for _ in range(count)]
    wqs, stage, sems = (next(it) for _ in range(3))
    length, width = qr.shape
    heads = width // HD
    starts = piece_rows(order, outs[0].shape[0], count)
    copies = load_projections(wq, wqs, sems, count)
    for copy in copies:
        copy.start()
    hg_o[...] = jnp.zeros_like(hg_o)
    gs_o[...] = jnp.zeros_like(gs_o)
    for copy in copies:
        copy.wait()

    def finish(r, _):
        rows = pl.ds(pl.multiple_of(r * block, block), block)
        dp_o[rows, 2 * width :] = dv[rows, :].astype(bf16)
        for j, (raw, grad) in enumerate(((qr, dq), (kr, dk))):
            for h in range(heads):
                cols = slice(h * HD, (h + 1) * HD)
                u = raw[rows, cols]
                inv = lax.rsqrt(jnp.mean(u * u, axis=-1, keepdims=True) + EPSILON)
                hat = u * inv
                t = grad[rows, cols]
                t = t * cosine[rows, :] - pltpu.roll(t, HD // 2, 1) * sine[rows, :]
                hg_o[j : j + 1, cols] += jnp.sum(t * hat, axis=0, keepdims=True)
                w = t * gains[j : j + 1, cols]
                w = inv * (w - hat * jnp.mean(w * hat, axis=-1, keepdims=True))
                dp_o[rows, j * width + h * HD : j * width + (h + 1) * HD] = w.astype(bf16)
        out = dot_nt(dp_o[rows, :], wqs[...])
        gs_o[...] += jnp.sum(out * x[rows, :].astype(f32), axis=0, keepdims=True)
        stage[rows, :] = out.astype(bf16)
        return 0

    lax.fori_loop(0, length // block, finish, 0)
    for copy in send_out(stage, outs, sems, 0, starts):
        copy.wait()


def proj_back(order, wq, qr, kr, dq, dk, dv, gains, cosine, sine, x, own_rows):
    n = wq.shape[0]
    length, width = qr.shape
    d = x.shape[1]
    count = length // own_rows + 1
    return pl.pallas_call(
        functools.partial(proj_back_body, count, min(256, length)),
        in_specs=[SMEM] + [ANY] + [VMEM] * 9,
        out_specs=[VMEM] * 3 + [ANY] * count,
        out_shape=[
            shape((length, 3 * width), bf16),
            shape((2, width), f32),
            shape((1, d), f32),
        ]
        + piece_shapes(own_rows, d, count),
        scratch_shapes=[
            pltpu.VMEM((d, 3 * width), bf16),
            pltpu.VMEM((length, d), bf16),
            pltpu.SemaphoreType.DMA((count + 3 * n,)),
        ],
        compiler_params=pltpu.CompilerParams(vmem_limit_bytes=36 << 20),
        cost_estimate=cost(12),
        name="proj_back",
    )(order, wq, qr, kr, dq, dk, dv, gains, cosine, sine, x)


def attn_grad_body(places, xa, xb, dp, ctx, da, db, qkv_keep, qkv_send, out_keep, out_send):
    width = ctx.shape[1]
    for x, d, qkv_o, out_o in ((xa, da, qkv_keep, out_keep), (xb, db, qkv_send, out_send)):
        grad = dot_tn(x[...], dp[...])
        for j in range(3):
            qkv_o[0, j] = grad[:, j * width : (j + 1) * width].astype(bf16)
        out_o[0] = dot_tn(ctx[...], d[...]).astype(bf16)


def attn_grad(places, x, dp, ctx, db, n):
    length, d = x.shape
    width = ctx.shape[1]
    depth = d // n
    even = pl.BlockSpec((length, depth), lambda m, at: (0, at[2 * m]))
    odd = pl.BlockSpec((length, depth), lambda m, at: (0, at[2 * m + 1]))
    return pl.pallas_call(
        attn_grad_body,
        grid_spec=pltpu.PrefetchScalarGridSpec(
            num_scalar_prefetch=1,
            grid=(n // 2,),
            in_specs=[
                even,
                odd,
                pl.BlockSpec((length, 3 * width), lambda m, at: (0, 0)),
                pl.BlockSpec((length, width), lambda m, at: (0, 0)),
                even,
                odd,
            ],
            out_specs=[pl.BlockSpec((1, 3, depth, width), lambda m, at: (m, 0, 0, 0))] * 2
            + [pl.BlockSpec((1, width, depth), lambda m, at: (m, 0, 0))] * 2,
        ),
        out_shape=[shape((n // 2, 3, depth, width), bf16)] * 2
        + [shape((n // 2, width, depth), bf16)] * 2,
        compiler_params=pltpu.CompilerParams(vmem_limit_bytes=VMEM_BYTES),
        cost_estimate=cost(6),
        name="attn_grad",
    )(places, x, x, dp, ctx, db, db)


def flat_rows(pieces):
    starts, at = [], 0
    for piece in pieces:
        starts.append(at)
        at += piece.shape[0]
    return starts


def moe_in_body(count, *refs):
    xp, gu, out, xs, sems = refs[:count], *refs[count:]

    @pl.when(pl.program_id(0) == 0)
    def _():
        for copy in fetch(xp, xs, sems, 0, flat_rows(xp)):
            copy.wait()

    out[...] = dot(xs[...], gu[...]).astype(bf16)


def moe_in(xp, gate_up, group=4):
    count = len(xp)
    d, columns = gate_up.shape
    rows = sum(p.shape[0] for p in xp)
    wide = 2 * group * LANES
    return pl.pallas_call(
        functools.partial(moe_in_body, count),
        grid=(columns // wide,),
        in_specs=[ANY] * count + [pl.BlockSpec((d, wide), lambda s: (0, s))],
        out_specs=pl.BlockSpec((rows, wide), lambda s: (0, s)),
        out_shape=shape((rows, columns), bf16),
        scratch_shapes=[pltpu.VMEM((rows, d), bf16), pltpu.SemaphoreType.DMA((count,))],
        compiler_params=pltpu.CompilerParams(vmem_limit_bytes=VMEM_BYTES),
        cost_estimate=cost(rows * 0.02 + 4),
        name="moe_in",
    )(*xp, gate_up)


def moe_mid_body(group, steps, sets, count, *refs):
    it = iter(refs)
    gates = next(it)
    cp = [next(it) for _ in range(count)]
    gus = [next(it) for _ in range(sets)]
    gu_w, dn_w = next(it), next(it)
    d_outs = [next(it) for _ in range(count)]
    m_outs = [next(it) for _ in range(count)]
    dgu_o, hw_o = next(it), next(it)
    cs, d_acc, m_acc, gg, stage, sems = (next(it) for _ in range(6))
    d = cs.shape[1]
    fw = LANES
    step = pl.program_id(0)

    @pl.when(step == 0)
    def _():
        copies = fetch(cp, cs, sems, 0, flat_rows(cp))
        d_acc[...] = jnp.zeros_like(d_acc)
        m_acc[...] = jnp.zeros_like(m_acc)
        gg[...] = jnp.zeros_like(gg)
        for copy in copies:
            copy.wait()

    d_hid = dot_nt(cs[...], dn_w[...])
    at = 0
    for gu in gus:
        rows = gu.shape[0]
        here = pl.ds(at, rows)
        table = gates[here, :].astype(f32)
        lane = lax.broadcasted_iota(jnp.int32, table.shape, 1)
        total = jnp.zeros(table.shape, f32)
        for i in range(group):
            g = gu[:, 2 * i * fw : (2 * i + 1) * fw].astype(f32)
            u = gu[:, (2 * i + 1) * fw : (2 * i + 2) * fw].astype(f32)
            dh = d_hid[at : at + rows, i * fw : (i + 1) * fw]
            z = jax.nn.sigmoid(g)
            swish = g * z
            h = swish * u
            expert = step * group + i
            own = jnp.sum(h * dh, axis=1, keepdims=True)
            total = total + jnp.where(lane == expert, own, 0.0)
            gate = jnp.sum(jnp.where(lane == expert, table, 0.0), axis=1, keepdims=True)
            dw = dh * gate
            d_g = dw * u * z * (1.0 + g * (1.0 - z))
            hw_o[here, i * fw : (i + 1) * fw] = (h * gate).astype(bf16)
            dgu_o[here, 2 * i * fw : (2 * i + 1) * fw] = d_g.astype(bf16)
            dgu_o[here, (2 * i + 1) * fw : (2 * i + 2) * fw] = (dw * swish).astype(bf16)
        gg[here, :] += total
        at += rows
    d_acc[...] += dot_nt(dgu_o[...], gu_w[...])
    m_acc[...] += dot(hw_o[...], dn_w[...])

    @pl.when(step == steps - 1)
    def _():
        stage[:, pl.ds(0, d)] = d_acc[...].astype(bf16)
        stage[:, pl.ds(d, LANES)] = gg[...].astype(bf16)
        copies = send_out(stage, d_outs, sems, 0, flat_rows(d_outs))
        cs[...] = m_acc[...].astype(bf16)
        copies = copies + send_out(cs, m_outs, sems, count, flat_rows(m_outs))
        for copy in copies:
            copy.wait()


def moe_mid(gates, cp, gus, gate_up, down, group=4):
    count = len(cp)
    hidden, d = down.shape
    rows = sum(p.shape[0] for p in cp)
    half = group * LANES
    steps = hidden // half
    return pl.pallas_call(
        functools.partial(moe_mid_body, group, steps, len(gus), count),
        grid=(steps,),
        in_specs=[pl.BlockSpec((rows, LANES), lambda s: (0, 0))]
        + [ANY] * count
        + [pl.BlockSpec((g.shape[0], 2 * half), lambda s: (0, s)) for g in gus]
        + [
            pl.BlockSpec((d, 2 * half), lambda s: (0, s)),
            pl.BlockSpec((half, d), lambda s: (s, 0)),
        ],
        out_specs=[ANY] * (2 * count)
        + [
            pl.BlockSpec((rows, 2 * half), lambda s: (0, s)),
            pl.BlockSpec((rows, half), lambda s: (0, s)),
        ],
        out_shape=[shape((p.shape[0], d + LANES), bf16) for p in cp]
        + [shape(p.shape, bf16) for p in cp]
        + [shape((rows, 2 * hidden), bf16), shape((rows, hidden), bf16)],
        scratch_shapes=[
            pltpu.VMEM((rows, d), bf16),
            pltpu.VMEM((rows, d), f32),
            pltpu.VMEM((rows, d), f32),
            pltpu.VMEM((rows, LANES), f32),
            pltpu.VMEM((rows, d + LANES), bf16),
            pltpu.SemaphoreType.DMA((2 * count,)),
        ],
        compiler_params=pltpu.CompilerParams(vmem_limit_bytes=VMEM_BYTES),
        cost_estimate=cost(rows * 0.04 + 6),
        name="moe_mid",
    )(gates, *cp, *gus, gate_up, down)


def turn_body(count, *refs):
    pieces, out, xs, sems = refs[:count], refs[count], refs[count + 1], refs[count + 2]
    for copy in fetch(pieces, xs, sems, 0, flat_rows(pieces)):
        copy.wait()
    d = xs.shape[1]
    size = 256
    eye = (
        lax.broadcasted_iota(jnp.int32, (size, size), 0)
        == lax.broadcasted_iota(jnp.int32, (size, size), 1)
    ).astype(bf16)
    for at in range(0, d, size):
        out[pl.ds(at, size), :] = dot_nt(eye, xs[:, pl.ds(at, size)]).astype(bf16)


def turn_rows(pieces):
    count = len(pieces)
    length = sum(p.shape[0] for p in pieces)
    d = pieces[0].shape[1]
    return pl.pallas_call(
        functools.partial(turn_body, count),
        in_specs=[ANY] * count,
        out_specs=VMEM,
        out_shape=shape((d, length), bf16),
        scratch_shapes=[pltpu.VMEM((length, d), bf16), pltpu.SemaphoreType.DMA((count,))],
        compiler_params=pltpu.CompilerParams(vmem_limit_bytes=VMEM_BYTES),
        cost_estimate=cost(4),
        name="turn_rows",
    )(*pieces)


def in_grad_body(n, group, sets, places, xt, *refs):
    dgus = refs[:sets]
    *outs, xs, sems = refs[-4:]
    depth, fw = outs[0].shape[3:]
    step = pl.program_id(0)

    def part(k):
        source = xt.at[pl.ds(pl.multiple_of(places[k] * depth, depth), depth)]
        return pltpu.make_async_copy(source, xs.at[pl.ds(k * depth, depth)], sems.at[k])

    @pl.when(step == 0)
    def _():
        for k in range(n):
            part(k).start()

    dgu = jnp.concatenate([ref[...] for ref in dgus], axis=0)
    for k in range(n):

        @pl.when(step == 0)
        def _(k=k):
            part(k).wait()

        grad = dot(xs[pl.ds(k * depth, depth), :], dgu)
        for i in range(group):
            for g in range(2):
                at = (2 * i + g) * fw
                outs[k % 2][k // 2, i, g] = grad[:, at : at + fw].astype(bf16)


def in_grad(places, xt, dgus, n, experts, first, number, held, whole=None, group=2):
    d, length = xt.shape
    depth = d // n
    fw = dgus[0].shape[1] // (2 * experts)
    start = first // group
    at = (first % held) // group
    before = [] if whole is None else list(whole)
    sets = len(dgus)
    return list(
        pl.pallas_call(
            functools.partial(in_grad_body, n, group, sets),
            grid=(number // group,),
            in_specs=[SMEM, ANY]
            + [pl.BlockSpec((a.shape[0], 2 * group * fw), lambda s: (0, s + start)) for a in dgus]
            + [ANY] * len(before),
            out_specs=[pl.BlockSpec((n // 2, group, 2, depth, fw), lambda s: (0, at + s, 0, 0, 0))]
            * 2,
            out_shape=[shape((n // 2, held, 2, depth, fw), bf16)] * 2,
            input_output_aliases={2 + sets: 0, 3 + sets: 1} if before else {},
            scratch_shapes=[pltpu.VMEM((d, length), bf16), pltpu.SemaphoreType.DMA((n,))],
            compiler_params=pltpu.CompilerParams(vmem_limit_bytes=VMEM_BYTES),
            cost_estimate=cost(1.5 * number + 3),
            name="in_grad",
        )(places, xt, *dgus, *before)
    )


def out_grad_body(group, count, sets, *refs):
    hws, pieces = refs[:sets], refs[sets : sets + count]
    out, cs, sems = refs[-3:]
    fw = out.shape[1]

    @pl.when(pl.program_id(0) == 0)
    def _():
        for copy in fetch(pieces, cs, sems, 0, flat_rows(pieces)):
            copy.wait()

    turned = jnp.concatenate([ref[...] for ref in hws], axis=0).T
    grad = dot(turned, cs[...])
    for i in range(group):
        out[i] = grad[i * fw : (i + 1) * fw].astype(bf16)


def out_grad(hws, cp, experts, part, whole=None, group=2):
    count = len(cp)
    length = sum(h.shape[0] for h in hws)
    d = cp[0].shape[1]
    fw = hws[0].shape[1] // experts
    steps = experts // (2 * group)
    at = part * steps
    before = [] if whole is None else [whole]
    return pl.pallas_call(
        functools.partial(out_grad_body, group, count, len(hws)),
        grid=(steps,),
        in_specs=[pl.BlockSpec((h.shape[0], group * fw), lambda s: (0, at + s)) for h in hws]
        + [ANY] * (count + len(before)),
        out_specs=pl.BlockSpec((group, fw, d), lambda s: (at + s, 0, 0)),
        out_shape=shape((experts, fw, d), bf16),
        input_output_aliases={len(hws) + count: 0} if before else {},
        scratch_shapes=[pltpu.VMEM((length, d), bf16), pltpu.SemaphoreType.DMA((count,))],
        compiler_params=pltpu.CompilerParams(vmem_limit_bytes=VMEM_BYTES),
        cost_estimate=cost(9),
        name="out_grad",
    )(*hws, *cp, *before)


def finish_body(*refs):
    keep, got, more, out = refs[-4:]
    out[...] = keep[0].astype(f32) + got[0].astype(f32) + more[0].astype(f32)


def finish(whole, terms, experts, first):
    number = terms[0].shape[1]
    rest = terms[0].shape[2:]
    zeros = (0,) * len(rest)
    before = [] if whole is None else [whole]
    each = 2
    at = first // each
    return pl.pallas_call(
        finish_body,
        grid=(number // each,),
        in_specs=[ANY] * len(before)
        + [pl.BlockSpec((1, each) + rest, lambda s: (0, s) + zeros)] * 3,
        out_specs=pl.BlockSpec((each,) + rest, lambda s: (at + s,) + zeros),
        out_shape=shape((experts,) + rest, f32),
        input_output_aliases={0: 0} if before else {},
        compiler_params=pltpu.CompilerParams(vmem_limit_bytes=VMEM_BYTES),
        cost_estimate=cost(2),
        name="finish",
    )(*before, *terms)


def place_body(*refs):
    part, out = refs[-2:]
    out[...] = part[...].astype(f32)


def place(part, experts, whole=None):
    rest = part.shape[1:]
    zeros = (0,) * len(rest)
    before = [] if whole is None else [whole]
    return pl.pallas_call(
        place_body,
        grid=(part.shape[0] // 2,),
        in_specs=[ANY] * len(before) + [pl.BlockSpec((2,) + rest, lambda s: (s,) + zeros)],
        out_specs=pl.BlockSpec((2,) + rest, lambda s: (s,) + zeros),
        out_shape=shape((experts,) + rest, f32),
        input_output_aliases={0: 0} if before else {},
        compiler_params=pltpu.CompilerParams(vmem_limit_bytes=VMEM_BYTES),
        cost_estimate=cost(3),
        name="place",
    )(*before, part)


def pack_body(w, out):
    fw = w.shape[3]
    for i in range(w.shape[0]):
        for g in range(2):
            at = (2 * i + g) * fw
            out[:, at : at + fw] = w[i, g]


def pack(gate_up, group=4):
    experts, _, depth, fw = gate_up.shape
    return pl.pallas_call(
        pack_body,
        grid=(experts // group,),
        in_specs=[pl.BlockSpec((group, 2, depth, fw), lambda s: (s, 0, 0, 0))],
        out_specs=pl.BlockSpec((depth, 2 * group * fw), lambda s: (0, s)),
        out_shape=shape((depth, 2 * experts * fw), bf16),
        compiler_params=pltpu.CompilerParams(vmem_limit_bytes=VMEM_BYTES),
        cost_estimate=cost(4),
        name="pack",
    )(gate_up)


def rope_tables(length):
    positions = np.arange(length, dtype=np.float32)
    power = -np.arange(HD // 2, dtype=np.float32) * np.float32(2.0) / np.float32(HD)
    inverse_freq = np.power(np.float32(ROPE_BASE), power)
    phases = positions[:, None] * inverse_freq[None, :]
    cosine, sine = np.cos(phases), np.sin(phases)
    tables = [cosine, cosine], [-sine, sine]
    return [np.concatenate(t, axis=-1).astype(np.float32) for t in tables]


def per_device(
    tokens,
    segments,
    routes,
    gate_values,
    cotangent,
    query_key_value,
    out_weight,
    head_gain,
    layer_gain,
    gate_up,
    down_weight,
):
    groups = lax.axis_size("tensor")
    n = lax.axis_size("dp")
    own_rows, d = tokens.shape
    seq_len = own_rows * groups
    heads = query_key_value.shape[2] // HD
    experts = gate_up.shape[0]
    depth = d // n
    steps = groups // 2
    top = routes.shape[1]

    x = tokens.astype(f32)
    routed = jnp.concatenate([routes.astype(bf16), gate_values], axis=1)
    routed = jnp.pad(routed, ((0, 0), (0, LANES - 2 * top)))
    normed = Gather(jnp.concatenate([tokens, routed], axis=1), groups)
    first = normed.step()

    width = query_key_value.shape[2]
    small = jnp.concatenate([layer_gain.reshape(-1), head_gain.reshape(-1)])
    size = small.shape[0]
    small = jnp.pad(small, (0, -size % (16 * width))).reshape(-1, width)
    outward = split_last(out_weight, max(1, depth // width))
    outward = [jnp.pad(a, ((0, 0), (0, width - a.shape[1]))) for a in outward]
    own = [query_key_value.reshape(-1, width)] + outward + [small]
    attn_weights = lax.all_gather(jnp.concatenate(own, axis=0), "dp", axis=0)

    ring = ring_of(groups)
    orders = [[ring[(ring.index(t) + k) % groups] for k in distances_of(groups)] for t in range(groups)]
    orders = jnp.array(orders, jnp.int32)
    order = lax.dynamic_slice(orders, (lax.axis_index("tensor"), 0), (1, groups)).reshape(groups)
    places = jnp.array([[i ^ k for k in range(n)] for i in range(n)], jnp.int32)
    places = lax.dynamic_slice(places, (lax.axis_index("dp"), 0), (1, n)).reshape(n)
    cosine, sine = rope_tables(seq_len)
    seg_row = segments.reshape(1, seq_len)
    seg_col = segments.reshape(seq_len, 1)
    expert_ids = jnp.arange(experts, dtype=jnp.int32)
    chosen = routes[:, :, None] == expert_ids
    (gate_up,) = tie((gate_up,), first)
    packed = pack(gate_up)

    done = normed.step()
    (packed,) = tie((packed,), done)
    gu = lax.all_gather(packed, "dp", axis=0, tiled=True)
    normed.step(after=[packed])
    normed.step()
    cut = 2 * depth
    small = [w[-small.shape[0] :].reshape(-1)[:size] for w in attn_weights]
    gain = jnp.concatenate([s[:cut].reshape(2, depth) for s in small], axis=1).astype(f32)
    gain_in, gain_mid = gain[0], gain[1]
    head_parts = [s[cut:].reshape(2, heads, HD // n) for s in small]
    gain_head = jnp.concatenate(head_parts, axis=2).reshape(2, heads * HD).astype(f32)
    pieces = normed.pieces()
    inv_in = lax.rsqrt(jnp.mean(x * x, axis=-1, keepdims=True) + EPSILON)
    x_hat = x * inv_in
    q, k, v, q_raw, k_raw, normed_all = attn_proj(
        order, pieces, attn_weights, gain_in[None, :], gain_head, cosine, sine
    )
    d_pieces = Gather(cotangent, groups)
    first = d_pieces.step(after=pieces)
    q, k, v = tie((q, k, v), first)
    context, lse, *attn = attn_core(
        order, attn_weights, q, k, v, seg_row, seg_col, own_rows, d
    )
    second = d_pieces.step(after=[q])
    routed = jnp.concatenate([p[:, d : d + 2 * top] for p in pieces], axis=0)
    named = routed[:, :top].astype(jnp.int32)[:, :, None] == expert_ids
    gate_table = jnp.sum(jnp.where(named, routed[:, top:].astype(f32)[:, :, None], 0.0), axis=1)
    gate_table = jnp.pad(gate_table.astype(bf16), ((0, 0), (0, LANES - experts)))
    attention = Scatter(attn, groups)
    done = attention.step(after=second)
    (down,) = tie((down_weight.reshape(-1, depth),), done)
    dn = lax.all_gather(down, "dp", axis=1, tiled=True)
    middle = x + attention.run().result()
    inv_mid = lax.rsqrt(jnp.mean(middle * middle, axis=-1, keepdims=True) + EPSILON)
    mid_hat = middle * inv_mid
    mid = Gather((mid_hat * gain_mid).astype(bf16), groups)

    hidden_in = []
    mid.step()
    for s in range(1, steps - 1):
        here = [mid.at(s), mid.at(-s)] + ([mid.at(0)] if s == 1 else [])
        mid.step(after=hidden_in[-1:])
        hidden_in.append(moe_in(here, gu))
    mid.step(after=hidden_in[-1:])
    normed_mid = mid.pieces()
    taken = normed_mid[:4]
    hidden_in.append(moe_in(taken, gu))
    d_pieces.step(after=taken)
    d_pieces.step(after=hidden_in[-1:])
    d_pieces = d_pieces.pieces()

    half_rows = hidden_in[-1].shape[0]
    d_far, d_near = d_pieces[:4], d_pieces[4:]
    far_out = list(moe_mid(gate_table[:half_rows], d_far, hidden_in[-1:], gu, dn))
    d_mid, moe, d_in, hidden = far_out[:4], far_out[4:8], far_out[8:9], far_out[9:]
    (mid_far,) = tie(normed_mid[:1], d_mid[:1])
    mid_turned = turn_rows([mid_far] + normed_mid[1:])
    d_normed = Scatter(d_mid, groups)
    done = d_normed.step()
    mixing = Scatter(moe, groups)
    second = d_normed.step(after=[mid_turned], riders=mixing.far)
    mixing.done, mixing.moved = 1, [m[:, :d] for m in d_normed.ridden]
    (table,) = tie((gate_table[half_rows:],), done + [mid_turned])
    near_out = list(moe_mid(table, d_near, hidden_in[:-1][::-1], gu, dn))
    count = len(d_near)
    d_mid, moe = d_mid + near_out[:count], moe + near_out[count : 2 * count]
    d_in, hidden = d_in + near_out[2 * count : -1], hidden + near_out[-1:]
    d_normed.block = dict(zip(distances_of(groups)[1:], d_mid[2:]))
    mixing.block = dict(zip(distances_of(groups)[1:], moe[2:]))
    third = d_normed.step(after=moe[-1:])

    (hidden_far,) = tie(hidden[:1], second + near_out[:1])
    dn_half = out_grad([hidden_far] + hidden[1:], d_pieces, experts, 0)
    dn_all = out_grad(hidden, d_pieces, experts, 1, dn_half)
    (ready,) = tie((dn_all,), third)
    dn_grad = lax.psum_scatter(ready, "dp", scatter_dimension=2, tiled=True)
    fourth = d_normed.step(after=[dn_all])

    def gradient(c, after, whole=None):
        (turned,) = tie((mid_turned,), after)
        return in_grad(places, turned, d_in, n, experts, c * each, each, 2 * each, whole)

    each = experts // CHUNKS
    low = gradient(0, third)
    d_normed_mid = d_normed.result()
    gate_sum = d_normed_mid[:, d:]
    d_normed_mid = d_normed_mid[:, :d]
    d_mid_hat = d_normed_mid * gain_mid
    d_middle = cotangent.astype(f32) + inv_mid * (
        d_mid_hat - mid_hat * jnp.mean(d_mid_hat * mid_hat, axis=-1, keepdims=True)
    )
    branch = Gather(d_middle.astype(bf16), groups)
    moved = branch.step(after=low)
    low = gradient(1, [d_middle], low)
    moved_on = branch.step(after=low)
    low_keep, low_send = low[0], tie(low[1:], moved)[0]
    low_terms = flip_reduce(low_keep, low_send, "dp", n)
    high = gradient(2, moved)
    moved = branch.step(after=high + low_terms[3:])
    high = gradient(3, moved_on, high)
    branch.step(after=high)
    high_keep, high_send = high[0], tie(high[1:], moved)[0]
    high_terms = flip_reduce(high_keep, high_send, "dp", n)
    d_branch = branch.pieces()

    moe_second = mixing.step(after=d_branch + high_terms[3:])
    dq, dk, dv, d_branch_all = attn_back(
        order, d_branch, attn_weights, q, k, v, lse, seg_row, seg_col
    )
    dq, dk, dv = tie((dq, dk, dv), moe_second)
    moe_third = mixing.step(after=low_terms[2:3])
    d_projected, head_part, in_part, *to_rows = proj_back(
        order, attn_weights, q_raw, k_raw, dq, dk, dv, gain_head, cosine, sine, normed_all, own_rows
    )
    d_normed = Scatter(to_rows, groups)
    late = [d_normed.step(after=moe_third)]
    (dn_grad,) = tie((dn_grad,), to_rows[:1])
    dn_grad = place(dn_grad, experts)
    late.append(d_normed.step(after=[dn_grad]))
    (projected,) = tie((d_projected,), late[0])
    qkv_keep, qkv_send, out_keep, out_send = attn_grad(
        places, normed_all, projected, context, d_branch_all, n
    )
    late.append(d_normed.step(after=[qkv_keep]))
    qkv_send, out_send = tie((qkv_send, out_send), late[1])
    qkv_terms = flip_reduce(qkv_keep, qkv_send, "dp", n)
    out_terms = flip_reduce(out_keep, out_send, "dp", n)

    (late_low,) = tie(low_terms[2:3], late[1])
    gu_grad = finish(None, low_terms[:2] + [late_low], experts, 0)
    late.append(
        d_normed.step(after=qkv_terms[3:] + out_terms[3:] + [gu_grad] + high_terms[2:3])
    )
    (late_high,) = tie(high_terms[2:3], late[2])
    gu_grad = finish(gu_grad, high_terms[:2] + [late_high], experts, 2 * each)
    late.append(mixing.step(after=late[3] + qkv_terms[2:3]))
    d_normed_in = d_normed.result()
    d_x_hat = d_normed_in * gain_in
    input_grad = d_middle + inv_in * (
        d_x_hat - x_hat * jnp.mean(d_x_hat * x_hat, axis=-1, keepdims=True)
    )
    mixed = (middle + mixing.result()).astype(bf16)
    gate_grad = jnp.sum(jnp.where(chosen, gate_sum[:, None, :experts], 0.0), axis=-1)
    out_terms = out_terms[:2] + list(tie(out_terms[2:3], late[4]))
    qkv_grad = sum(t[0].astype(f32) for t in qkv_terms[:3])
    out_weight_grad = sum(t[0].astype(f32) for t in out_terms[:3])

    mid_part = jnp.sum(d_normed_mid * mid_hat, axis=0)
    (in_part,) = tie((in_part,), late[3])
    layer_part = jnp.stack([in_part[0] / gain_in, mid_part]).reshape(2, n, groups, -1)
    layer_part = jnp.stack(relative([layer_part[:, :, t] for t in range(groups)], "tensor"))
    for bit in bits_of(groups):
        pairs = layer_part.reshape((layer_part.shape[0] // 2, 2) + layer_part.shape[1:])
        layer_part = pairs[:, 0] + flip_step(pairs[:, 1], "tensor", groups, bit)
    head_parts = split_last(head_part.reshape(2, heads, HD), n)
    rows = [
        jnp.concatenate([layer_part[0, :, k].reshape(-1), h.reshape(-1)])
        for k, h in enumerate(head_parts)
    ]
    rows = tie((jnp.stack(relative(rows, "dp")),), out_terms[2:])[0]
    summed = flip_reduce_rows(rows, "dp", n)
    cut = 2 * (depth // groups)
    layer_grad = summed[:cut].reshape(2, depth // groups)
    head_grad = summed[cut:].reshape(2, heads, HD // n)

    return (
        mixed,
        input_grad,
        gate_grad,
        qkv_grad,
        out_weight_grad,
        head_grad,
        layer_grad,
        gu_grad,
        dn_grad,
    )


def solution(mesh):
    return jax.shard_map(
        per_device,
        mesh=mesh,
        in_specs=(
            P(("dp", "tensor"), None),
            P("dp", None),
            P(("dp", "tensor"), None),
            P(("dp", "tensor"), None),
            P(("dp", "tensor"), None),
            P(None, "dp", "tensor"),
            P("tensor", "dp"),
            P(None, "tensor", "dp"),
            P(None, "dp"),
            P(None, None, "dp", "tensor"),
            P(None, "tensor", "dp"),
        ),
        out_specs=(
            P(("dp", "tensor"), None),
            P(("dp", "tensor"), None),
            P(("dp", "tensor"), None),
            P(None, "dp", "tensor"),
            P("tensor", "dp"),
            P(None, "tensor", "dp"),
            P(None, ("dp", "tensor")),
            P(None, None, "dp", "tensor"),
            P(None, "tensor", "dp"),
        ),
        check_vma=False,
    )
```

time: 761 us -> 587 us (0.77)
  waiting for transfers between devices: 391 us -> 154 us
  Pallas kernels: 166 us -> 242 us
  other arithmetic: 72 us -> 47.4 us
  starting transfers between devices: 96 us -> 76 us
  local copies, waits for them, and re-layouts: 24.5 us -> 41.3 us
  between operations: 2.32 us -> 15.6 us
    ppermute x64 -> x62, waiting for transfers between devices: 248 us -> 126 us  [ring_step(): return lax.ppermute(value, 'tensor', pairs)]
    ppermute x38 -> x13, waiting for transfers between devices: 143 us -> 28.1 us  [flip_step(): return lax.ppermute(value, axis, [(s, s ^ bit) for s in range(count)])]
    pallas_call x6 -> x20, Pallas kernels: 164 us -> 236 us  [the longest x2 60.4 us: moe_mid(): pl.pallas_call(functools.partial(moe_mid_body, group, steps, len(gus), co...]
    ppermute x38 -> x13, starting transfers between devices: 24.8 us -> 8.74 us  [flip_step(): return lax.ppermute(value, axis, [(s, s ^ bit) for s in range(count)])]
    concatenate x9 -> x6, other arithmetic: 14.2 us -> 2.41 us  [the longest x1 2.23 us: per_device(): attn_weights = lax.all_gather(jnp.concatenate(own, axis=0), 'dp', axis=0)]
    add x7 -> x5, other arithmetic: 15.3 us -> 5.15 us  [the longest x1 3.12 us: per_device(): qkv_grad = sum((t[0].astype(f32) for t in qkv_terms[:3]))]
    unnamed x202 -> x208, local copies, waits for them, and re-layouts: 14.3 us -> 24.3 us
    convert_element_type x30 -> x33, other arithmetic: 26.1 us -> 35.1 us  [the longest x12 11.6 us: step(): low = (self.block[distance].astype(f32) + low).astype(dtype)]
  transfers between devices with their start and end apart: 102 -> 79, of which waited for: 46 -> 45; matrix products, arithmetic and copies ran while one was open for 10% -> 10% of each run, Pallas kernels for 6% -> 38%
where the time goes in v2:
time: 587 us; the launch traced here: 576 us
  Pallas kernels  242 us (41%)
  waiting for transfers between devices  154 us (26%)
  starting transfers between devices  76 us (13%)
  other arithmetic  47.4 us (8%)
  local copies, waits for them, and re-layouts  41.3 us (7%)
  between operations  15.6 us (3%)
    ppermute x62, waiting for transfers between devices, ring_step(): return lax.ppermute(value, 'tensor', pairs)  126 us
    ppermute x62, starting transfers between devices, ring_step(): return lax.ppermute(value, 'tensor', pairs)  67.1 us
    pallas_call x2, Pallas kernels, moe_mid(): pl.pallas_call(functools.partial(moe_mid_body, group, steps, len(gus), co...  60.4 us
    pallas_call x4, Pallas kernels, in_grad(): pl.pallas_call(functools.partial(in_grad_body, n, group, sets), grid=(num...  39.1 us
    pallas_call x3, Pallas kernels, moe_in(): pl.pallas_call(functools.partial(moe_in_body, count), grid=(columns // wi...  38.7 us
    ppermute x13, waiting for transfers between devices, flip_step(): return lax.ppermute(value, axis, [(s, s ^ bit) for s in range(count)])  28.1 us
    unnamed x208, local copies, waits for them, and re-layouts  24.3 us
    pallas_call x2, Pallas kernels, out_grad(): pl.pallas_call(functools.partial(out_grad_body, group, count, len(hws)),...  19.4 us
  transfers between devices with their start and end apart: 79, of which 45 were waited for; matrix products, arithmetic and copies ran while one was open for 10% of the time, Pallas kernels for 38%

profile of v2, /device:TPU:0, one launch (start us, length us, event | category | flops | bytes accessed | tf_op | source)
XLA Modules:
  0.0 576.5 jit_solution(14154704780934270671)
XLA Ops:
  15.4 12.6 %collective-permute-done.2.refs_7_ = bf16[128,2176]{1,0:T(8,128)(2,1)S(1)} collective-permute-done((bf16[128,2176]{1,0:T(8,128)(2,1)S(1)}, bf16[128,2176]{1,0:T(8,128)(2,1)S(1)}, u32[]{:S(2)}, u32[]{:S(2)}) %collective-permute-start.2) | collective-permute-done | bytes 557088 | tf_op jit(solution)/shard_map/ppermute | solution.py:58
  30.0 5.1 pack.1
  35.2 6.8 %collective-permute-done.3.refs_5_ = bf16[128,2176]{1,0:T(8,128)(2,1)} collective-permute-done((bf16[128,2176]{1,0:T(8,128)(2,1)S(1)}, bf16[128,2176]{1,0:T(8,128)(2,1)}, u32[]{:S(2)}, u32[]{:S(2)}) %collective-permute-start.3) | collective-permute-done | bytes 557088 | tf_op jit(solution)/shard_map/ppermute | solution.py:58
  45.8 10.7 %collective-permute-done.4.refs_4_ = bf16[128,2176]{1,0:T(8,128)(2,1)S(1)} collective-permute-done((bf16[128,2176]{1,0:T(8,128)(2,1)S(1)}, bf16[128,2176]{1,0:T(8,128)(2,1)S(1)}, u32[]{:S(2)}, u32[]{:S(2)}) %collective-permute-start.4) | collective-permute-done | bytes 557088 | tf_op jit(solution)/shard_map/ppermute | solution.py:58
  69.3 13.2 %attn_proj.1 = (bf16[1024,256]{1,0:T(8,128)(2,1)}, bf16[1024,256]{1,0:T(8,128)(2,1)}, bf16[1024,256]{1,0:T(8,128)(2,1)}, f32[1024,256]{1,0:T(8,128)}, f32[1024,256]{1,0:T(8,128)}, /*index=5*/bf16[1024,2048]{1,0:T(8,128)(2,1)}) custom-call(s32[8]{0:T(128)} %dynamic-slice_bitcast_fusion.1.refs_0_, bf16[64,2176]{1,0:T(8,128)(2,1)} %copy-done.80, ...), custom_call_target="tpu_custom_call" | custom-call | flops 6000000000 | bytes 1048576 | tf_op jit(solution)/shard_map/attn_proj/pallas_call | solution.py:308
  90.2 6.7 %attn_core.1 = (bf16[1024,256]{1,0:T(8,128)(2,1)S(1)}, f32[2,1024,1]{2,1,0:T(8,128)S(1)}, bf16[64,2048]{1,0:T(8,128)(2,1)S(1)}, bf16[64,2048]{1,0:T(8,128)(2,1)S...) custom-call(s32[8]{0:T(128)S(1)} %copy-done.14, ...), custom_call_target="tpu_custom_call" | custom-call | flops 6000000000 | bytes 1048576 | tf_op jit(solution)/shard_map/attn_core/pallas_call | solution.py:367
  102.4 4.3 collective-permute-done.12
  112.0 9.6 %collective-permute-done.17 = bf16[128,2048]{1,0:T(8,128)(2,1)S(1)} collective-permute-done((bf16[128,2048]{1,0:T(8,128)(2,1)S(1)}, bf16[128,2048]{1,0:T(8,128)(2,1)S(1)}, u32[]{:S(2)}, u32[]{:S(2)}) %collective-permute-start.17) | collective-permute-done | bytes 524320 | tf_op jit(solution)/shard_map/ppermute | solution.py:58
  124.1 9.9 %collective-permute-done.18 = bf16[128,2048]{1,0:T(8,128)(2,1)S(1)} collective-permute-done((bf16[128,2048]{1,0:T(8,128)(2,1)S(1)}, bf16[128,2048]{1,0:T(8,128)(2,1)S(1)}, u32[]{:S(2)}, u32[]{:S(2)}) %collective-permute-start.18) | collective-permute-done | bytes 524320 | tf_op jit(solution)/shard_map/ppermute | solution.py:58
  137.9 8.6 %collective-permute-done.19 = bf16[128,2048]{1,0:T(8,128)(2,1)S(1)} collective-permute-done((bf16[128,2048]{1,0:T(8,128)(2,1)S(1)}, bf16[128,2048]{1,0:T(8,128)(2,1)S(1)}, u32[]{:S(2)}, u32[]{:S(2)}) %collective-permute-start.19) | collective-permute-done | bytes 524320 | tf_op jit(solution)/shard_map/ppermute | solution.py:58
  152.7 11.3 %collective-permute-done.22.refs_0_.refs_6_ = bf16[128,2048]{1,0:T(8,128)(2,1)S(1)} collective-permute-done((bf16[128,2048]{1,0:T(8,128)(2,1)S(1)}, bf16[128,2048]{1,0:T(8,128)(2,1)S(1)}, u32[]{:S(2)}, u32[]{:S(2)}) %collective-permute-start.22) | collective-permute-done | bytes 524320 | tf_op jit(solution)/shard_map/ppermute | solution.py:58
  168.3 14.3 %moe_in.3.refs_7_ = bf16[384,4096]{1,0:T(8,128)(2,1)} custom-call(bf16[128,2048]{1,0:T(8,128)(2,1)} %copy-done.92, bf16[128,2048]{1,0:T(8,128)(2,1)} %copy-done.93, bf16[128,2048]{1,0:T(8,128)(2,1)} %copy-done.62, bf16[2048,4096]{1,0:T(8,128)(2,1)} %all-gather.5.cloned.1.call-done.refs_3_.refs_2_.refs_4_.refs_6_.refs_8_), custom_call_target="tpu_custom_call" | custom-call | flops 7008000000 | bytes 1048576 | tf_op jit(solution)/shard_map/moe_in/pallas_call | solution.py:579
  184.7 11.3 %moe_in.4.refs_6_ = bf16[256,4096]{1,0:T(8,128)(2,1)} custom-call(bf16[128,2048]{1,0:T(8,128)(2,1)} %collective-permute-done.23.refs_0_.refs_4_, bf16[128,2048]{1,0:T(8,128)(2,1)} %collective-permute-done.21.refs_1_.refs_5_, bf16[2048,4096]{1,0:T(8,128)(2,1)} %all-gather.5.cloned.1.call-done.refs_3_.refs_2_.refs_4_.refs_6_.refs_8_), custom_call_target="tpu_custom_call" | custom-call | flops 5472000000 | bytes 1048576 | tf_op jit(solution)/shard_map/moe_in/pallas_call | solution.py:579
  208.4 13.1 %moe_in.5.refs_5_ = bf16[384,4096]{1,0:T(8,128)(2,1)} custom-call(bf16[64,2048]{1,0:T(8,128)(2,1)} %collective-permute-done.26.refs_0_, bf16[64,2048]{1,0:T(8,128)(2,1)} %collective-permute-done.27.refs_1_, bf16[128,2048]{1,0:T(8,128)(2,1)} %copy-done.74, bf16[128,2048]{1,0:T(8,128)(2,1)} %copy-done.73, ...), custom_call_target="tpu_custom_call" | custom-call | flops 7008000000 | bytes 1048576 | tf_op jit(solution)/shard_map/moe_in/pallas_call | solution.py:579
  230.6 24.5 %moe_mid.2 = (bf16[64,2176]{1,0:T(8,128)(2,1)}, bf16[64,2176]{1,0:T(8,128)(2,1)}, bf16[128,2176]{1,0:T(8,128)(2,1)}, bf16[128,2176]{1,0:T(8,128)(2,1)}, bf16[64,...) custom-call(bf16[384,128]{1,0:T(8,128)(2,1)} %pad_slice_fusion.refs_, ...), custom_call_target="tpu_custom_call" | custom-call | flops 12816000000 | bytes 1048576 | tf_op jit(solution)/shard_map/moe_mid/pallas_call | solution.py:661
  257.9 5.6 turn_rows.1.xt
  269.4 35.9 %moe_mid.3 = (bf16[128,2176]{1,0:T(8,128)(2,1)}, bf16[128,2176]{1,0:T(8,128)(2,1)}, bf16[128,2176]{1,0:T(8,128)(2,1)}, bf16[128,2176]{1,0:T(8,128)(2,1)}, bf16[1...) custom-call(bf16[640,128]{1,0:T(8,128)(2,1)} %pad_slice_fusion.1.ref, ...), custom_call_target="tpu_custom_call" | custom-call | flops 18959998976 | bytes 1048576 | tf_op jit(solution)/shard_map/moe_mid/pallas_call | solution.py:661
  311.4 9.7 %out_grad.2.refs_11_ = bf16[16,128,2048]{2,1,0:T(8,128)(2,1)} custom-call(bf16[384,2048]{1,0:T(8,128)(2,1)} %get-tuple-element.206.refs_0_, bf16[640,2048]{1,0:T(8,128)(2,1)} %get-tuple-element.205.refs_1_, bf16[64,2048]{1,0:T(8,128)(2,1)} %copy-done.64, bf16[64,2048]{1,0:T(8,128)(2,1)} %copy-done.65, bf16[128,2048]{1,0:T(8,128)(2,1)} %copy-done.39, ...), custom_call_target="tpu_custom_call" | custom-call | flops 5400000000 | bytes 1048576 | tf_op jit(solution)/shard_map/out_grad/pallas_call | solution.py:803
  321.1 9.7 %out_grad.3 = bf16[16,128,2048]{2,1,0:T(8,128)(2,1)} custom-call(bf16[384,2048]{1,0:T(8,128)(2,1)} %get-tuple-element.206.refs_0_, bf16[640,2048]{1,0:T(8,128)(2,1)} %get-tuple-element.205.refs_1_, bf16[64,2048]{1,0:T(8,128)(2,1)} %copy-done.64, bf16[64,2048]{1,0:T(8,128)(2,1)} %copy-done.65, ...), custom_call_target="tpu_custom_call", output_to_operand_aliasing={{}: (11, {})} | custom-call | flops 5400000000 | bytes 1048576 | tf_op jit(solution)/shard_map/out_grad/pallas_call | solution.py:803
  336.5 9.8 %in_grad.4 = (bf16[2,8,2,512,128]{4,3,2,1,0:T(8,128)(2,1)}, bf16[2,8,2,512,128]{4,3,2,1,0:T(8,128)(2,1)}) custom-call(s32[4]{0:T(128)} %dynamic-slice_bitcast_fusion.places, bf16[2048,1024]{1,0:T(8,128)(2,1)} %turn_rows.1.xt, bf16[384,4096]{1,0:T(8,128)(2,1)} %get-tuple-element.210.refs_0_, bf16[640,4096]{1,0:T(8,128)(2,1)} %get-tuple-element.211.refs_1_), custom_call_target="tpu_custom_call" | custom-call | flops 5400000000 | bytes 1048576 | tf_op jit(solution)/shard_map/in_grad/pallas_call | solution.py:761
  354.7 9.9 %in_grad.5 = (bf16[2,8,2,512,128]{4,3,2,1,0:T(8,128)(2,1)}, bf16[2,8,2,512,128]{4,3,2,1,0:T(8,128)(2,1)}) custom-call(s32[4]{0:T(128)} %dynamic-slice_bitcast_fusion.places, bf16[2048,1024]{1,0:T(8,128)(2,1)} %turn_rows.1.xt, bf16[384,4096]{1,0:T(8,128)(2,1)} %get-tuple-element.210.refs_0_, ...), custom_call_target="tpu_custom_call", output_to_operand_aliasing={{0}: (4, {}), {1}: (5, {})} | custom-call | flops 5400000000 | bytes 1048576 | tf_op jit(solution)/shard_map/in_grad/pallas_call | solution.py:761
  366.8 9.7 %in_grad.6 = (bf16[2,8,2,512,128]{4,3,2,1,0:T(8,128)(2,1)}, bf16[2,8,2,512,128]{4,3,2,1,0:T(8,128)(2,1)}) custom-call(s32[4]{0:T(128)} %dynamic-slice_bitcast_fusion.places, bf16[2048,1024]{1,0:T(8,128)(2,1)} %turn_rows.1.xt, bf16[384,4096]{1,0:T(8,128)(2,1)} %get-tuple-element.210.refs_0_, bf16[640,4096]{1,0:T(8,128)(2,1)} %get-tuple-element.211.refs_1_), custom_call_target="tpu_custom_call" | custom-call | flops 5400000000 | bytes 1048576 | tf_op jit(solution)/shard_map/in_grad/pallas_call | solution.py:761
  383.5 9.7 %in_grad.7 = (bf16[2,8,2,512,128]{4,3,2,1,0:T(8,128)(2,1)}, bf16[2,8,2,512,128]{4,3,2,1,0:T(8,128)(2,1)}) custom-call(s32[4]{0:T(128)} %dynamic-slice_bitcast_fusion.places, bf16[2048,1024]{1,0:T(8,128)(2,1)} %turn_rows.1.xt, bf16[384,4096]{1,0:T(8,128)(2,1)} %get-tuple-element.210.refs_0_, ...), custom_call_target="tpu_custom_call", output_to_operand_aliasing={{0}: (4, {}), {1}: (5, {})} | custom-call | flops 5400000000 | bytes 1048576 | tf_op jit(solution)/shard_map/in_grad/pallas_call | solution.py:761
  412.0 15.5 %attn_back.1 = (f32[1024,256]{1,0:T(8,128)}, f32[1024,256]{1,0:T(8,128)}, f32[1024,256]{1,0:T(8,128)}, bf16[1024,2048]{1,0:T(8,128)(2,1)}) custom-call(s32[8]{0:T(128)} %dynamic-slice_bitcast_fusion.1.refs_0_, bf16[64,2048]{1,0:T(8,128)(2,1)} %copy-done.98, bf16[64,2048]{1,0:T(8,128)(2,1)} %copy-done.99, bf16[128,2048]{1,0:T(8,128)(2,1)} %copy-done.76, ...), custom_call_target="tpu_custom_call" | custom-call | flops 8400000000 | bytes 1048576 | tf_op jit(solution)/shard_map/attn_back/pallas_call | solution.py:428
  429.1 18.8 %collective-permute-done.52.refs_2_ = bf16[1,8,2,512,128]{4,3,2,1,0:T(8,128)(2,1)S(1)} collective-permute-done((bf16[1,8,2,512,128]{4,3,2,1,0:T(8,128)(2,1)}, bf16[1,8,2,512,128]{4,3,2,1,0:T(8,128)(2,1)S(1)}, u32[]{:S(2)}, u32[]{:S(2)}) %collective-permute-start.52) | collective-permute-done | bytes 2097184 | tf_op jit(solution)/shard_map/ppermute | solution.py:145
  455.9 12.0 %proj_back.1 = (bf16[1024,768]{1,0:T(8,128)(2,1)S(1)}, f32[2,256]{1,0:T(2,128)S(1)}, f32[1,2048]{1,0:T(1,128)S(1)}, bf16[64,2048]{1,0:T(8,128)(2,1)}, bf16[64,20...) custom-call(s32[8]{0:T(128)S(1)} %copy-done.15, ...), custom_call_target="tpu_custom_call" | custom-call | flops 7200000000 | bytes 1048576 | tf_op jit(solution)/shard_map/proj_back/pallas_call | solution.py:495
  473.0 4.5 collective-permute-done.55
  480.3 6.0 %place.1 = f32[16,128,512]{2,1,0:T(8,128)} custom-call(bf16[16,128,512]{2,1,0:T(8,128)(2,1)} %reduce-scatter.2.cloned.1.call-done.refs_0_), custom_call_target="tpu_custom_call" | custom-call | flops 1800000000 | bytes 1048576 | tf_op jit(solution)/shard_map/place/pallas_call | solution.py:853
  488.9 9.7 %attn_grad.1 = (bf16[2,3,512,256]{3,2,1,0:T(8,128)(2,1)}, bf16[2,3,512,256]{3,2,1,0:T(8,128)(2,1)}, bf16[2,256,512]{2,1,0:T(8,128)(2,1)}, bf16[2,256,512]{2,1,0:T(8,128)(2,1)}) custom-call(s32[4]{0:T(128)} %dynamic-slice_bitcast_fusion.places, bf16[1024,2048]{1,0:T(8,128)(2,1)} %get-tuple-element.248.refs_10_.xa.xb, ...), custom_call_target="tpu_custom_call" | custom-call | flops 3600000000 | bytes 1048576 | tf_op jit(solution)/shard_map/attn_grad/pallas_call | solution.py:531
  505.3 5.3 finish.2.refs_0_
  527.9 5.3 finish.3
  555.4 6.8 %collective-permute-done.67 = bf16[128,2048]{1,0:T(8,128)(2,1)S(1)} collective-permute-done((bf16[128,2048]{1,0:T(8,128)(2,1)}, bf16[128,2048]{1,0:T(8,128)(2,1)S(1)}, u32[]{:S(2)}, u32[]{:S(2)}) %collective-permute-start.67) | collective-permute-done | bytes 524320 | tf_op jit(solution)/shard_map/ppermute | solution.py:58
  (520 shorter events, 214.8 us)
Async XLA Ops:
  7.2 58.9 %all-gather.9.cloned.1.call-start = ((), (), s32[]{:S(2)}) async-start(), calls=%async_computation.4 | async-start | bytes 5283840 | tf_op jit(solution)/shard_map/all_gather | solution.py:934
  12.0 155.7 %all-gather.5.cloned.1.call-start = ((), (), s32[]{:S(2)}) async-start(), calls=%async_computation.1 | async-start | bytes 20971520 | tf_op jit(solution)/shard_map/all_gather | solution.py:952
  12.3 15.7 %collective-permute-start.2 = (bf16[128,2176]{1,0:T(8,128)(2,1)S(1)}, bf16[128,2176]{1,0:T(8,128)(2,1)S(1)}, u32[]{:S(2)}, u32[]{:S(2)}) collective-permute-start(bf16[128,2176]{1,0:T(8,128)(2,1)S(1)} %fusion.12.refs_9_), channel_id=1, source_target_pairs={{0,1},{2,0},{4,2},{6,4},{7,6},{5,7},{3,5},{1,3},{8,9},{10,8},{12,1... | collective-permute-start | bytes 1671176 | tf_op jit(solution)/shard_map/ppermute | solution.py:58
  43.0 182.3 %all-gather.7.cloned.1.call-start = ((), (), s32[]{:S(2)}) async-start(), calls=%async_computation.2 | async-start | bytes 10485760 | tf_op jit(solution)/shard_map/all_gather | solution.py:981
  64.0 18.6 %collective-permute-start.8 = (bf16[128,2048]{1,0:T(8,128)(2,1)S(1)}, bf16[128,2048]{1,0:T(8,128)(2,1)}, u32[]{:S(2)}, u32[]{:S(2)}) collective-permute-start(bf16[128,2048]{1,0:T(8,128)(2,1)S(1)} %copy-done.34), channel_id=1, source_target_pairs={{0,2},{2,4},{4,6},{6,7},{7,5},{5,3},{3,1},{1,0},{8,10},{10,12},{12... | collective-permute-start | bytes 1572872 | tf_op jit(solution)/shard_map/ppermute | solution.py:58
  65.3 17.3 %collective-permute-start.9 = (bf16[128,2048]{1,0:T(8,128)(2,1)S(1)}, bf16[128,2048]{1,0:T(8,128)(2,1)}, u32[]{:S(2)}, u32[]{:S(2)}) collective-permute-start(bf16[128,2048]{1,0:T(8,128)(2,1)S(1)} %copy-done.34), channel_id=1, source_target_pairs={{0,1},{2,0},{4,2},{6,4},{7,6},{5,7},{3,5},{1,3},{8,9},{10,8},{12,1... | collective-permute-start | bytes 1572872 | tf_op jit(solution)/shard_map/ppermute | solution.py:58
  82.6 17.6 %collective-permute-start.10 = (bf16[128,2048]{1,0:T(8,128)(2,1)}, bf16[128,2048]{1,0:T(8,128)(2,1)S(1)}, u32[]{:S(2)}, u32[]{:S(2)}) collective-permute-start(bf16[128,2048]{1,0:T(8,128)(2,1)} %collective-permute-done.8.refs_4_.refs_9_), channel_id=1, source_target_pairs={{0,2},{2,4},{4,6},{6,7},{7,5},{5,3},{3,1},{1,0},{8,10},{10,12},{12... | collective-permute-start | bytes 1572872 | tf_op jit(solution)/shard_map/ppermute | solution.py:58
  84.1 16.2 %collective-permute-start.11 = (bf16[128,2048]{1,0:T(8,128)(2,1)}, bf16[128,2048]{1,0:T(8,128)(2,1)S(1)}, u32[]{:S(2)}, u32[]{:S(2)}) collective-permute-start(bf16[128,2048]{1,0:T(8,128)(2,1)} %collective-permute-done.9.refs_3_.refs_8_), channel_id=1, source_target_pairs={{0,1},{2,0},{4,2},{6,4},{7,6},{5,7},{3,5},{1,3},{8,9},{10,8},{12,1... | collective-permute-start | bytes 1572872 | tf_op jit(solution)/shard_map/ppermute | solution.py:58
  108.7 371.6 %reduce-scatter.2.cloned.1.call-start = ((), (), s32[]{:S(2)}) async-start(), calls=%async_computation.3 | async-start | bytes 10485760 | tf_op jit(solution)/shard_map/reduce_scatter | solution.py:1025
  152.7 14.8 %collective-permute-start.20 = (bf16[128,2048]{1,0:T(8,128)(2,1)S(1)}, bf16[128,2048]{1,0:T(8,128)(2,1)S(1)}, u32[]{:S(2)}, u32[]{:S(2)}) collective-permute-start(bf16[128,2048]{1,0:T(8,128)(2,1)S(1)} %multiply_convert_fusion.refs_2_.refs_8_), channel_id=1, source_target_pairs={{0,2},{2,4},{4,6},{6,7},{7,5},{5,3},{3,1},{1,0},{8,10},{10,12},{12... | collective-permute-start | bytes 1572872 | tf_op jit(solution)/shard_map/ppermute | solution.py:58
  164.0 18.5 %collective-permute-start.23 = (bf16[128,2048]{1,0:T(8,128)(2,1)S(1)}, bf16[128,2048]{1,0:T(8,128)(2,1)}, u32[]{:S(2)}, u32[]{:S(2)}) collective-permute-start(bf16[128,2048]{1,0:T(8,128)(2,1)S(1)} %collective-permute-done.22.refs_0_.refs_6_), channel_id=1, source_target_pairs={{0,1},{2,0},{4,2},{6,4},{7,6},{5,7},{3,5},{1,3},{8,9},{10,8},{12,1... | collective-permute-start | bytes 1572872 | tf_op jit(solution)/shard_map/ppermute | solution.py:58
  167.5 15.1 %collective-permute-start.21 = (bf16[128,2048]{1,0:T(8,128)(2,1)S(1)}, bf16[128,2048]{1,0:T(8,128)(2,1)}, u32[]{:S(2)}, u32[]{:S(2)}) collective-permute-start(bf16[128,2048]{1,0:T(8,128)(2,1)S(1)} %collective-permute-done.20.refs_1_.refs_7_), channel_id=1, source_target_pairs={{0,2},{2,4},{4,6},{6,7},{7,5},{5,3},{3,1},{1,0},{8,10},{10,12},{12... | collective-permute-start | bytes 1572872 | tf_op jit(solution)/shard_map/ppermute | solution.py:58
  206.3 15.1 %collective-permute-start.28 = (bf16[128,2048]{1,0:T(8,128)(2,1)S(1)}, bf16[128,2048]{1,0:T(8,128)(2,1)S(1)}, u32[]{:S(2)}, u32[]{:S(2)}) collective-permute-start(bf16[128,2048]{1,0:T(8,128)(2,1)S(1)} %copy-done.52), channel_id=1, source_target_pairs={{0,2},{2,4},{4,6},{6,7},{7,5},{5,3},{3,1},{1,0},{8,10},{10,12},{12... | collective-permute-start | bytes 1572872 | tf_op jit(solution)/shard_map/ppermute | solution.py:58
  207.4 14.8 %collective-permute-start.29 = (bf16[128,2048]{1,0:T(8,128)(2,1)S(1)}, bf16[128,2048]{1,0:T(8,128)(2,1)S(1)}, u32[]{:S(2)}, u32[]{:S(2)}) collective-permute-start(bf16[128,2048]{1,0:T(8,128)(2,1)S(1)} %copy-done.54), channel_id=1, source_target_pairs={{0,1},{2,0},{4,2},{6,4},{7,6},{5,7},{3,5},{1,3},{8,9},{10,8},{12,1... | collective-permute-start | bytes 1572872 | tf_op jit(solution)/shard_map/ppermute | solution.py:58
  266.9 38.4 %collective-permute-start.34 = (bf16[192,2176]{1,0:T(8,128)(2,1)S(1)}, bf16[192,2176]{1,0:T(8,128)(2,1)S(1)}, u32[]{:S(2)}, u32[]{:S(2)}) collective-permute-start(bf16[192,2176]{1,0:T(8,128)(2,1)S(1)} %fusion.10), channel_id=1, source_target_pairs={{0,2},{2,4},{4,6},{6,7},{7,5},{5,3},{3,1},{1,0},{8,10},{10,12},{12... | collective-permute-start | bytes 2506760 | tf_op jit(solution)/shard_map/ppermute | solution.py:58
  268.1 39.3 %collective-permute-start.35 = (bf16[192,2176]{1,0:T(8,128)(2,1)S(1)}, bf16[192,2176]{1,0:T(8,128)(2,1)}, u32[]{:S(2)}, u32[]{:S(2)}) collective-permute-start(bf16[192,2176]{1,0:T(8,128)(2,1)S(1)} %fusion.11), channel_id=1, source_target_pairs={{0,1},{2,0},{4,2},{6,4},{7,6},{5,7},{3,5},{1,3},{8,9},{10,8},{12,1... | collective-permute-start | bytes 2506760 | tf_op jit(solution)/shard_map/ppermute | solution.py:58
  309.4 21.4 %collective-permute-start.36 = (bf16[128,2176]{1,0:T(8,128)(2,1)}, bf16[128,2176]{1,0:T(8,128)(2,1)S(1)}, u32[]{:S(2)}, u32[]{:S(2)}) collective-permute-start(bf16[128,2176]{1,0:T(8,128)(2,1)} %add_convert_fusion.6), channel_id=1, source_target_pairs={{0,2},{2,4},{4,6},{6,7},{7,5},{5,3},{3,1},{1,0},{8,10},{10,12},{12... | collective-permute-start | bytes 1671176 | tf_op jit(solution)/shard_map/ppermute | solution.py:58
  310.5 20.3 %collective-permute-start.37 = (bf16[128,2176]{1,0:T(8,128)(2,1)}, bf16[128,2176]{1,0:T(8,128)(2,1)S(1)}, u32[]{:S(2)}, u32[]{:S(2)}) collective-permute-start(bf16[128,2176]{1,0:T(8,128)(2,1)} %add_convert_fusion.5), channel_id=1, source_target_pairs={{0,1},{2,0},{4,2},{6,4},{7,6},{5,7},{3,5},{1,3},{8,9},{10,8},{12,1... | collective-permute-start | bytes 1671176 | tf_op jit(solution)/shard_map/ppermute | solution.py:58
  333.2 15.3 %collective-permute-start.38 = (bf16[128,2176]{1,0:T(8,128)(2,1)}, bf16[128,2176]{1,0:T(8,128)(2,1)S(1)}, u32[]{:S(2)}, u32[]{:S(2)}) collective-permute-start(bf16[128,2176]{1,0:T(8,128)(2,1)} %add_convert_fusion.4), channel_id=1, source_target_pairs={{0,2},{2,4},{4,6},{6,7},{7,5},{5,3},{3,1},{1,0},{8,10},{10,12},{12... | collective-permute-start | bytes 1671176 | tf_op jit(solution)/shard_map/ppermute | solution.py:58
  334.4 15.1 %collective-permute-start.39 = (bf16[128,2176]{1,0:T(8,128)(2,1)S(1)}, bf16[128,2176]{1,0:T(8,128)(2,1)S(1)}, u32[]{:S(2)}, u32[]{:S(2)}) collective-permute-start(bf16[128,2176]{1,0:T(8,128)(2,1)S(1)} %add_convert_fusion.3), channel_id=1, source_target_pairs={{0,1},{2,0},{4,2},{6,4},{7,6},{5,7},{3,5},{1,3},{8,9},{10,8},{12,1... | collective-permute-start | bytes 1671176 | tf_op jit(solution)/shard_map/ppermute | solution.py:58
  364.7 15.9 %collective-permute-start.42 = (bf16[128,2048]{1,0:T(8,128)(2,1)S(1)}, bf16[128,2048]{1,0:T(8,128)(2,1)S(1)}, u32[]{:S(2)}, u32[]{:S(2)}) collective-permute-start(bf16[128,2048]{1,0:T(8,128)(2,1)S(1)} %collective-permute-done.40.refs_8_), channel_id=1, source_target_pairs={{0,2},{2,4},{4,6},{6,7},{7,5},{5,3},{3,1},{1,0},{8,10},{10,12},{12... | collective-permute-start | bytes 1572872 | tf_op jit(solution)/shard_map/ppermute | solution.py:58
  399.7 48.2 %collective-permute-start.52 = (bf16[1,8,2,512,128]{4,3,2,1,0:T(8,128)(2,1)}, bf16[1,8,2,512,128]{4,3,2,1,0:T(8,128)(2,1)S(1)}, u32[]{:S(2)}, u32[]{:S(2)}) collective-permute-start(bf16[1,8,2,512,128]{4,3,2,1,0:T(8,128)(2,1)} %add_convert_fusion.1), channel_id=1, source_target_pairs={{0,16},{8,24},{16,0},{24,8},{1,17},{9,25},{17,1},{25,9},{2,18},{10... | collective-permute-start | bytes 6291464 | tf_op jit(solution)/shard_map/ppermute | solution.py:145
  409.8 17.8 %collective-permute-start.50 = (bf16[128,2048]{1,0:T(8,128)(2,1)}, bf16[128,2048]{1,0:T(8,128)(2,1)}, u32[]{:S(2)}, u32[]{:S(2)}) collective-permute-start(bf16[128,2048]{1,0:T(8,128)(2,1)} %add_convert_fusion.21), channel_id=1, source_target_pairs={{0,2},{2,4},{4,6},{6,7},{7,5},{5,3},{3,1},{1,0},{8,10},{10,12},{12... | collective-permute-start | bytes 1572872 | tf_op jit(solution)/shard_map/ppermute | solution.py:58
  411.2 17.7 %collective-permute-start.51 = (bf16[128,2048]{1,0:T(8,128)(2,1)}, bf16[128,2048]{1,0:T(8,128)(2,1)S(1)}, u32[]{:S(2)}, u32[]{:S(2)}) collective-permute-start(bf16[128,2048]{1,0:T(8,128)(2,1)} %add_convert_fusion.20), channel_id=1, source_target_pairs={{0,1},{2,0},{4,2},{6,4},{7,6},{5,7},{3,5},{1,3},{8,9},{10,8},{12,1... | collective-permute-start | bytes 1572872 | tf_op jit(solution)/shard_map/ppermute | solution.py:58
  447.9 21.9 %collective-permute-start.53 = (bf16[128,2048]{1,0:T(8,128)(2,1)S(1)}, bf16[128,2048]{1,0:T(8,128)(2,1)}, u32[]{:S(2)}, u32[]{:S(2)}) collective-permute-start(bf16[128,2048]{1,0:T(8,128)(2,1)S(1)} %add_convert_fusion.19), channel_id=1, source_target_pairs={{0,2},{2,4},{4,6},{6,7},{7,5},{5,3},{3,1},{1,0},{8,10},{10,12},{12... | collective-permute-start | bytes 1572872 | tf_op jit(solution)/shard_map/ppermute | solution.py:58
  449.3 20.6 %collective-permute-start.54 = (bf16[128,2048]{1,0:T(8,128)(2,1)S(1)}, bf16[128,2048]{1,0:T(8,128)(2,1)}, u32[]{:S(2)}, u32[]{:S(2)}) collective-permute-start(bf16[128,2048]{1,0:T(8,128)(2,1)S(1)} %add_convert_fusion.18), channel_id=1, source_target_pairs={{0,1},{2,0},{4,2},{6,4},{7,6},{5,7},{3,5},{1,3},{8,9},{10,8},{12,1... | collective-permute-start | bytes 1572872 | tf_op jit(solution)/shard_map/ppermute | solution.py:58
  471.9 50.0 %collective-permute-start.63 = (bf16[1,8,2,512,128]{4,3,2,1,0:T(8,128)(2,1)}, bf16[1,8,2,512,128]{4,3,2,1,0:T(8,128)(2,1)}, u32[]{:S(2)}, u32[]{:S(2)}) collective-permute-start(bf16[1,8,2,512,128]{4,3,2,1,0:T(8,128)(2,1)} %add_convert_fusion), channel_id=1, source_target_pairs={{0,16},{8,24},{16,0},{24,8},{1,17},{9,25},{17,1},{25,9},{2,18},{10... | collective-permute-start | bytes 6291464 | tf_op jit(solution)/shard_map/ppermute | solution.py:145
  501.1 14.7 %collective-permute-start.59 = (bf16[128,2048]{1,0:T(8,128)(2,1)}, bf16[128,2048]{1,0:T(8,128)(2,1)}, u32[]{:S(2)}, u32[]{:S(2)}) collective-permute-start(bf16[128,2048]{1,0:T(8,128)(2,1)} %add_convert_fusion.13), channel_id=1, source_target_pairs={{0,2},{2,4},{4,6},{6,7},{7,5},{5,3},{3,1},{1,0},{8,10},{10,12},{12... | collective-permute-start | bytes 1572872 | tf_op jit(solution)/shard_map/ppermute | solution.py:58
  501.8 18.6 %collective-permute-start.61 = (bf16[2,3,512,256]{3,2,1,0:T(8,128)(2,1)}, bf16[2,3,512,256]{3,2,1,0:T(8,128)(2,1)S(1)}, u32[]{:S(2)}, u32[]{:S(2)}) collective-permute-start(bf16[2,3,512,256]{3,2,1,0:T(8,128)(2,1)} %get-tuple-element.272), channel_id=1, source_target_pairs={{0,8},{8,0},{16,24},{24,16},{1,9},{9,1},{17,25},{25,17},{2,10},{10... | collective-permute-start | bytes 4718600 | tf_op jit(solution)/shard_map/ppermute | solution.py:145
  504.0 14.4 %collective-permute-start.60 = (bf16[128,2048]{1,0:T(8,128)(2,1)}, bf16[128,2048]{1,0:T(8,128)(2,1)}, u32[]{:S(2)}, u32[]{:S(2)}) collective-permute-start(bf16[128,2048]{1,0:T(8,128)(2,1)} %add_convert_fusion.12), channel_id=1, source_target_pairs={{0,1},{2,0},{4,2},{6,4},{7,6},{5,7},{3,5},{1,3},{8,9},{10,8},{12,1... | collective-permute-start | bytes 1572872 | tf_op jit(solution)/shard_map/ppermute | solution.py:58
  525.9 29.5 %collective-permute-start.69 = (bf16[1,256,512]{2,1,0:T(8,128)(2,1)}, bf16[1,256,512]{2,1,0:T(8,128)(2,1)S(1)}, u32[]{:S(2)}, u32[]{:S(2)}) collective-permute-start(bf16[1,256,512]{2,1,0:T(8,128)(2,1)} %add_convert_fusion.28), channel_id=1, source_target_pairs={{0,16},{8,24},{16,0},{24,8},{1,17},{9,25},{17,1},{25,9},{2,18},{10... | collective-permute-start | bytes 786440 | tf_op jit(solution)/shard_map/ppermute | solution.py:145
  527.1 23.1 %collective-permute-start.66 = (bf16[1,3,512,256]{3,2,1,0:T(8,128)(2,1)}, bf16[1,3,512,256]{3,2,1,0:T(8,128)(2,1)}, u32[]{:S(2)}, u32[]{:S(2)}) collective-permute-start(bf16[1,3,512,256]{3,2,1,0:T(8,128)(2,1)} %add_convert_fusion.2), channel_id=1, source_target_pairs={{0,16},{8,24},{16,0},{24,8},{1,17},{9,25},{17,1},{25,9},{2,18},{10... | collective-permute-start | bytes 2359304 | tf_op jit(solution)/shard_map/ppermute | solution.py:145
  (152 other events, 1669.4 us)
Sparse Core Ops, SparseCore 0:
  12.1 37.3 all-gather.8
  51.6 105.9 all-gather.4
  159.2 58.2 all-gather.6
  331.8 71.2 reduce-scatter.1

commit v3 on v2

--- a/solution.py
+++ b/solution.py
@@ -375,7 +375,7 @@
             pltpu.VMEM((length, d), bf16),
             pltpu.SemaphoreType.DMA((count + output_copies(n, d // n, width),)),
         ],
-        compiler_params=pltpu.CompilerParams(vmem_limit_bytes=36 << 20),
+        compiler_params=pltpu.CompilerParams(vmem_limit_bytes=VMEM_BYTES),
         cost_estimate=cost(10),
         name="attn_core",
     )(order, wo, q, k, v, seg_row, seg_col)
@@ -507,7 +507,7 @@
             pltpu.VMEM((length, d), bf16),
             pltpu.SemaphoreType.DMA((count + 3 * n,)),
         ],
-        compiler_params=pltpu.CompilerParams(vmem_limit_bytes=36 << 20),
+        compiler_params=pltpu.CompilerParams(vmem_limit_bytes=VMEM_BYTES),
         cost_estimate=cost(12),
         name="proj_back",
     )(order, wq, qr, kr, dq, dk, dv, gains, cosine, sine, x)
@@ -792,27 +792,23 @@
         out[i] = grad[i * fw : (i + 1) * fw].astype(bf16)
 
 
-def out_grad(hws, cp, experts, part, whole=None, group=2):
+def out_grad(hws, cp, experts, group=2):
     count = len(cp)
     length = sum(h.shape[0] for h in hws)
     d = cp[0].shape[1]
     fw = hws[0].shape[1] // experts
-    steps = experts // (2 * group)
-    at = part * steps
-    before = [] if whole is None else [whole]
     return pl.pallas_call(
         functools.partial(out_grad_body, group, count, len(hws)),
-        grid=(steps,),
-        in_specs=[pl.BlockSpec((h.shape[0], group * fw), lambda s: (0, at + s)) for h in hws]
-        + [ANY] * (count + len(before)),
-        out_specs=pl.BlockSpec((group, fw, d), lambda s: (at + s, 0, 0)),
+        grid=(experts // group,),
+        in_specs=[pl.BlockSpec((h.shape[0], group * fw), lambda s: (0, s)) for h in hws]
+        + [ANY] * count,
+        out_specs=pl.BlockSpec((group, fw, d), lambda s: (s, 0, 0)),
         out_shape=shape((experts, fw, d), bf16),
-        input_output_aliases={len(hws) + count: 0} if before else {},
         scratch_shapes=[pltpu.VMEM((length, d), bf16), pltpu.SemaphoreType.DMA((count,))],
         compiler_params=pltpu.CompilerParams(vmem_limit_bytes=VMEM_BYTES),
-        cost_estimate=cost(9),
+        cost_estimate=cost(12),
         name="out_grad",
-    )(*hws, *cp, *before)
+    )(*hws, *cp)
 
 
 def finish_body(*refs):
@@ -1019,8 +1015,7 @@
     third = d_normed.step(after=moe[-1:])
 
     (hidden_far,) = tie(hidden[:1], second + near_out[:1])
-    dn_half = out_grad([hidden_far] + hidden[1:], d_pieces, experts, 0)
-    dn_all = out_grad(hidden, d_pieces, experts, 1, dn_half)
+    dn_all = out_grad([hidden_far] + hidden[1:], d_pieces, experts)
     (ready,) = tie((dn_all,), third)
     dn_grad = lax.psum_scatter(ready, "dp", scatter_dimension=2, tiled=True)
     fourth = d_normed.step(after=[dn_all])
@@ -1057,32 +1052,33 @@
         order, d_branch, attn_weights, q, k, v, lse, seg_row, seg_col
     )
     dq, dk, dv = tie((dq, dk, dv), moe_second)
-    moe_third = mixing.step(after=low_terms[2:3])
+    moe_third = mixing.step()
     d_projected, head_part, in_part, *to_rows = proj_back(
         order, attn_weights, q_raw, k_raw, dq, dk, dv, gain_head, cosine, sine, normed_all, own_rows
     )
     d_normed = Scatter(to_rows, groups)
-    late = [d_normed.step(after=moe_third)]
-    (dn_grad,) = tie((dn_grad,), to_rows[:1])
-    dn_grad = place(dn_grad, experts)
-    late.append(d_normed.step(after=[dn_grad]))
+    late = [d_normed.step(after=moe_third + low_terms[2:3])]
     (projected,) = tie((d_projected,), late[0])
     qkv_keep, qkv_send, out_keep, out_send = attn_grad(
         places, normed_all, projected, context, d_branch_all, n
     )
-    late.append(d_normed.step(after=[qkv_keep]))
+    late.append(d_normed.step())
     qkv_send, out_send = tie((qkv_send, out_send), late[1])
     qkv_terms = flip_reduce(qkv_keep, qkv_send, "dp", n)
     out_terms = flip_reduce(out_keep, out_send, "dp", n)
+    (dn_grad,) = tie((dn_grad,), late[0])
+    dn_grad = place(dn_grad, experts)
+    late.append(
+        d_normed.step(after=[qkv_keep, dn_grad])
+    )
 
     (late_low,) = tie(low_terms[2:3], late[1])
     gu_grad = finish(None, low_terms[:2] + [late_low], experts, 0)
-    late.append(
-        d_normed.step(after=qkv_terms[3:] + out_terms[3:] + [gu_grad] + high_terms[2:3])
-    )
-    (late_high,) = tie(high_terms[2:3], late[2])
+    late.append(d_normed.step(after=[gu_grad] + qkv_terms[3:] + out_terms[3:] + high_terms[2:3]))
+    (late_high,) = tie(high_terms[2:3], late[3])
     gu_grad = finish(gu_grad, high_terms[:2] + [late_high], experts, 2 * each)
-    late.append(mixing.step(after=late[3] + qkv_terms[2:3]))
+    late.append(mixing.step(after=late[3]))
+    qkv_terms = qkv_terms[:2] + list(tie(qkv_terms[2:3], late[4]))
     d_normed_in = d_normed.result()
     d_x_hat = d_normed_in * gain_in
     input_grad = d_middle + inv_in * (
@@ -1095,7 +1091,7 @@
     out_weight_grad = sum(t[0].astype(f32) for t in out_terms[:3])
 
     mid_part = jnp.sum(d_normed_mid * mid_hat, axis=0)
-    (in_part,) = tie((in_part,), late[3])
+    (in_part,) = tie((in_part,), late[2])
     layer_part = jnp.stack([in_part[0] / gain_in, mid_part]).reshape(2, n, groups, -1)
     layer_part = jnp.stack(relative([layer_part[:, :, t] for t in range(groups)], "tensor"))
     for bit in bits_of(groups):
@@ -1106,7 +1102,7 @@
         jnp.concatenate([layer_part[0, :, k].reshape(-1), h.reshape(-1)])
         for k, h in enumerate(head_parts)
     ]
-    rows = tie((jnp.stack(relative(rows, "dp")),), out_terms[2:])[0]
+    rows = jnp.stack(relative(rows, "dp"))
     summed = flip_reduce_rows(rows, "dp", n)
     cut = 2 * (depth // groups)
     layer_grad = summed[:cut].reshape(2, depth // groups)

time: 587 us -> 569 us (0.969)
  waiting for transfers between devices: 154 us -> 134 us
  local copies, waits for them, and re-layouts: 41.3 us -> 25.1 us
  starting transfers between devices: 76 us -> 83.6 us
  Pallas kernels: 242 us -> 248 us
    ppermute x13, waiting for transfers between devices: 28.1 us -> 1.12 us  [flip_step(): return lax.ppermute(value, axis, [(s, s ^ bit) for s in range(count)])]
    unnamed x208 -> x140, local copies, waits for them, and re-layouts: 24.3 us -> 3.93 us
    ppermute x62, waiting for transfers between devices: 126 us -> 132 us  [ring_step(): return lax.ppermute(value, 'tensor', pairs)]
    pallas_call x1, Pallas kernels: 12 us -> 18 us  [proj_back(): pl.pallas_call(functools.partial(proj_back_body, count, min(256, length))...]
    pallas_call x2 -> x1, Pallas kernels: 19.4 us -> 15.3 us  [out_grad(): pl.pallas_call(functools.partial(out_grad_body, group, count, len(hws)),...]
  transfers between devices with their start and end apart: 79 -> 79, of which waited for: 45 -> 40; matrix products, arithmetic and copies ran while one was open for 10% -> 11% of each run, Pallas kernels for 38% -> 40%
where the time goes in v3:
time: 569 us; the launch traced here: 558 us
  Pallas kernels  248 us (44%)
  waiting for transfers between devices  134 us (24%)
  starting transfers between devices  83.6 us (15%)
  other arithmetic  52.6 us (9%)
  local copies, waits for them, and re-layouts  25.1 us (4%)
  between operations  15.4 us (3%)
    ppermute x62, waiting for transfers between devices, ring_step(): return lax.ppermute(value, 'tensor', pairs)  132 us
    ppermute x62, starting transfers between devices, ring_step(): return lax.ppermute(value, 'tensor', pairs)  71.7 us
    pallas_call x2, Pallas kernels, moe_mid(): pl.pallas_call(functools.partial(moe_mid_body, group, steps, len(gus), co...  60.4 us
    pallas_call x4, Pallas kernels, in_grad(): pl.pallas_call(functools.partial(in_grad_body, n, group, sets), grid=(num...  39 us
    pallas_call x3, Pallas kernels, moe_in(): pl.pallas_call(functools.partial(moe_in_body, count), grid=(columns // wi...  38.9 us
    pallas_call x1, Pallas kernels, proj_back(): pl.pallas_call(functools.partial(proj_back_body, count, min(256, length))...  18 us
    pallas_call x1, Pallas kernels, attn_back(): pl.pallas_call(functools.partial(attn_back_body, count, min(256, length))...  15.5 us
    pallas_call x1, Pallas kernels, out_grad(): pl.pallas_call(functools.partial(out_grad_body, group, count, len(hws)),...  15.3 us
  transfers between devices with their start and end apart: 79, of which 40 were waited for; matrix products, arithmetic and copies ran while one was open for 11% of the time, Pallas kernels for 40%

profile of v3, /device:TPU:0, one launch (start us, length us, event | category | flops | bytes accessed | tf_op | source)
XLA Modules:
  0.0 558.4 jit_solution(602438138369619452)
XLA Ops:
  15.4 12.6 %collective-permute-done.2.refs_7_ = bf16[128,2176]{1,0:T(8,128)(2,1)S(1)} collective-permute-done((bf16[128,2176]{1,0:T(8,128)(2,1)S(1)}, bf16[128,2176]{1,0:T(8,128)(2,1)S(1)}, u32[]{:S(2)}, u32[]{:S(2)}) %collective-permute-start.2) | collective-permute-done | bytes 557088 | tf_op jit(solution)/shard_map/ppermute | solution.py:58
  30.0 5.1 pack.1
  35.2 6.7 %collective-permute-done.3.refs_5_ = bf16[128,2176]{1,0:T(8,128)(2,1)S(1)} collective-permute-done((bf16[128,2176]{1,0:T(8,128)(2,1)S(1)}, bf16[128,2176]{1,0:T(8,128)(2,1)S(1)}, u32[]{:S(2)}, u32[]{:S(2)}) %collective-permute-start.3) | collective-permute-done | bytes 557088 | tf_op jit(solution)/shard_map/ppermute | solution.py:58
  45.2 10.9 %collective-permute-done.4.refs_4_ = bf16[128,2176]{1,0:T(8,128)(2,1)S(1)} collective-permute-done((bf16[128,2176]{1,0:T(8,128)(2,1)}, bf16[128,2176]{1,0:T(8,128)(2,1)S(1)}, u32[]{:S(2)}, u32[]{:S(2)}) %collective-permute-start.4) | collective-permute-done | bytes 557088 | tf_op jit(solution)/shard_map/ppermute | solution.py:58
  69.2 13.3 %attn_proj.1 = (bf16[1024,256]{1,0:T(8,128)(2,1)}, bf16[1024,256]{1,0:T(8,128)(2,1)}, bf16[1024,256]{1,0:T(8,128)(2,1)}, f32[1024,256]{1,0:T(8,128)}, f32[1024,256]{1,0:T(8,128)}, /*index=5*/bf16[1024,2048]{1,0:T(8,128)(2,1)}) custom-call(s32[8]{0:T(128)} %dynamic-slice_bitcast_fusion.1.refs_0_, bf16[64,2176]{1,0:T(8,128)(2,1)} %copy-done.42, ...), custom_call_target="tpu_custom_call" | custom-call | flops 6000000000 | bytes 1048576 | tf_op jit(solution)/shard_map/attn_proj/pallas_call | solution.py:308
  84.6 10.4 %attn_core.1 = (bf16[1024,256]{1,0:T(8,128)(2,1)}, f32[2,1024,1]{2,1,0:T(8,128)}, bf16[64,2048]{1,0:T(8,128)(2,1)}, bf16[64,2048]{1,0:T(8,128)(2,1)}, bf16[128,2...) custom-call(s32[8]{0:T(128)} %dynamic-slice_bitcast_fusion.1.refs_0_, ...), custom_call_target="tpu_custom_call" | custom-call | flops 6000000000 | bytes 1048576 | tf_op jit(solution)/shard_map/attn_core/pallas_call | solution.py:367
  97.2 4.6 collective-permute-done.12
  108.3 8.7 %collective-permute-done.17 = bf16[128,2048]{1,0:T(8,128)(2,1)S(1)} collective-permute-done((bf16[128,2048]{1,0:T(8,128)(2,1)S(1)}, bf16[128,2048]{1,0:T(8,128)(2,1)S(1)}, u32[]{:S(2)}, u32[]{:S(2)}) %collective-permute-start.17) | collective-permute-done | bytes 524320 | tf_op jit(solution)/shard_map/ppermute | solution.py:58
  121.8 9.1 %collective-permute-done.18 = bf16[128,2048]{1,0:T(8,128)(2,1)S(1)} collective-permute-done((bf16[128,2048]{1,0:T(8,128)(2,1)S(1)}, bf16[128,2048]{1,0:T(8,128)(2,1)S(1)}, u32[]{:S(2)}, u32[]{:S(2)}) %collective-permute-start.18) | collective-permute-done | bytes 524320 | tf_op jit(solution)/shard_map/ppermute | solution.py:58
  136.0 6.6 %collective-permute-done.19 = bf16[128,2048]{1,0:T(8,128)(2,1)S(1)} collective-permute-done((bf16[128,2048]{1,0:T(8,128)(2,1)S(1)}, bf16[128,2048]{1,0:T(8,128)(2,1)S(1)}, u32[]{:S(2)}, u32[]{:S(2)}) %collective-permute-start.19) | collective-permute-done | bytes 524320 | tf_op jit(solution)/shard_map/ppermute | solution.py:58
  142.6 4.2 collective-permute-done.15
  150.9 11.3 %collective-permute-done.22.refs_0_.refs_6_ = bf16[128,2048]{1,0:T(8,128)(2,1)S(1)} collective-permute-done((bf16[128,2048]{1,0:T(8,128)(2,1)S(1)}, bf16[128,2048]{1,0:T(8,128)(2,1)S(1)}, u32[]{:S(2)}, u32[]{:S(2)}) %collective-permute-start.22) | collective-permute-done | bytes 524320 | tf_op jit(solution)/shard_map/ppermute | solution.py:58
  165.2 14.3 %moe_in.3.refs_7_ = bf16[384,4096]{1,0:T(8,128)(2,1)} custom-call(bf16[128,2048]{1,0:T(8,128)(2,1)} %copy-done.57, bf16[128,2048]{1,0:T(8,128)(2,1)} %copy-done.58, bf16[128,2048]{1,0:T(8,128)(2,1)} %copy-done.28, bf16[2048,4096]{1,0:T(8,128)(2,1)} %all-gather.5.cloned.1.call-done.refs_3_.refs_2_.refs_4_.refs_6_.refs_8_), custom_call_target="tpu_custom_call" | custom-call | flops 7008000000 | bytes 1048576 | tf_op jit(solution)/shard_map/moe_in/pallas_call | solution.py:579
  182.5 11.5 %moe_in.4.refs_6_ = bf16[256,4096]{1,0:T(8,128)(2,1)} custom-call(bf16[128,2048]{1,0:T(8,128)(2,1)} %collective-permute-done.23.refs_0_.refs_4_, bf16[128,2048]{1,0:T(8,128)(2,1)} %collective-permute-done.21.refs_1_.refs_5_, bf16[2048,4096]{1,0:T(8,128)(2,1)} %all-gather.5.cloned.1.call-done.refs_3_.refs_2_.refs_4_.refs_6_.refs_8_), custom_call_target="tpu_custom_call" | custom-call | flops 5472000000 | bytes 1048576 | tf_op jit(solution)/shard_map/moe_in/pallas_call | solution.py:579
  208.7 13.1 %moe_in.5.refs_5_ = bf16[384,4096]{1,0:T(8,128)(2,1)} custom-call(bf16[64,2048]{1,0:T(8,128)(2,1)} %copy-done.60, bf16[64,2048]{1,0:T(8,128)(2,1)} %copy-done.61, bf16[128,2048]{1,0:T(8,128)(2,1)} %copy-done.39, bf16[128,2048]{1,0:T(8,128)(2,1)} %copy-done.38, bf16[2048,4096]{1,0:T(8,128)(2,1)} %all-gather.5.cloned.1.call-done.refs_3_.refs_2_.refs_4_.refs_6_.refs_8_), custom_call_target="tpu_custom_call" | custom-call | flops 7008000000 | bytes 1048576 | tf_op jit(solution)/shard_map/moe_in/pallas_call | solution.py:579
  231.3 24.5 %moe_mid.2 = (bf16[64,2176]{1,0:T(8,128)(2,1)}, bf16[64,2176]{1,0:T(8,128)(2,1)}, bf16[128,2176]{1,0:T(8,128)(2,1)}, bf16[128,2176]{1,0:T(8,128)(2,1)}, bf16[64,...) custom-call(bf16[384,128]{1,0:T(8,128)(2,1)} %pad_slice_fusion.refs_, ...), custom_call_target="tpu_custom_call" | custom-call | flops 12816000000 | bytes 1048576 | tf_op jit(solution)/shard_map/moe_mid/pallas_call | solution.py:661
  258.7 5.5 turn_rows.1.xt
  270.0 35.8 %moe_mid.3 = (bf16[128,2176]{1,0:T(8,128)(2,1)}, bf16[128,2176]{1,0:T(8,128)(2,1)}, bf16[128,2176]{1,0:T(8,128)(2,1)}, bf16[128,2176]{1,0:T(8,128)(2,1)}, bf16[1...) custom-call(bf16[640,128]{1,0:T(8,128)(2,1)} %pad_slice_fusion.1.ref, ...), custom_call_target="tpu_custom_call" | custom-call | flops 18959998976 | bytes 1048576 | tf_op jit(solution)/shard_map/moe_mid/pallas_call | solution.py:661
  311.2 15.3 %out_grad.1 = bf16[16,128,2048]{2,1,0:T(8,128)(2,1)} custom-call(bf16[384,2048]{1,0:T(8,128)(2,1)} %get-tuple-element.201.refs_0_, bf16[640,2048]{1,0:T(8,128)(2,1)} %get-tuple-element.202.refs_1_, bf16[64,2048]{1,0:T(8,128)(2,1)} %copy-done.62, bf16[64,2048]{1,0:T(8,128)(2,1)} %copy-done.63, bf16[128,2048]{1,0:T(8,128)(2,1)} %collective-permute-done.29.refs_3_.refs_4_, ...), custom_call_target="tpu_custom_call" | custom-call | flops 7200000000 | bytes 1048576 | tf_op jit(solution)/shard_map/out_grad/pallas_call | solution.py:800
  329.3 7.0 %collective-permute-done.37 = bf16[128,2176]{1,0:T(8,128)(2,1)S(1)} collective-permute-done((bf16[128,2176]{1,0:T(8,128)(2,1)}, bf16[128,2176]{1,0:T(8,128)(2,1)S(1)}, u32[]{:S(2)}, u32[]{:S(2)}) %collective-permute-start.37) | collective-permute-done | bytes 557088 | tf_op jit(solution)/shard_map/ppermute | solution.py:58
  339.7 9.8 %in_grad.4 = (bf16[2,8,2,512,128]{4,3,2,1,0:T(8,128)(2,1)}, bf16[2,8,2,512,128]{4,3,2,1,0:T(8,128)(2,1)}) custom-call(s32[4]{0:T(128)} %dynamic-slice_bitcast_fusion.places, bf16[2048,1024]{1,0:T(8,128)(2,1)} %turn_rows.1.xt, bf16[384,4096]{1,0:T(8,128)(2,1)} %get-tuple-element.206.refs_0_, bf16[640,4096]{1,0:T(8,128)(2,1)} %get-tuple-element.207.refs_1_), custom_call_target="tpu_custom_call" | custom-call | flops 5400000000 | bytes 1048576 | tf_op jit(solution)/shard_map/in_grad/pallas_call | solution.py:761
  359.0 9.9 %in_grad.5 = (bf16[2,8,2,512,128]{4,3,2,1,0:T(8,128)(2,1)}, bf16[2,8,2,512,128]{4,3,2,1,0:T(8,128)(2,1)}) custom-call(s32[4]{0:T(128)} %dynamic-slice_bitcast_fusion.places, bf16[2048,1024]{1,0:T(8,128)(2,1)} %turn_rows.1.xt, bf16[384,4096]{1,0:T(8,128)(2,1)} %get-tuple-element.206.refs_0_, ...), custom_call_target="tpu_custom_call", output_to_operand_aliasing={{0}: (4, {}), {1}: (5, {})} | custom-call | flops 5400000000 | bytes 1048576 | tf_op jit(solution)/shard_map/in_grad/pallas_call | solution.py:761
  371.0 9.7 %in_grad.6 = (bf16[2,8,2,512,128]{4,3,2,1,0:T(8,128)(2,1)}, bf16[2,8,2,512,128]{4,3,2,1,0:T(8,128)(2,1)}) custom-call(s32[4]{0:T(128)} %dynamic-slice_bitcast_fusion.places, bf16[2048,1024]{1,0:T(8,128)(2,1)} %turn_rows.1.xt, bf16[384,4096]{1,0:T(8,128)(2,1)} %get-tuple-element.206.refs_0_, bf16[640,4096]{1,0:T(8,128)(2,1)} %get-tuple-element.207.refs_1_), custom_call_target="tpu_custom_call" | custom-call | flops 5400000000 | bytes 1048576 | tf_op jit(solution)/shard_map/in_grad/pallas_call | solution.py:761
  380.7 4.3 add_convert_fusion.1
  387.2 9.7 %in_grad.7 = (bf16[2,8,2,512,128]{4,3,2,1,0:T(8,128)(2,1)}, bf16[2,8,2,512,128]{4,3,2,1,0:T(8,128)(2,1)}) custom-call(s32[4]{0:T(128)} %dynamic-slice_bitcast_fusion.places, bf16[2048,1024]{1,0:T(8,128)(2,1)} %turn_rows.1.xt, bf16[384,4096]{1,0:T(8,128)(2,1)} %get-tuple-element.206.refs_0_, ...), custom_call_target="tpu_custom_call", output_to_operand_aliasing={{0}: (4, {}), {1}: (5, {})} | custom-call | flops 5400000000 | bytes 1048576 | tf_op jit(solution)/shard_map/in_grad/pallas_call | solution.py:761
  418.3 15.5 %attn_back.1 = (f32[1024,256]{1,0:T(8,128)}, f32[1024,256]{1,0:T(8,128)}, f32[1024,256]{1,0:T(8,128)}, bf16[1024,2048]{1,0:T(8,128)(2,1)}) custom-call(s32[8]{0:T(128)} %dynamic-slice_bitcast_fusion.1.refs_0_, bf16[64,2048]{1,0:T(8,128)(2,1)} %copy-done.64, bf16[64,2048]{1,0:T(8,128)(2,1)} %copy-done.65, bf16[128,2048]{1,0:T(8,128)(2,1)} %collective-permute-done.46.refs_3_, ...), custom_call_target="tpu_custom_call" | custom-call | flops 8400000000 | bytes 1048576 | tf_op jit(solution)/shard_map/attn_back/pallas_call | solution.py:428
  436.3 18.0 %proj_back.1 = (bf16[1024,768]{1,0:T(8,128)(2,1)}, f32[2,256]{1,0:T(2,128)}, f32[1,2048]{1,0:T(1,128)}, bf16[64,2048]{1,0:T(8,128)(2,1)}, bf16[64,2048]{1,0:T(8,...) custom-call(s32[8]{0:T(128)} %dynamic-slice_bitcast_fusion.1.refs_0_, ...), custom_call_target="tpu_custom_call" | custom-call | flops 7200000000 | bytes 1048576 | tf_op jit(solution)/shard_map/proj_back/pallas_call | solution.py:495
  466.8 9.8 %attn_grad.1 = (bf16[2,3,512,256]{3,2,1,0:T(8,128)(2,1)}, bf16[2,3,512,256]{3,2,1,0:T(8,128)(2,1)}, bf16[2,256,512]{2,1,0:T(8,128)(2,1)}, bf16[2,256,512]{2,1,0:T(8,128)(2,1)}) custom-call(s32[4]{0:T(128)} %dynamic-slice_bitcast_fusion.places, bf16[1024,2048]{1,0:T(8,128)(2,1)} %get-tuple-element.242.refs_10_.xa.xb, ...), custom_call_target="tpu_custom_call" | custom-call | flops 3600000000 | bytes 1048576 | tf_op jit(solution)/shard_map/attn_grad/pallas_call | solution.py:531
  479.8 6.0 %place.1 = f32[16,128,512]{2,1,0:T(8,128)} custom-call(bf16[16,128,512]{2,1,0:T(8,128)(2,1)} %reduce-scatter.2.cloned.1.call-done.refs_0_), custom_call_target="tpu_custom_call" | custom-call | flops 1800000000 | bytes 1048576 | tf_op jit(solution)/shard_map/place/pallas_call | solution.py:849
  489.3 5.4 finish.2.refs_0_
  522.4 6.0 %collective-permute-done.64 = bf16[128,2048]{1,0:T(8,128)(2,1)} collective-permute-done((bf16[128,2048]{1,0:T(8,128)(2,1)}, bf16[128,2048]{1,0:T(8,128)(2,1)}, u32[]{:S(2)}, u32[]{:S(2)}) %collective-permute-start.64) | collective-permute-done | bytes 524320 | tf_op jit(solution)/shard_map/ppermute | solution.py:58
  535.9 5.4 finish.3
  (449 shorter events, 203.0 us)
Async XLA Ops:
  7.2 58.8 %all-gather.9.cloned.1.call-start = ((), (), s32[]{:S(2)}) async-start(), calls=%async_computation.4 | async-start | bytes 5283840 | tf_op jit(solution)/shard_map/all_gather | solution.py:930
  12.0 153.2 %all-gather.5.cloned.1.call-start = ((), (), s32[]{:S(2)}) async-start(), calls=%async_computation.1 | async-start | bytes 20971520 | tf_op jit(solution)/shard_map/all_gather | solution.py:948
  12.3 15.7 %collective-permute-start.2 = (bf16[128,2176]{1,0:T(8,128)(2,1)S(1)}, bf16[128,2176]{1,0:T(8,128)(2,1)S(1)}, u32[]{:S(2)}, u32[]{:S(2)}) collective-permute-start(bf16[128,2176]{1,0:T(8,128)(2,1)S(1)} %fusion.12.refs_9_), channel_id=1, source_target_pairs={{0,1},{2,0},{4,2},{6,4},{7,6},{5,7},{3,5},{1,3},{8,9},{10,8},{12,1... | collective-permute-start | bytes 1671176 | tf_op jit(solution)/shard_map/ppermute | solution.py:58
  15.3 14.4 %collective-permute-start = (bf16[128,2176]{1,0:T(8,128)(2,1)S(1)}, bf16[128,2176]{1,0:T(8,128)(2,1)S(1)}, u32[]{:S(2)}, u32[]{:S(2)}) collective-permute-start(bf16[128,2176]{1,0:T(8,128)(2,1)S(1)} %fusion.12.refs_9_), channel_id=1, source_target_pairs={{0,2},{2,4},{4,6},{6,7},{7,5},{5,3},{3,1},{1,0},{8,10},{10,12},{12... | collective-permute-start | bytes 1671176 | tf_op jit(solution)/shard_map/ppermute | solution.py:58
  43.1 182.8 %all-gather.7.cloned.1.call-start = ((), (), s32[]{:S(2)}) async-start(), calls=%async_computation.2 | async-start | bytes 10485760 | tf_op jit(solution)/shard_map/all_gather | solution.py:977
  63.9 18.6 %collective-permute-start.8 = (bf16[128,2048]{1,0:T(8,128)(2,1)S(1)}, bf16[128,2048]{1,0:T(8,128)(2,1)S(1)}, u32[]{:S(2)}, u32[]{:S(2)}) collective-permute-start(bf16[128,2048]{1,0:T(8,128)(2,1)S(1)} %copy-done.13), channel_id=1, source_target_pairs={{0,2},{2,4},{4,6},{6,7},{7,5},{5,3},{3,1},{1,0},{8,10},{10,12},{12... | collective-permute-start | bytes 1572872 | tf_op jit(solution)/shard_map/ppermute | solution.py:58
  65.5 17.1 %collective-permute-start.9 = (bf16[128,2048]{1,0:T(8,128)(2,1)S(1)}, bf16[128,2048]{1,0:T(8,128)(2,1)}, u32[]{:S(2)}, u32[]{:S(2)}) collective-permute-start(bf16[128,2048]{1,0:T(8,128)(2,1)S(1)} %copy-done.13), channel_id=1, source_target_pairs={{0,1},{2,0},{4,2},{6,4},{7,6},{5,7},{3,5},{1,3},{8,9},{10,8},{12,1... | collective-permute-start | bytes 1572872 | tf_op jit(solution)/shard_map/ppermute | solution.py:58
  104.9 374.9 %reduce-scatter.2.cloned.1.call-start = ((), (), s32[]{:S(2)}) async-start(), calls=%async_computation.3 | async-start | bytes 10485760 | tf_op jit(solution)/shard_map/reduce_scatter | solution.py:1020
  148.0 14.2 %collective-permute-start.22 = (bf16[128,2048]{1,0:T(8,128)(2,1)S(1)}, bf16[128,2048]{1,0:T(8,128)(2,1)S(1)}, u32[]{:S(2)}, u32[]{:S(2)}) collective-permute-start(bf16[128,2048]{1,0:T(8,128)(2,1)S(1)} %multiply_convert_fusion.refs_2_.refs_8_), channel_id=1, source_target_pairs={{0,1},{2,0},{4,2},{6,4},{7,6},{5,7},{3,5},{1,3},{8,9},{10,8},{12,1... | collective-permute-start | bytes 1572872 | tf_op jit(solution)/shard_map/ppermute | solution.py:58
  149.0 14.5 %collective-permute-start.20 = (bf16[128,2048]{1,0:T(8,128)(2,1)S(1)}, bf16[128,2048]{1,0:T(8,128)(2,1)S(1)}, u32[]{:S(2)}, u32[]{:S(2)}) collective-permute-start(bf16[128,2048]{1,0:T(8,128)(2,1)S(1)} %multiply_convert_fusion.refs_2_.refs_8_), channel_id=1, source_target_pairs={{0,2},{2,4},{4,6},{6,7},{7,5},{5,3},{3,1},{1,0},{8,10},{10,12},{12... | collective-permute-start | bytes 1572872 | tf_op jit(solution)/shard_map/ppermute | solution.py:58
  162.2 17.5 %collective-permute-start.23 = (bf16[128,2048]{1,0:T(8,128)(2,1)S(1)}, bf16[128,2048]{1,0:T(8,128)(2,1)}, u32[]{:S(2)}, u32[]{:S(2)}) collective-permute-start(bf16[128,2048]{1,0:T(8,128)(2,1)S(1)} %collective-permute-done.22.refs_0_.refs_6_), channel_id=1, source_target_pairs={{0,1},{2,0},{4,2},{6,4},{7,6},{5,7},{3,5},{1,3},{8,9},{10,8},{12,1... | collective-permute-start | bytes 1572872 | tf_op jit(solution)/shard_map/ppermute | solution.py:58
  163.6 16.1 %collective-permute-start.21 = (bf16[128,2048]{1,0:T(8,128)(2,1)S(1)}, bf16[128,2048]{1,0:T(8,128)(2,1)}, u32[]{:S(2)}, u32[]{:S(2)}) collective-permute-start(bf16[128,2048]{1,0:T(8,128)(2,1)S(1)} %collective-permute-done.20.refs_1_.refs_7_), channel_id=1, source_target_pairs={{0,2},{2,4},{4,6},{6,7},{7,5},{5,3},{3,1},{1,0},{8,10},{10,12},{12... | collective-permute-start | bytes 1572872 | tf_op jit(solution)/shard_map/ppermute | solution.py:58
  179.6 14.3 %collective-permute-start.24 = (bf16[128,2048]{1,0:T(8,128)(2,1)}, bf16[128,2048]{1,0:T(8,128)(2,1)S(1)}, u32[]{:S(2)}, u32[]{:S(2)}) collective-permute-start(bf16[128,2048]{1,0:T(8,128)(2,1)} %collective-permute-done.21.refs_1_.refs_5_), channel_id=1, source_target_pairs={{0,2},{2,4},{4,6},{6,7},{7,5},{5,3},{3,1},{1,0},{8,10},{10,12},{12... | collective-permute-start | bytes 1572872 | tf_op jit(solution)/shard_map/ppermute | solution.py:58
  206.7 15.1 %collective-permute-start.28 = (bf16[128,2048]{1,0:T(8,128)(2,1)}, bf16[128,2048]{1,0:T(8,128)(2,1)S(1)}, u32[]{:S(2)}, u32[]{:S(2)}) collective-permute-start(bf16[128,2048]{1,0:T(8,128)(2,1)} %copy-done.55), channel_id=1, source_target_pairs={{0,2},{2,4},{4,6},{6,7},{7,5},{5,3},{3,1},{1,0},{8,10},{10,12},{12... | collective-permute-start | bytes 1572872 | tf_op jit(solution)/shard_map/ppermute | solution.py:58
  267.6 38.3 %collective-permute-start.34 = (bf16[192,2176]{1,0:T(8,128)(2,1)S(1)}, bf16[192,2176]{1,0:T(8,128)(2,1)S(1)}, u32[]{:S(2)}, u32[]{:S(2)}) collective-permute-start(bf16[192,2176]{1,0:T(8,128)(2,1)S(1)} %fusion.10), channel_id=1, source_target_pairs={{0,2},{2,4},{4,6},{6,7},{7,5},{5,3},{3,1},{1,0},{8,10},{10,12},{12... | collective-permute-start | bytes 2506760 | tf_op jit(solution)/shard_map/ppermute | solution.py:58
  268.9 39.0 %collective-permute-start.35 = (bf16[192,2176]{1,0:T(8,128)(2,1)S(1)}, bf16[192,2176]{1,0:T(8,128)(2,1)}, u32[]{:S(2)}, u32[]{:S(2)}) collective-permute-start(bf16[192,2176]{1,0:T(8,128)(2,1)S(1)} %fusion.11), channel_id=1, source_target_pairs={{0,1},{2,0},{4,2},{6,4},{7,6},{5,7},{3,5},{1,3},{8,9},{10,8},{12,1... | collective-permute-start | bytes 2506760 | tf_op jit(solution)/shard_map/ppermute | solution.py:58
  309.9 17.4 %collective-permute-start.36 = (bf16[128,2176]{1,0:T(8,128)(2,1)}, bf16[128,2176]{1,0:T(8,128)(2,1)}, u32[]{:S(2)}, u32[]{:S(2)}) collective-permute-start(bf16[128,2176]{1,0:T(8,128)(2,1)} %add_convert_fusion.6), channel_id=1, source_target_pairs={{0,2},{2,4},{4,6},{6,7},{7,5},{5,3},{3,1},{1,0},{8,10},{10,12},{12... | collective-permute-start | bytes 1671176 | tf_op jit(solution)/shard_map/ppermute | solution.py:58
  336.5 15.3 %collective-permute-start.38 = (bf16[128,2176]{1,0:T(8,128)(2,1)}, bf16[128,2176]{1,0:T(8,128)(2,1)S(1)}, u32[]{:S(2)}, u32[]{:S(2)}) collective-permute-start(bf16[128,2176]{1,0:T(8,128)(2,1)} %add_convert_fusion.4), channel_id=1, source_target_pairs={{0,2},{2,4},{4,6},{6,7},{7,5},{5,3},{3,1},{1,0},{8,10},{10,12},{12... | collective-permute-start | bytes 1671176 | tf_op jit(solution)/shard_map/ppermute | solution.py:58
  337.7 15.3 %collective-permute-start.39 = (bf16[128,2176]{1,0:T(8,128)(2,1)S(1)}, bf16[128,2176]{1,0:T(8,128)(2,1)}, u32[]{:S(2)}, u32[]{:S(2)}) collective-permute-start(bf16[128,2176]{1,0:T(8,128)(2,1)S(1)} %add_convert_fusion.3), channel_id=1, source_target_pairs={{0,1},{2,0},{4,2},{6,4},{7,6},{5,7},{3,5},{1,3},{8,9},{10,8},{12,1... | collective-permute-start | bytes 1671176 | tf_op jit(solution)/shard_map/ppermute | solution.py:58
  369.0 16.1 %collective-permute-start.42 = (bf16[128,2048]{1,0:T(8,128)(2,1)}, bf16[128,2048]{1,0:T(8,128)(2,1)S(1)}, u32[]{:S(2)}, u32[]{:S(2)}) collective-permute-start(bf16[128,2048]{1,0:T(8,128)(2,1)} %collective-permute-done.40.refs_8_), channel_id=1, source_target_pairs={{0,2},{2,4},{4,6},{6,7},{7,5},{5,3},{3,1},{1,0},{8,10},{10,12},{12... | collective-permute-start | bytes 1572872 | tf_op jit(solution)/shard_map/ppermute | solution.py:58
  369.8 15.3 %collective-permute-start.43 = (bf16[128,2048]{1,0:T(8,128)(2,1)}, bf16[128,2048]{1,0:T(8,128)(2,1)}, u32[]{:S(2)}, u32[]{:S(2)}) collective-permute-start(bf16[128,2048]{1,0:T(8,128)(2,1)} %collective-permute-done.41.refs_7_), channel_id=1, source_target_pairs={{0,1},{2,0},{4,2},{6,4},{7,6},{5,7},{3,5},{1,3},{8,9},{10,8},{12,1... | collective-permute-start | bytes 1572872 | tf_op jit(solution)/shard_map/ppermute | solution.py:58
  403.6 50.7 %collective-permute-start.54 = (bf16[1,8,2,512,128]{4,3,2,1,0:T(8,128)(2,1)}, bf16[1,8,2,512,128]{4,3,2,1,0:T(8,128)(2,1)}, u32[]{:S(2)}, u32[]{:S(2)}) collective-permute-start(bf16[1,8,2,512,128]{4,3,2,1,0:T(8,128)(2,1)} %add_convert_fusion.1), channel_id=1, source_target_pairs={{0,16},{8,24},{16,0},{24,8},{1,17},{9,25},{17,1},{25,9},{2,18},{10... | collective-permute-start | bytes 6291464 | tf_op jit(solution)/shard_map/ppermute | solution.py:145
  416.1 17.8 %collective-permute-start.50 = (bf16[128,2048]{1,0:T(8,128)(2,1)}, bf16[128,2048]{1,0:T(8,128)(2,1)S(1)}, u32[]{:S(2)}, u32[]{:S(2)}) collective-permute-start(bf16[128,2048]{1,0:T(8,128)(2,1)} %add_convert_fusion.21), channel_id=1, source_target_pairs={{0,2},{2,4},{4,6},{6,7},{7,5},{5,3},{3,1},{1,0},{8,10},{10,12},{12... | collective-permute-start | bytes 1572872 | tf_op jit(solution)/shard_map/ppermute | solution.py:58
  416.7 18.0 %collective-permute-start.52 = (bf16[128,2048]{1,0:T(8,128)(2,1)}, bf16[128,2048]{1,0:T(8,128)(2,1)S(1)}, u32[]{:S(2)}, u32[]{:S(2)}) collective-permute-start(bf16[128,2048]{1,0:T(8,128)(2,1)} %add_convert_fusion.20), channel_id=1, source_target_pairs={{0,1},{2,0},{4,2},{6,4},{7,6},{5,7},{3,5},{1,3},{8,9},{10,8},{12,1... | collective-permute-start | bytes 1572872 | tf_op jit(solution)/shard_map/ppermute | solution.py:58
  434.0 20.3 %collective-permute-start.51 = (bf16[128,2048]{1,0:T(8,128)(2,1)S(1)}, bf16[128,2048]{1,0:T(8,128)(2,1)S(1)}, u32[]{:S(2)}, u32[]{:S(2)}) collective-permute-start(bf16[128,2048]{1,0:T(8,128)(2,1)S(1)} %add_convert_fusion.19), channel_id=1, source_target_pairs={{0,2},{2,4},{4,6},{6,7},{7,5},{5,3},{3,1},{1,0},{8,10},{10,12},{12... | collective-permute-start | bytes 1572872 | tf_op jit(solution)/shard_map/ppermute | solution.py:58
  435.0 19.3 %collective-permute-start.53 = (bf16[128,2048]{1,0:T(8,128)(2,1)S(1)}, bf16[128,2048]{1,0:T(8,128)(2,1)}, u32[]{:S(2)}, u32[]{:S(2)}) collective-permute-start(bf16[128,2048]{1,0:T(8,128)(2,1)S(1)} %add_convert_fusion.17), channel_id=1, source_target_pairs={{0,1},{2,0},{4,2},{6,4},{7,6},{5,7},{3,5},{1,3},{8,9},{10,8},{12,1... | collective-permute-start | bytes 1572872 | tf_op jit(solution)/shard_map/ppermute | solution.py:58
  456.0 57.8 %collective-permute-start.63 = (bf16[1,8,2,512,128]{4,3,2,1,0:T(8,128)(2,1)}, bf16[1,8,2,512,128]{4,3,2,1,0:T(8,128)(2,1)}, u32[]{:S(2)}, u32[]{:S(2)}) collective-permute-start(bf16[1,8,2,512,128]{4,3,2,1,0:T(8,128)(2,1)} %add_convert_fusion), channel_id=1, source_target_pairs={{0,16},{8,24},{16,0},{24,8},{1,17},{9,25},{17,1},{25,9},{2,18},{10... | collective-permute-start | bytes 6291464 | tf_op jit(solution)/shard_map/ppermute | solution.py:145
  488.8 15.5 %collective-permute-start.61 = (bf16[2,3,512,256]{3,2,1,0:T(8,128)(2,1)}, bf16[2,3,512,256]{3,2,1,0:T(8,128)(2,1)}, u32[]{:S(2)}, u32[]{:S(2)}) collective-permute-start(bf16[2,3,512,256]{3,2,1,0:T(8,128)(2,1)} %get-tuple-element.265), channel_id=1, source_target_pairs={{0,8},{8,0},{16,24},{24,16},{1,9},{9,1},{17,25},{25,17},{2,10},{10... | collective-permute-start | bytes 4718600 | tf_op jit(solution)/shard_map/ppermute | solution.py:145
  513.8 14.6 %collective-permute-start.64 = (bf16[128,2048]{1,0:T(8,128)(2,1)}, bf16[128,2048]{1,0:T(8,128)(2,1)}, u32[]{:S(2)}, u32[]{:S(2)}) collective-permute-start(bf16[128,2048]{1,0:T(8,128)(2,1)} %add_convert_fusion.11), channel_id=1, source_target_pairs={{0,2},{2,4},{4,6},{6,7},{7,5},{5,3},{3,1},{1,0},{8,10},{10,12},{12... | collective-permute-start | bytes 1572872 | tf_op jit(solution)/shard_map/ppermute | solution.py:58
  515.2 14.4 %collective-permute-start.65 = (bf16[128,2048]{1,0:T(8,128)(2,1)}, bf16[128,2048]{1,0:T(8,128)(2,1)}, u32[]{:S(2)}, u32[]{:S(2)}) collective-permute-start(bf16[128,2048]{1,0:T(8,128)(2,1)} %add_convert_fusion.10), channel_id=1, source_target_pairs={{0,1},{2,0},{4,2},{6,4},{7,6},{5,7},{3,5},{1,3},{8,9},{10,8},{12,1... | collective-permute-start | bytes 1572872 | tf_op jit(solution)/shard_map/ppermute | solution.py:58
  519.1 22.2 %collective-permute-start.69 = (bf16[1,256,512]{2,1,0:T(8,128)(2,1)S(1)}, bf16[1,256,512]{2,1,0:T(8,128)(2,1)}, u32[]{:S(2)}, u32[]{:S(2)}) collective-permute-start(bf16[1,256,512]{2,1,0:T(8,128)(2,1)S(1)} %add_convert_fusion.28), channel_id=1, source_target_pairs={{0,16},{8,24},{16,0},{24,8},{1,17},{9,25},{17,1},{25,9},{2,18},{10... | collective-permute-start | bytes 786440 | tf_op jit(solution)/shard_map/ppermute | solution.py:145
  520.1 24.3 %collective-permute-start.68 = (bf16[1,3,512,256]{3,2,1,0:T(8,128)(2,1)}, bf16[1,3,512,256]{3,2,1,0:T(8,128)(2,1)}, u32[]{:S(2)}, u32[]{:S(2)}) collective-permute-start(bf16[1,3,512,256]{3,2,1,0:T(8,128)(2,1)} %add_convert_fusion.2), channel_id=1, source_target_pairs={{0,16},{8,24},{16,0},{24,8},{1,17},{9,25},{17,1},{25,9},{2,18},{10... | collective-permute-start | bytes 2359304 | tf_op jit(solution)/shard_map/ppermute | solution.py:145
  (116 other events, 1174.7 us)
Sparse Core Ops, SparseCore 0:
  12.1 37.3 all-gather.8
  51.6 105.9 all-gather.4
  159.2 58.2 all-gather.6
  339.8 71.1 reduce-scatter.1

commit v4 on v3

--- a/solution.py
+++ b/solution.py
@@ -258,46 +258,42 @@
     return (seg_col[pl.ds(first, rows), :] == seg_row[:, pl.ds(0, width)]) & (key_pos <= row_pos)
 
 
-def attn_proj_body(count, block, *refs):
+def attn_proj_body(count, *refs):
     it = iter(refs)
     order = next(it)
     pieces = [next(it) for _ in range(count)]
     wq = next(it)
     gain, gains, cosine, sine = (next(it) for _ in range(4))
     q_o, k_o, v_o, qr_o, kr_o, x_o = (next(it) for _ in range(6))
-    xs, xn, wqs, sems = (next(it) for _ in range(4))
-    length, width = q_o.shape
+    xs, wqs, sems = (next(it) for _ in range(3))
+    block, width = q_o.shape
     heads = width // HD
-    starts = piece_rows(order, pieces[0].shape[0], count)
-    copies = load_projections(wq, wqs, sems, count)
-    for copy in copies:
-        copy.start()
-    for copy in fetch(pieces, xs, sems, 0, starts) + copies:
-        copy.wait()
-
-    def project(r, _):
-        rows = pl.ds(pl.multiple_of(r * block, block), block)
-        wide = xs[rows, :].astype(f32)
-        inv = lax.rsqrt(jnp.mean(wide * wide, axis=-1, keepdims=True) + EPSILON)
-        xn[rows, :] = (wide * inv * gain[...]).astype(bf16)
-        out = dot(xn[rows, :], wqs[...])
-        v_o[rows, :] = out[:, 2 * width :].astype(bf16)
-        for j, (raw_o, hat_o) in enumerate(((qr_o, q_o), (kr_o, k_o))):
-            raw = out[:, j * width : (j + 1) * width]
-            raw_o[rows, :] = raw
-            for h in range(heads):
-                cols = slice(h * HD, (h + 1) * HD)
-                u = raw[:, cols]
-                inv = lax.rsqrt(jnp.mean(u * u, axis=-1, keepdims=True) + EPSILON)
-                u = u * inv * gains[j : j + 1, cols]
-                u = u * cosine[rows, :] + pltpu.roll(u, HD // 2, 1) * sine[rows, :]
-                hat_o[rows, cols] = u.astype(bf16)
-        return 0
-
-    lax.fori_loop(0, length // block, project, 0)
-    keep = pltpu.make_async_copy(xn, x_o, sems.at[0])
-    keep.start()
-    keep.wait()
+    step = pl.program_id(0)
+
+    @pl.when(step == 0)
+    def _():
+        starts = piece_rows(order, pieces[0].shape[0], count)
+        copies = load_projections(wq, wqs, sems, count)
+        for copy in copies:
+            copy.start()
+        for copy in fetch(pieces, xs, sems, 0, starts) + copies:
+            copy.wait()
+
+    wide = xs[pl.ds(pl.multiple_of(step * block, block), block), :].astype(f32)
+    inv = lax.rsqrt(jnp.mean(wide * wide, axis=-1, keepdims=True) + EPSILON)
+    x_o[...] = (wide * inv * gain[...]).astype(bf16)
+    out = dot(x_o[...], wqs[...])
+    v_o[...] = out[:, 2 * width :].astype(bf16)
+    for j, (raw_o, hat_o) in enumerate(((qr_o, q_o), (kr_o, k_o))):
+        raw = out[:, j * width : (j + 1) * width]
+        raw_o[...] = raw
+        for h in range(heads):
+            cols = slice(h * HD, (h + 1) * HD)
+            u = raw[:, cols]
+            inv = lax.rsqrt(jnp.mean(u * u, axis=-1, keepdims=True) + EPSILON)
+            u = u * inv * gains[j : j + 1, cols]
+            u = u * cosine[...] + pltpu.roll(u, HD // 2, 1) * sine[...]
+            hat_o[:, cols] = u.astype(bf16)
 
 
 def attn_proj(order, pieces, wq, gain, gains, cosine, sine):
@@ -305,15 +301,23 @@
     d = gain.shape[1]
     length = cosine.shape[0]
     width = wq.shape[2]
+    block = min(256, length)
+
+    def rows(columns):
+        return pl.BlockSpec((block, columns), lambda r: (r, 0))
+
+    def whole(a):
+        return pl.BlockSpec(a.shape, lambda r: (0, 0))
+
     return pl.pallas_call(
-        functools.partial(attn_proj_body, count, min(256, length)),
-        in_specs=[SMEM] + [ANY] * (count + 1) + [VMEM] * 4,
-        out_specs=[VMEM] * 5 + [ANY],
+        functools.partial(attn_proj_body, count),
+        grid=(length // block,),
+        in_specs=[SMEM] + [ANY] * (count + 1) + [whole(gain), whole(gains), rows(HD), rows(HD)],
+        out_specs=[rows(width)] * 5 + [rows(d)],
         out_shape=[shape((length, width), bf16)] * 3
         + [shape((length, width), f32)] * 2
         + [shape((length, d), bf16)],
         scratch_shapes=[
-            pltpu.VMEM((length, d), bf16),
             pltpu.VMEM((length, d), bf16),
             pltpu.VMEM((d, 3 * width), bf16),
             pltpu.SemaphoreType.DMA((count + 3 * n,)),
@@ -442,7 +446,7 @@
     )(order, *pieces, wo, q, k, v, lse, seg_row, seg_col)
 
 
-def proj_back_body(count, block, *refs):
+def proj_back_body(count, steps, *refs):
     it = iter(refs)
     order = next(it)
     wq = next(it)
@@ -451,40 +455,42 @@
     dp_o, hg_o, gs_o = (next(it) for _ in range(3))
     outs = [next(it) for _ in range(count)]
     wqs, stage, sems = (next(it) for _ in range(3))
-    length, width = qr.shape
+    block, width = qr.shape
     heads = width // HD
-    starts = piece_rows(order, outs[0].shape[0], count)
-    copies = load_projections(wq, wqs, sems, count)
-    for copy in copies:
-        copy.start()
-    hg_o[...] = jnp.zeros_like(hg_o)
-    gs_o[...] = jnp.zeros_like(gs_o)
-    for copy in copies:
-        copy.wait()
-
-    def finish(r, _):
-        rows = pl.ds(pl.multiple_of(r * block, block), block)
-        dp_o[rows, 2 * width :] = dv[rows, :].astype(bf16)
-        for j, (raw, grad) in enumerate(((qr, dq), (kr, dk))):
-            for h in range(heads):
-                cols = slice(h * HD, (h + 1) * HD)
-                u = raw[rows, cols]
-                inv = lax.rsqrt(jnp.mean(u * u, axis=-1, keepdims=True) + EPSILON)
-                hat = u * inv
-                t = grad[rows, cols]
-                t = t * cosine[rows, :] - pltpu.roll(t, HD // 2, 1) * sine[rows, :]
-                hg_o[j : j + 1, cols] += jnp.sum(t * hat, axis=0, keepdims=True)
-                w = t * gains[j : j + 1, cols]
-                w = inv * (w - hat * jnp.mean(w * hat, axis=-1, keepdims=True))
-                dp_o[rows, j * width + h * HD : j * width + (h + 1) * HD] = w.astype(bf16)
-        out = dot_nt(dp_o[rows, :], wqs[...])
-        gs_o[...] += jnp.sum(out * x[rows, :].astype(f32), axis=0, keepdims=True)
-        stage[rows, :] = out.astype(bf16)
-        return 0
-
-    lax.fori_loop(0, length // block, finish, 0)
-    for copy in send_out(stage, outs, sems, 0, starts):
-        copy.wait()
+    step = pl.program_id(0)
+
+    @pl.when(step == 0)
+    def _():
+        copies = load_projections(wq, wqs, sems, count)
+        for copy in copies:
+            copy.start()
+        hg_o[...] = jnp.zeros_like(hg_o)
+        gs_o[...] = jnp.zeros_like(gs_o)
+        for copy in copies:
+            copy.wait()
+
+    dp_o[:, 2 * width :] = dv[...].astype(bf16)
+    for j, (raw, grad) in enumerate(((qr, dq), (kr, dk))):
+        for h in range(heads):
+            cols = slice(h * HD, (h + 1) * HD)
+            u = raw[:, cols]
+            inv = lax.rsqrt(jnp.mean(u * u, axis=-1, keepdims=True) + EPSILON)
+            hat = u * inv
+            t = grad[:, cols]
+            t = t * cosine[...] - pltpu.roll(t, HD // 2, 1) * sine[...]
+            hg_o[j : j + 1, cols] += jnp.sum(t * hat, axis=0, keepdims=True)
+            w = t * gains[j : j + 1, cols]
+            w = inv * (w - hat * jnp.mean(w * hat, axis=-1, keepdims=True))
+            dp_o[:, j * width + h * HD : j * width + (h + 1) * HD] = w.astype(bf16)
+    out = dot_nt(dp_o[...], wqs[...])
+    gs_o[...] += jnp.sum(out * x[...].astype(f32), axis=0, keepdims=True)
+    stage[pl.ds(pl.multiple_of(step * block, block), block), :] = out.astype(bf16)
+
+    @pl.when(step == steps - 1)
+    def _():
+        starts = piece_rows(order, outs[0].shape[0], count)
+        for copy in send_out(stage, outs, sems, 0, starts):
+            copy.wait()
 
 
 def proj_back(order, wq, qr, kr, dq, dk, dv, gains, cosine, sine, x, own_rows):
@@ -492,10 +498,22 @@
     length, width = qr.shape
     d = x.shape[1]
     count = length // own_rows + 1
+    block = min(256, length)
+    steps = length // block
+
+    def rows(columns):
+        return pl.BlockSpec((block, columns), lambda r: (r, 0))
+
+    def whole(dims):
+        return pl.BlockSpec(dims, lambda r: (0, 0))
+
     return pl.pallas_call(
-        functools.partial(proj_back_body, count, min(256, length)),
-        in_specs=[SMEM] + [ANY] + [VMEM] * 9,
-        out_specs=[VMEM] * 3 + [ANY] * count,
+        functools.partial(proj_back_body, count, steps),
+        grid=(steps,),
+        in_specs=[SMEM, ANY]
+        + [rows(width)] * 5
+        + [whole(gains.shape), rows(HD), rows(HD), rows(d)],
+        out_specs=[rows(3 * width), whole((2, width)), whole((1, d))] + [ANY] * count,
         out_shape=[
             shape((length, 3 * width), bf16),
             shape((2, width), f32),
@@ -848,9 +866,9 @@
     before = [] if whole is None else [whole]
     return pl.pallas_call(
         place_body,
-        grid=(part.shape[0] // 2,),
-        in_specs=[ANY] * len(before) + [pl.BlockSpec((2,) + rest, lambda s: (s,) + zeros)],
-        out_specs=pl.BlockSpec((2,) + rest, lambda s: (s,) + zeros),
+        grid=(part.shape[0] // 4,),
+        in_specs=[ANY] * len(before) + [pl.BlockSpec((4,) + rest, lambda s: (s,) + zeros)],
+        out_specs=pl.BlockSpec((4,) + rest, lambda s: (s,) + zeros),
         out_shape=shape((experts,) + rest, f32),
         input_output_aliases={0: 0} if before else {},
         compiler_params=pltpu.CompilerParams(vmem_limit_bytes=VMEM_BYTES),
@@ -867,7 +885,7 @@
             out[:, at : at + fw] = w[i, g]
 
 
-def pack(gate_up, group=4):
+def pack(gate_up, group=2):
     experts, _, depth, fw = gate_up.shape
     return pl.pallas_call(
         pack_body,

time: 569 us -> 566 us (level)
    pallas_call x3, Pallas kernels: 37.3 us -> 31 us  [the longest x1 15.5 us: proj_back(): pl.pallas_call(functools.partial(proj_back_body, count, steps), grid=(ste...]
  transfers between devices with their start and end apart: 79 -> 79, of which waited for: 40 -> 42; matrix products, arithmetic and copies ran while one was open for 11% -> 11% of each run, Pallas kernels for 40% -> 39%
where the time goes in v4:
time: 566 us; the launch traced here: 556 us
  Pallas kernels  243 us (43%)
  waiting for transfers between devices  137 us (24%)
  starting transfers between devices  82.5 us (15%)
  other arithmetic  52.6 us (9%)
  local copies, waits for them, and re-layouts  25.4 us (4%)
  between operations  15.3 us (3%)
    ppermute x62, waiting for transfers between devices, ring_step(): return lax.ppermute(value, 'tensor', pairs)  134 us
    ppermute x62, starting transfers between devices, ring_step(): return lax.ppermute(value, 'tensor', pairs)  72 us
    pallas_call x2, Pallas kernels, moe_mid(): pl.pallas_call(functools.partial(moe_mid_body, group, steps, len(gus), co...  60.4 us
    pallas_call x4, Pallas kernels, in_grad(): pl.pallas_call(functools.partial(in_grad_body, n, group, sets), grid=(num...  39.1 us
    pallas_call x3, Pallas kernels, moe_in(): pl.pallas_call(functools.partial(moe_in_body, count), grid=(columns // wi...  38.8 us
    pallas_call x1, Pallas kernels, proj_back(): pl.pallas_call(functools.partial(proj_back_body, count, steps), grid=(ste...  15.5 us
    pallas_call x1, Pallas kernels, attn_back(): pl.pallas_call(functools.partial(attn_back_body, count, min(256, length))...  15.5 us
    pallas_call x1, Pallas kernels, out_grad(): pl.pallas_call(functools.partial(out_grad_body, group, count, len(hws)),...  15.3 us
  transfers between devices with their start and end apart: 79, of which 42 were waited for; matrix products, arithmetic and copies ran while one was open for 11% of the time, Pallas kernels for 39%

profile of v4, /device:TPU:0, one launch (start us, length us, event | category | flops | bytes accessed | tf_op | source)
XLA Modules:
  0.0 555.9 jit_solution(7150192394157174029)
XLA Ops:
  15.4 12.6 %collective-permute-done.2.refs_7_ = bf16[128,2176]{1,0:T(8,128)(2,1)S(1)} collective-permute-done((bf16[128,2176]{1,0:T(8,128)(2,1)S(1)}, bf16[128,2176]{1,0:T(8,128)(2,1)S(1)}, u32[]{:S(2)}, u32[]{:S(2)}) %collective-permute-start.2) | collective-permute-done | bytes 557088 | tf_op jit(solution)/shard_map/ppermute | solution.py:58
  30.0 6.8 %pack.1 = bf16[512,4096]{1,0:T(8,128)(2,1)} custom-call(bf16[16,2,512,128]{3,2,1,0:T(8,128)(2,1)} %w), custom_call_target="tpu_custom_call" | custom-call | flops 2400000000 | bytes 1048576 | tf_op jit(solution)/shard_map/pack/pallas_call | solution.py:890
  36.8 5.1 collective-permute-done.3.refs_5_
  45.2 10.9 %collective-permute-done.4.refs_4_ = bf16[128,2176]{1,0:T(8,128)(2,1)S(1)} collective-permute-done((bf16[128,2176]{1,0:T(8,128)(2,1)}, bf16[128,2176]{1,0:T(8,128)(2,1)S(1)}, u32[]{:S(2)}, u32[]{:S(2)}) %collective-permute-start.4) | collective-permute-done | bytes 557088 | tf_op jit(solution)/shard_map/ppermute | solution.py:58
  69.2 11.3 %attn_proj.1 = (bf16[1024,256]{1,0:T(8,128)(2,1)}, bf16[1024,256]{1,0:T(8,128)(2,1)}, bf16[1024,256]{1,0:T(8,128)(2,1)}, f32[1024,256]{1,0:T(8,128)}, f32[1024,256]{1,0:T(8,128)}, /*index=5*/bf16[1024,2048]{1,0:T(8,128)(2,1)}) custom-call(s32[8]{0:T(128)} %dynamic-slice_bitcast_fusion.1.refs_0_, bf16[64,2176]{1,0:T(8,128)(2,1)} %copy-done.42, ...), custom_call_target="tpu_custom_call" | custom-call | flops 6000000000 | bytes 1048576 | tf_op jit(solution)/shard_map/attn_proj/pallas_call | solution.py:312
  82.6 10.4 %attn_core.1 = (bf16[1024,256]{1,0:T(8,128)(2,1)}, f32[2,1024,1]{2,1,0:T(8,128)}, bf16[64,2048]{1,0:T(8,128)(2,1)}, bf16[64,2048]{1,0:T(8,128)(2,1)}, bf16[128,2...) custom-call(s32[8]{0:T(128)} %dynamic-slice_bitcast_fusion.1.refs_0_, ...), custom_call_target="tpu_custom_call" | custom-call | flops 6000000000 | bytes 1048576 | tf_op jit(solution)/shard_map/attn_core/pallas_call | solution.py:371
  95.4 4.6 collective-permute-done.12
  106.0 8.9 %collective-permute-done.17 = bf16[128,2048]{1,0:T(8,128)(2,1)S(1)} collective-permute-done((bf16[128,2048]{1,0:T(8,128)(2,1)S(1)}, bf16[128,2048]{1,0:T(8,128)(2,1)S(1)}, u32[]{:S(2)}, u32[]{:S(2)}) %collective-permute-start.17) | collective-permute-done | bytes 524320 | tf_op jit(solution)/shard_map/ppermute | solution.py:58
  118.9 9.0 %collective-permute-done.18 = bf16[128,2048]{1,0:T(8,128)(2,1)S(1)} collective-permute-done((bf16[128,2048]{1,0:T(8,128)(2,1)S(1)}, bf16[128,2048]{1,0:T(8,128)(2,1)S(1)}, u32[]{:S(2)}, u32[]{:S(2)}) %collective-permute-start.18) | collective-permute-done | bytes 524320 | tf_op jit(solution)/shard_map/ppermute | solution.py:58
  133.9 6.6 %collective-permute-done.19 = bf16[128,2048]{1,0:T(8,128)(2,1)S(1)} collective-permute-done((bf16[128,2048]{1,0:T(8,128)(2,1)S(1)}, bf16[128,2048]{1,0:T(8,128)(2,1)S(1)}, u32[]{:S(2)}, u32[]{:S(2)}) %collective-permute-start.19) | collective-permute-done | bytes 524320 | tf_op jit(solution)/shard_map/ppermute | solution.py:58
  149.3 11.4 %collective-permute-done.22.refs_0_.refs_6_ = bf16[128,2048]{1,0:T(8,128)(2,1)S(1)} collective-permute-done((bf16[128,2048]{1,0:T(8,128)(2,1)S(1)}, bf16[128,2048]{1,0:T(8,128)(2,1)S(1)}, u32[]{:S(2)}, u32[]{:S(2)}) %collective-permute-start.22) | collective-permute-done | bytes 524320 | tf_op jit(solution)/shard_map/ppermute | solution.py:58
  163.3 14.4 %moe_in.3.refs_7_ = bf16[384,4096]{1,0:T(8,128)(2,1)} custom-call(bf16[128,2048]{1,0:T(8,128)(2,1)} %copy-done.57, bf16[128,2048]{1,0:T(8,128)(2,1)} %copy-done.58, bf16[128,2048]{1,0:T(8,128)(2,1)} %copy-done.28, bf16[2048,4096]{1,0:T(8,128)(2,1)} %all-gather.5.cloned.1.call-done.refs_3_.refs_2_.refs_4_.refs_6_.refs_8_), custom_call_target="tpu_custom_call" | custom-call | flops 7008000000 | bytes 1048576 | tf_op jit(solution)/shard_map/moe_in/pallas_call | solution.py:597
  180.2 11.4 %moe_in.4.refs_6_ = bf16[256,4096]{1,0:T(8,128)(2,1)} custom-call(bf16[128,2048]{1,0:T(8,128)(2,1)} %collective-permute-done.23.refs_0_.refs_4_, bf16[128,2048]{1,0:T(8,128)(2,1)} %collective-permute-done.21.refs_1_.refs_5_, bf16[2048,4096]{1,0:T(8,128)(2,1)} %all-gather.5.cloned.1.call-done.refs_3_.refs_2_.refs_4_.refs_6_.refs_8_), custom_call_target="tpu_custom_call" | custom-call | flops 5472000000 | bytes 1048576 | tf_op jit(solution)/shard_map/moe_in/pallas_call | solution.py:597
  205.4 13.0 %moe_in.5.refs_5_ = bf16[384,4096]{1,0:T(8,128)(2,1)} custom-call(bf16[64,2048]{1,0:T(8,128)(2,1)} %copy-done.60, bf16[64,2048]{1,0:T(8,128)(2,1)} %copy-done.61, bf16[128,2048]{1,0:T(8,128)(2,1)} %copy-done.39, bf16[128,2048]{1,0:T(8,128)(2,1)} %copy-done.38, bf16[2048,4096]{1,0:T(8,128)(2,1)} %all-gather.5.cloned.1.call-done.refs_3_.refs_2_.refs_4_.refs_6_.refs_8_), custom_call_target="tpu_custom_call" | custom-call | flops 7008000000 | bytes 1048576 | tf_op jit(solution)/shard_map/moe_in/pallas_call | solution.py:597
  228.7 24.5 %moe_mid.2 = (bf16[64,2176]{1,0:T(8,128)(2,1)}, bf16[64,2176]{1,0:T(8,128)(2,1)}, bf16[128,2176]{1,0:T(8,128)(2,1)}, bf16[128,2176]{1,0:T(8,128)(2,1)}, bf16[64,...) custom-call(bf16[384,128]{1,0:T(8,128)(2,1)} %pad_slice_fusion.refs_, ...), custom_call_target="tpu_custom_call" | custom-call | flops 12816000000 | bytes 1048576 | tf_op jit(solution)/shard_map/moe_mid/pallas_call | solution.py:679
  256.0 5.5 turn_rows.1.xt
  266.7 35.8 %moe_mid.3 = (bf16[128,2176]{1,0:T(8,128)(2,1)}, bf16[128,2176]{1,0:T(8,128)(2,1)}, bf16[128,2176]{1,0:T(8,128)(2,1)}, bf16[128,2176]{1,0:T(8,128)(2,1)}, bf16[1...) custom-call(bf16[640,128]{1,0:T(8,128)(2,1)} %pad_slice_fusion.1.ref, ...), custom_call_target="tpu_custom_call" | custom-call | flops 18959998976 | bytes 1048576 | tf_op jit(solution)/shard_map/moe_mid/pallas_call | solution.py:679
  308.6 15.3 %out_grad.1 = bf16[16,128,2048]{2,1,0:T(8,128)(2,1)} custom-call(bf16[384,2048]{1,0:T(8,128)(2,1)} %get-tuple-element.201.refs_0_, bf16[640,2048]{1,0:T(8,128)(2,1)} %get-tuple-element.202.refs_1_, bf16[64,2048]{1,0:T(8,128)(2,1)} %copy-done.62, bf16[64,2048]{1,0:T(8,128)(2,1)} %copy-done.63, bf16[128,2048]{1,0:T(8,128)(2,1)} %collective-permute-done.29.refs_3_.refs_4_, ...), custom_call_target="tpu_custom_call" | custom-call | flops 7200000000 | bytes 1048576 | tf_op jit(solution)/shard_map/out_grad/pallas_call | solution.py:818
  326.0 9.5 %collective-permute-done.37 = bf16[128,2176]{1,0:T(8,128)(2,1)S(1)} collective-permute-done((bf16[128,2176]{1,0:T(8,128)(2,1)}, bf16[128,2176]{1,0:T(8,128)(2,1)S(1)}, u32[]{:S(2)}, u32[]{:S(2)}) %collective-permute-start.37) | collective-permute-done | bytes 557088 | tf_op jit(solution)/shard_map/ppermute | solution.py:58
  338.9 9.8 %in_grad.4 = (bf16[2,8,2,512,128]{4,3,2,1,0:T(8,128)(2,1)}, bf16[2,8,2,512,128]{4,3,2,1,0:T(8,128)(2,1)}) custom-call(s32[4]{0:T(128)} %dynamic-slice_bitcast_fusion.places, bf16[2048,1024]{1,0:T(8,128)(2,1)} %turn_rows.1.xt, bf16[384,4096]{1,0:T(8,128)(2,1)} %get-tuple-element.206.refs_0_, bf16[640,4096]{1,0:T(8,128)(2,1)} %get-tuple-element.207.refs_1_), custom_call_target="tpu_custom_call" | custom-call | flops 5400000000 | bytes 1048576 | tf_op jit(solution)/shard_map/in_grad/pallas_call | solution.py:779
  358.5 10.0 %in_grad.5 = (bf16[2,8,2,512,128]{4,3,2,1,0:T(8,128)(2,1)}, bf16[2,8,2,512,128]{4,3,2,1,0:T(8,128)(2,1)}) custom-call(s32[4]{0:T(128)} %dynamic-slice_bitcast_fusion.places, bf16[2048,1024]{1,0:T(8,128)(2,1)} %turn_rows.1.xt, bf16[384,4096]{1,0:T(8,128)(2,1)} %get-tuple-element.206.refs_0_, ...), custom_call_target="tpu_custom_call", output_to_operand_aliasing={{0}: (4, {}), {1}: (5, {})} | custom-call | flops 5400000000 | bytes 1048576 | tf_op jit(solution)/shard_map/in_grad/pallas_call | solution.py:779
  370.7 9.7 %in_grad.6 = (bf16[2,8,2,512,128]{4,3,2,1,0:T(8,128)(2,1)}, bf16[2,8,2,512,128]{4,3,2,1,0:T(8,128)(2,1)}) custom-call(s32[4]{0:T(128)} %dynamic-slice_bitcast_fusion.places, bf16[2048,1024]{1,0:T(8,128)(2,1)} %turn_rows.1.xt, bf16[384,4096]{1,0:T(8,128)(2,1)} %get-tuple-element.206.refs_0_, bf16[640,4096]{1,0:T(8,128)(2,1)} %get-tuple-element.207.refs_1_), custom_call_target="tpu_custom_call" | custom-call | flops 5400000000 | bytes 1048576 | tf_op jit(solution)/shard_map/in_grad/pallas_call | solution.py:779
  380.4 4.3 add_convert_fusion.1
  386.8 9.7 %in_grad.7 = (bf16[2,8,2,512,128]{4,3,2,1,0:T(8,128)(2,1)}, bf16[2,8,2,512,128]{4,3,2,1,0:T(8,128)(2,1)}) custom-call(s32[4]{0:T(128)} %dynamic-slice_bitcast_fusion.places, bf16[2048,1024]{1,0:T(8,128)(2,1)} %turn_rows.1.xt, bf16[384,4096]{1,0:T(8,128)(2,1)} %get-tuple-element.206.refs_0_, ...), custom_call_target="tpu_custom_call", output_to_operand_aliasing={{0}: (4, {}), {1}: (5, {})} | custom-call | flops 5400000000 | bytes 1048576 | tf_op jit(solution)/shard_map/in_grad/pallas_call | solution.py:779
  417.7 15.5 %attn_back.1 = (f32[1024,256]{1,0:T(8,128)}, f32[1024,256]{1,0:T(8,128)}, f32[1024,256]{1,0:T(8,128)}, bf16[1024,2048]{1,0:T(8,128)(2,1)}) custom-call(s32[8]{0:T(128)} %dynamic-slice_bitcast_fusion.1.refs_0_, bf16[64,2048]{1,0:T(8,128)(2,1)} %copy-done.64, bf16[64,2048]{1,0:T(8,128)(2,1)} %copy-done.65, bf16[128,2048]{1,0:T(8,128)(2,1)} %collective-permute-done.46.refs_3_, ...), custom_call_target="tpu_custom_call" | custom-call | flops 8400000000 | bytes 1048576 | tf_op jit(solution)/shard_map/attn_back/pallas_call | solution.py:432
  435.6 15.5 %proj_back.1 = (bf16[1024,768]{1,0:T(8,128)(2,1)}, f32[2,256]{1,0:T(2,128)}, f32[1,2048]{1,0:T(1,128)}, bf16[64,2048]{1,0:T(8,128)(2,1)}, bf16[64,2048]{1,0:T(8,...) custom-call(s32[8]{0:T(128)} %dynamic-slice_bitcast_fusion.1.refs_0_, ...), custom_call_target="tpu_custom_call" | custom-call | flops 7200000000 | bytes 1048576 | tf_op jit(solution)/shard_map/proj_back/pallas_call | solution.py:510
  456.7 4.3 collective-permute-done.57
  466.0 9.8 %attn_grad.1 = (bf16[2,3,512,256]{3,2,1,0:T(8,128)(2,1)}, bf16[2,3,512,256]{3,2,1,0:T(8,128)(2,1)}, bf16[2,256,512]{2,1,0:T(8,128)(2,1)}, bf16[2,256,512]{2,1,0:T(8,128)(2,1)}) custom-call(s32[4]{0:T(128)} %dynamic-slice_bitcast_fusion.places, bf16[1024,2048]{1,0:T(8,128)(2,1)} %get-tuple-element.242.refs_10_.xa.xb, ...), custom_call_target="tpu_custom_call" | custom-call | flops 3600000000 | bytes 1048576 | tf_op jit(solution)/shard_map/attn_grad/pallas_call | solution.py:549
  479.4 4.3 place.1
  487.1 5.4 finish.2.refs_0_
  519.9 6.1 %collective-permute-done.64 = bf16[128,2048]{1,0:T(8,128)(2,1)} collective-permute-done((bf16[128,2048]{1,0:T(8,128)(2,1)}, bf16[128,2048]{1,0:T(8,128)(2,1)}, u32[]{:S(2)}, u32[]{:S(2)}) %collective-permute-start.64) | collective-permute-done | bytes 524320 | tf_op jit(solution)/shard_map/ppermute | solution.py:58
  533.5 5.4 finish.3
  (449 shorter events, 204.0 us)
Async XLA Ops:
  7.2 58.8 %all-gather.9.cloned.1.call-start = ((), (), s32[]{:S(2)}) async-start(), calls=%async_computation.4 | async-start | bytes 5283840 | tf_op jit(solution)/shard_map/all_gather | solution.py:948
  12.0 151.3 %all-gather.5.cloned.1.call-start = ((), (), s32[]{:S(2)}) async-start(), calls=%async_computation.1 | async-start | bytes 20971520 | tf_op jit(solution)/shard_map/all_gather | solution.py:966
  12.3 15.7 %collective-permute-start.2 = (bf16[128,2176]{1,0:T(8,128)(2,1)S(1)}, bf16[128,2176]{1,0:T(8,128)(2,1)S(1)}, u32[]{:S(2)}, u32[]{:S(2)}) collective-permute-start(bf16[128,2176]{1,0:T(8,128)(2,1)S(1)} %fusion.12.refs_9_), channel_id=1, source_target_pairs={{0,1},{2,0},{4,2},{6,4},{7,6},{5,7},{3,5},{1,3},{8,9},{10,8},{12,1... | collective-permute-start | bytes 1671176 | tf_op jit(solution)/shard_map/ppermute | solution.py:58
  15.3 14.4 %collective-permute-start = (bf16[128,2176]{1,0:T(8,128)(2,1)S(1)}, bf16[128,2176]{1,0:T(8,128)(2,1)S(1)}, u32[]{:S(2)}, u32[]{:S(2)}) collective-permute-start(bf16[128,2176]{1,0:T(8,128)(2,1)S(1)} %fusion.12.refs_9_), channel_id=1, source_target_pairs={{0,2},{2,4},{4,6},{6,7},{7,5},{5,3},{3,1},{1,0},{8,10},{10,12},{12... | collective-permute-start | bytes 1671176 | tf_op jit(solution)/shard_map/ppermute | solution.py:58
  28.0 13.9 %collective-permute-start.3 = (bf16[128,2176]{1,0:T(8,128)(2,1)S(1)}, bf16[128,2176]{1,0:T(8,128)(2,1)S(1)}, u32[]{:S(2)}, u32[]{:S(2)}) collective-permute-start(bf16[128,2176]{1,0:T(8,128)(2,1)S(1)} %collective-permute-done.2.refs_7_), channel_id=1, source_target_pairs={{0,1},{2,0},{4,2},{6,4},{7,6},{5,7},{3,5},{1,3},{8,9},{10,8},{12,1... | collective-permute-start | bytes 1671176 | tf_op jit(solution)/shard_map/ppermute | solution.py:58
  43.1 179.5 %all-gather.7.cloned.1.call-start = ((), (), s32[]{:S(2)}) async-start(), calls=%async_computation.2 | async-start | bytes 10485760 | tf_op jit(solution)/shard_map/all_gather | solution.py:995
  63.9 16.6 %collective-permute-start.8 = (bf16[128,2048]{1,0:T(8,128)(2,1)S(1)}, bf16[128,2048]{1,0:T(8,128)(2,1)S(1)}, u32[]{:S(2)}, u32[]{:S(2)}) collective-permute-start(bf16[128,2048]{1,0:T(8,128)(2,1)S(1)} %copy-done.13), channel_id=1, source_target_pairs={{0,2},{2,4},{4,6},{6,7},{7,5},{5,3},{3,1},{1,0},{8,10},{10,12},{12... | collective-permute-start | bytes 1572872 | tf_op jit(solution)/shard_map/ppermute | solution.py:58
  65.5 15.0 %collective-permute-start.9 = (bf16[128,2048]{1,0:T(8,128)(2,1)S(1)}, bf16[128,2048]{1,0:T(8,128)(2,1)}, u32[]{:S(2)}, u32[]{:S(2)}) collective-permute-start(bf16[128,2048]{1,0:T(8,128)(2,1)S(1)} %copy-done.13), channel_id=1, source_target_pairs={{0,1},{2,0},{4,2},{6,4},{7,6},{5,7},{3,5},{1,3},{8,9},{10,8},{12,1... | collective-permute-start | bytes 1572872 | tf_op jit(solution)/shard_map/ppermute | solution.py:58
  102.9 376.4 %reduce-scatter.2.cloned.1.call-start = ((), (), s32[]{:S(2)}) async-start(), calls=%async_computation.3 | async-start | bytes 10485760 | tf_op jit(solution)/shard_map/reduce_scatter | solution.py:1038
  145.7 15.0 %collective-permute-start.22 = (bf16[128,2048]{1,0:T(8,128)(2,1)S(1)}, bf16[128,2048]{1,0:T(8,128)(2,1)S(1)}, u32[]{:S(2)}, u32[]{:S(2)}) collective-permute-start(bf16[128,2048]{1,0:T(8,128)(2,1)S(1)} %multiply_convert_fusion.refs_2_.refs_8_), channel_id=1, source_target_pairs={{0,1},{2,0},{4,2},{6,4},{7,6},{5,7},{3,5},{1,3},{8,9},{10,8},{12,1... | collective-permute-start | bytes 1572872 | tf_op jit(solution)/shard_map/ppermute | solution.py:58
  148.0 14.1 %collective-permute-start.20 = (bf16[128,2048]{1,0:T(8,128)(2,1)S(1)}, bf16[128,2048]{1,0:T(8,128)(2,1)S(1)}, u32[]{:S(2)}, u32[]{:S(2)}) collective-permute-start(bf16[128,2048]{1,0:T(8,128)(2,1)S(1)} %multiply_convert_fusion.refs_2_.refs_8_), channel_id=1, source_target_pairs={{0,2},{2,4},{4,6},{6,7},{7,5},{5,3},{3,1},{1,0},{8,10},{10,12},{12... | collective-permute-start | bytes 1572872 | tf_op jit(solution)/shard_map/ppermute | solution.py:58
  160.7 17.1 %collective-permute-start.23 = (bf16[128,2048]{1,0:T(8,128)(2,1)S(1)}, bf16[128,2048]{1,0:T(8,128)(2,1)}, u32[]{:S(2)}, u32[]{:S(2)}) collective-permute-start(bf16[128,2048]{1,0:T(8,128)(2,1)S(1)} %collective-permute-done.22.refs_0_.refs_6_), channel_id=1, source_target_pairs={{0,1},{2,0},{4,2},{6,4},{7,6},{5,7},{3,5},{1,3},{8,9},{10,8},{12,1... | collective-permute-start | bytes 1572872 | tf_op jit(solution)/shard_map/ppermute | solution.py:58
  162.1 15.7 %collective-permute-start.21 = (bf16[128,2048]{1,0:T(8,128)(2,1)S(1)}, bf16[128,2048]{1,0:T(8,128)(2,1)}, u32[]{:S(2)}, u32[]{:S(2)}) collective-permute-start(bf16[128,2048]{1,0:T(8,128)(2,1)S(1)} %collective-permute-done.20.refs_1_.refs_7_), channel_id=1, source_target_pairs={{0,2},{2,4},{4,6},{6,7},{7,5},{5,3},{3,1},{1,0},{8,10},{10,12},{12... | collective-permute-start | bytes 1572872 | tf_op jit(solution)/shard_map/ppermute | solution.py:58
  203.4 15.0 %collective-permute-start.28 = (bf16[128,2048]{1,0:T(8,128)(2,1)}, bf16[128,2048]{1,0:T(8,128)(2,1)S(1)}, u32[]{:S(2)}, u32[]{:S(2)}) collective-permute-start(bf16[128,2048]{1,0:T(8,128)(2,1)} %copy-done.55), channel_id=1, source_target_pairs={{0,2},{2,4},{4,6},{6,7},{7,5},{5,3},{3,1},{1,0},{8,10},{10,12},{12... | collective-permute-start | bytes 1572872 | tf_op jit(solution)/shard_map/ppermute | solution.py:58
  264.3 38.3 %collective-permute-start.34 = (bf16[192,2176]{1,0:T(8,128)(2,1)S(1)}, bf16[192,2176]{1,0:T(8,128)(2,1)S(1)}, u32[]{:S(2)}, u32[]{:S(2)}) collective-permute-start(bf16[192,2176]{1,0:T(8,128)(2,1)S(1)} %fusion.10), channel_id=1, source_target_pairs={{0,2},{2,4},{4,6},{6,7},{7,5},{5,3},{3,1},{1,0},{8,10},{10,12},{12... | collective-permute-start | bytes 2506760 | tf_op jit(solution)/shard_map/ppermute | solution.py:58
  266.2 38.4 %collective-permute-start.35 = (bf16[192,2176]{1,0:T(8,128)(2,1)S(1)}, bf16[192,2176]{1,0:T(8,128)(2,1)}, u32[]{:S(2)}, u32[]{:S(2)}) collective-permute-start(bf16[192,2176]{1,0:T(8,128)(2,1)S(1)} %fusion.11), channel_id=1, source_target_pairs={{0,1},{2,0},{4,2},{6,4},{7,6},{5,7},{3,5},{1,3},{8,9},{10,8},{12,1... | collective-permute-start | bytes 2506760 | tf_op jit(solution)/shard_map/ppermute | solution.py:58
  306.6 17.4 %collective-permute-start.36 = (bf16[128,2176]{1,0:T(8,128)(2,1)}, bf16[128,2176]{1,0:T(8,128)(2,1)}, u32[]{:S(2)}, u32[]{:S(2)}) collective-permute-start(bf16[128,2176]{1,0:T(8,128)(2,1)} %add_convert_fusion.6), channel_id=1, source_target_pairs={{0,2},{2,4},{4,6},{6,7},{7,5},{5,3},{3,1},{1,0},{8,10},{10,12},{12... | collective-permute-start | bytes 1671176 | tf_op jit(solution)/shard_map/ppermute | solution.py:58
  335.6 15.4 %collective-permute-start.38 = (bf16[128,2176]{1,0:T(8,128)(2,1)}, bf16[128,2176]{1,0:T(8,128)(2,1)S(1)}, u32[]{:S(2)}, u32[]{:S(2)}) collective-permute-start(bf16[128,2176]{1,0:T(8,128)(2,1)} %add_convert_fusion.4), channel_id=1, source_target_pairs={{0,2},{2,4},{4,6},{6,7},{7,5},{5,3},{3,1},{1,0},{8,10},{10,12},{12... | collective-permute-start | bytes 1671176 | tf_op jit(solution)/shard_map/ppermute | solution.py:58
  337.2 15.3 %collective-permute-start.39 = (bf16[128,2176]{1,0:T(8,128)(2,1)S(1)}, bf16[128,2176]{1,0:T(8,128)(2,1)}, u32[]{:S(2)}, u32[]{:S(2)}) collective-permute-start(bf16[128,2176]{1,0:T(8,128)(2,1)S(1)} %add_convert_fusion.3), channel_id=1, source_target_pairs={{0,1},{2,0},{4,2},{6,4},{7,6},{5,7},{3,5},{1,3},{8,9},{10,8},{12,1... | collective-permute-start | bytes 1671176 | tf_op jit(solution)/shard_map/ppermute | solution.py:58
  368.6 16.1 %collective-permute-start.42 = (bf16[128,2048]{1,0:T(8,128)(2,1)}, bf16[128,2048]{1,0:T(8,128)(2,1)S(1)}, u32[]{:S(2)}, u32[]{:S(2)}) collective-permute-start(bf16[128,2048]{1,0:T(8,128)(2,1)} %collective-permute-done.40.refs_8_), channel_id=1, source_target_pairs={{0,2},{2,4},{4,6},{6,7},{7,5},{5,3},{3,1},{1,0},{8,10},{10,12},{12... | collective-permute-start | bytes 1572872 | tf_op jit(solution)/shard_map/ppermute | solution.py:58
  369.9 14.8 %collective-permute-start.43 = (bf16[128,2048]{1,0:T(8,128)(2,1)}, bf16[128,2048]{1,0:T(8,128)(2,1)}, u32[]{:S(2)}, u32[]{:S(2)}) collective-permute-start(bf16[128,2048]{1,0:T(8,128)(2,1)} %collective-permute-done.41.refs_7_), channel_id=1, source_target_pairs={{0,1},{2,0},{4,2},{6,4},{7,6},{5,7},{3,5},{1,3},{8,9},{10,8},{12,1... | collective-permute-start | bytes 1572872 | tf_op jit(solution)/shard_map/ppermute | solution.py:58
  403.6 49.0 %collective-permute-start.54 = (bf16[1,8,2,512,128]{4,3,2,1,0:T(8,128)(2,1)}, bf16[1,8,2,512,128]{4,3,2,1,0:T(8,128)(2,1)}, u32[]{:S(2)}, u32[]{:S(2)}) collective-permute-start(bf16[1,8,2,512,128]{4,3,2,1,0:T(8,128)(2,1)} %add_convert_fusion.1), channel_id=1, source_target_pairs={{0,16},{8,24},{16,0},{24,8},{1,17},{9,25},{17,1},{25,9},{2,18},{10... | collective-permute-start | bytes 6291464 | tf_op jit(solution)/shard_map/ppermute | solution.py:145
  415.5 17.8 %collective-permute-start.50 = (bf16[128,2048]{1,0:T(8,128)(2,1)}, bf16[128,2048]{1,0:T(8,128)(2,1)S(1)}, u32[]{:S(2)}, u32[]{:S(2)}) collective-permute-start(bf16[128,2048]{1,0:T(8,128)(2,1)} %add_convert_fusion.21), channel_id=1, source_target_pairs={{0,2},{2,4},{4,6},{6,7},{7,5},{5,3},{3,1},{1,0},{8,10},{10,12},{12... | collective-permute-start | bytes 1572872 | tf_op jit(solution)/shard_map/ppermute | solution.py:58
  415.8 18.0 %collective-permute-start.52 = (bf16[128,2048]{1,0:T(8,128)(2,1)}, bf16[128,2048]{1,0:T(8,128)(2,1)S(1)}, u32[]{:S(2)}, u32[]{:S(2)}) collective-permute-start(bf16[128,2048]{1,0:T(8,128)(2,1)} %add_convert_fusion.20), channel_id=1, source_target_pairs={{0,1},{2,0},{4,2},{6,4},{7,6},{5,7},{3,5},{1,3},{8,9},{10,8},{12,1... | collective-permute-start | bytes 1572872 | tf_op jit(solution)/shard_map/ppermute | solution.py:58
  433.4 19.2 %collective-permute-start.51 = (bf16[128,2048]{1,0:T(8,128)(2,1)S(1)}, bf16[128,2048]{1,0:T(8,128)(2,1)S(1)}, u32[]{:S(2)}, u32[]{:S(2)}) collective-permute-start(bf16[128,2048]{1,0:T(8,128)(2,1)S(1)} %add_convert_fusion.19), channel_id=1, source_target_pairs={{0,2},{2,4},{4,6},{6,7},{7,5},{5,3},{3,1},{1,0},{8,10},{10,12},{12... | collective-permute-start | bytes 1572872 | tf_op jit(solution)/shard_map/ppermute | solution.py:58
  434.4 18.2 %collective-permute-start.53 = (bf16[128,2048]{1,0:T(8,128)(2,1)S(1)}, bf16[128,2048]{1,0:T(8,128)(2,1)}, u32[]{:S(2)}, u32[]{:S(2)}) collective-permute-start(bf16[128,2048]{1,0:T(8,128)(2,1)S(1)} %add_convert_fusion.17), channel_id=1, source_target_pairs={{0,1},{2,0},{4,2},{6,4},{7,6},{5,7},{3,5},{1,3},{8,9},{10,8},{12,1... | collective-permute-start | bytes 1572872 | tf_op jit(solution)/shard_map/ppermute | solution.py:58
  454.8 56.6 %collective-permute-start.63 = (bf16[1,8,2,512,128]{4,3,2,1,0:T(8,128)(2,1)}, bf16[1,8,2,512,128]{4,3,2,1,0:T(8,128)(2,1)}, u32[]{:S(2)}, u32[]{:S(2)}) collective-permute-start(bf16[1,8,2,512,128]{4,3,2,1,0:T(8,128)(2,1)} %add_convert_fusion), channel_id=1, source_target_pairs={{0,16},{8,24},{16,0},{24,8},{1,17},{9,25},{17,1},{25,9},{2,18},{10... | collective-permute-start | bytes 6291464 | tf_op jit(solution)/shard_map/ppermute | solution.py:145
  486.6 15.3 %collective-permute-start.61 = (bf16[2,3,512,256]{3,2,1,0:T(8,128)(2,1)}, bf16[2,3,512,256]{3,2,1,0:T(8,128)(2,1)}, u32[]{:S(2)}, u32[]{:S(2)}) collective-permute-start(bf16[2,3,512,256]{3,2,1,0:T(8,128)(2,1)} %get-tuple-element.265), channel_id=1, source_target_pairs={{0,8},{8,0},{16,24},{24,16},{1,9},{9,1},{17,25},{25,17},{2,10},{10... | collective-permute-start | bytes 4718600 | tf_op jit(solution)/shard_map/ppermute | solution.py:145
  511.4 14.6 %collective-permute-start.64 = (bf16[128,2048]{1,0:T(8,128)(2,1)}, bf16[128,2048]{1,0:T(8,128)(2,1)}, u32[]{:S(2)}, u32[]{:S(2)}) collective-permute-start(bf16[128,2048]{1,0:T(8,128)(2,1)} %add_convert_fusion.11), channel_id=1, source_target_pairs={{0,2},{2,4},{4,6},{6,7},{7,5},{5,3},{3,1},{1,0},{8,10},{10,12},{12... | collective-permute-start | bytes 1572872 | tf_op jit(solution)/shard_map/ppermute | solution.py:58
  512.8 14.4 %collective-permute-start.65 = (bf16[128,2048]{1,0:T(8,128)(2,1)}, bf16[128,2048]{1,0:T(8,128)(2,1)}, u32[]{:S(2)}, u32[]{:S(2)}) collective-permute-start(bf16[128,2048]{1,0:T(8,128)(2,1)} %add_convert_fusion.10), channel_id=1, source_target_pairs={{0,1},{2,0},{4,2},{6,4},{7,6},{5,7},{3,5},{1,3},{8,9},{10,8},{12,1... | collective-permute-start | bytes 1572872 | tf_op jit(solution)/shard_map/ppermute | solution.py:58
  516.6 22.3 %collective-permute-start.69 = (bf16[1,256,512]{2,1,0:T(8,128)(2,1)S(1)}, bf16[1,256,512]{2,1,0:T(8,128)(2,1)}, u32[]{:S(2)}, u32[]{:S(2)}) collective-permute-start(bf16[1,256,512]{2,1,0:T(8,128)(2,1)S(1)} %add_convert_fusion.28), channel_id=1, source_target_pairs={{0,16},{8,24},{16,0},{24,8},{1,17},{9,25},{17,1},{25,9},{2,18},{10... | collective-permute-start | bytes 786440 | tf_op jit(solution)/shard_map/ppermute | solution.py:145
  517.7 24.3 %collective-permute-start.68 = (bf16[1,3,512,256]{3,2,1,0:T(8,128)(2,1)}, bf16[1,3,512,256]{3,2,1,0:T(8,128)(2,1)}, u32[]{:S(2)}, u32[]{:S(2)}) collective-permute-start(bf16[1,3,512,256]{3,2,1,0:T(8,128)(2,1)} %add_convert_fusion.2), channel_id=1, source_target_pairs={{0,16},{8,24},{16,0},{24,8},{1,17},{9,25},{17,1},{25,9},{2,18},{10... | collective-permute-start | bytes 2359304 | tf_op jit(solution)/shard_map/ppermute | solution.py:145
  (116 other events, 1172.6 us)
Sparse Core Ops, SparseCore 0:
  12.1 37.3 all-gather.8
  51.6 105.9 all-gather.4
  159.2 58.2 all-gather.6
  339.0 70.5 reduce-scatter.1

commit v5 on v4

--- a/solution.py
+++ b/solution.py
@@ -578,15 +578,17 @@
     return starts
 
 
+def held(piece):
+    return pl.BlockSpec(piece.shape, lambda s: (0, 0))
+
+
+def stacked(pieces):
+    return jnp.concatenate([piece[...] for piece in pieces], axis=0)
+
+
 def moe_in_body(count, *refs):
-    xp, gu, out, xs, sems = refs[:count], *refs[count:]
-
-    @pl.when(pl.program_id(0) == 0)
-    def _():
-        for copy in fetch(xp, xs, sems, 0, flat_rows(xp)):
-            copy.wait()
-
-    out[...] = dot(xs[...], gu[...]).astype(bf16)
+    xp, gu, out = refs[:count], *refs[count:]
+    out[...] = dot(stacked(xp), gu[...]).astype(bf16)
 
 
 def moe_in(xp, gate_up, group=4):
@@ -597,10 +599,9 @@
     return pl.pallas_call(
         functools.partial(moe_in_body, count),
         grid=(columns // wide,),
-        in_specs=[ANY] * count + [pl.BlockSpec((d, wide), lambda s: (0, s))],
+        in_specs=[held(p) for p in xp] + [pl.BlockSpec((d, wide), lambda s: (0, s))],
         out_specs=pl.BlockSpec((rows, wide), lambda s: (0, s)),
         out_shape=shape((rows, columns), bf16),
-        scratch_shapes=[pltpu.VMEM((rows, d), bf16), pltpu.SemaphoreType.DMA((count,))],
         compiler_params=pltpu.CompilerParams(vmem_limit_bytes=VMEM_BYTES),
         cost_estimate=cost(rows * 0.02 + 4),
         name="moe_in",
@@ -623,14 +624,11 @@
 
     @pl.when(step == 0)
     def _():
-        copies = fetch(cp, cs, sems, 0, flat_rows(cp))
         d_acc[...] = jnp.zeros_like(d_acc)
         m_acc[...] = jnp.zeros_like(m_acc)
         gg[...] = jnp.zeros_like(gg)
-        for copy in copies:
-            copy.wait()
-
-    d_hid = dot_nt(cs[...], dn_w[...])
+
+    d_hid = dot_nt(stacked(cp), dn_w[...])
     at = 0
     for gu in gus:
         rows = gu.shape[0]
@@ -680,7 +678,7 @@
         functools.partial(moe_mid_body, group, steps, len(gus), count),
         grid=(steps,),
         in_specs=[pl.BlockSpec((rows, LANES), lambda s: (0, 0))]
-        + [ANY] * count
+        + [held(p) for p in cp]
         + [pl.BlockSpec((g.shape[0], 2 * half), lambda s: (0, s)) for g in gus]
         + [
             pl.BlockSpec((d, 2 * half), lambda s: (0, s)),
@@ -885,7 +883,7 @@
             out[:, at : at + fw] = w[i, g]
 
 
-def pack(gate_up, group=2):
+def pack(gate_up, group=4):
     experts, _, depth, fw = gate_up.shape
     return pl.pallas_call(
         pack_body,

time: 566 us -> 564 us (level)
  Pallas kernels: 243 us -> 235 us
  transfers between devices with their start and end apart: 79 -> 79, of which waited for: 42 -> 42; matrix products, arithmetic and copies ran while one was open for 11% -> 11% of each run, Pallas kernels for 39% -> 38%
where the time goes in v5:
time: 564 us; the launch traced here: 554 us
  Pallas kernels  235 us (42%)
  waiting for transfers between devices  141 us (25%)
  starting transfers between devices  84.2 us (15%)
  other arithmetic  52.4 us (9%)
  local copies, waits for them, and re-layouts  25.5 us (5%)
  between operations  15.3 us (3%)
    ppermute x62, waiting for transfers between devices, ring_step(): return lax.ppermute(value, 'tensor', pairs)  138 us
    ppermute x62, starting transfers between devices, ring_step(): return lax.ppermute(value, 'tensor', pairs)  72.5 us
    pallas_call x2, Pallas kernels, moe_mid(): pl.pallas_call(functools.partial(moe_mid_body, group, steps, len(gus), co...  58.1 us
    pallas_call x4, Pallas kernels, in_grad(): pl.pallas_call(functools.partial(in_grad_body, n, group, sets), grid=(num...  39 us
    pallas_call x3, Pallas kernels, moe_in(): pl.pallas_call(functools.partial(moe_in_body, count), grid=(columns // wi...  34.5 us
    pallas_call x1, Pallas kernels, proj_back(): pl.pallas_call(functools.partial(proj_back_body, count, steps), grid=(ste...  15.5 us
    pallas_call x1, Pallas kernels, attn_back(): pl.pallas_call(functools.partial(attn_back_body, count, min(256, length))...  15.5 us
    pallas_call x1, Pallas kernels, out_grad(): pl.pallas_call(functools.partial(out_grad_body, group, count, len(hws)),...  15.3 us
  transfers between devices with their start and end apart: 79, of which 42 were waited for; matrix products, arithmetic and copies ran while one was open for 11% of the time, Pallas kernels for 38%

profile of v5, /device:TPU:0, one launch (start us, length us, event | category | flops | bytes accessed | tf_op | source)
XLA Modules:
  0.0 553.9 jit_solution(3516502357972211702)
XLA Ops:
  15.4 12.6 %collective-permute-done.2.refs_7_ = bf16[128,2176]{1,0:T(8,128)(2,1)S(1)} collective-permute-done((bf16[128,2176]{1,0:T(8,128)(2,1)S(1)}, bf16[128,2176]{1,0:T(8,128)(2,1)S(1)}, u32[]{:S(2)}, u32[]{:S(2)}) %collective-permute-start.2) | collective-permute-done | bytes 557088 | tf_op jit(solution)/shard_map/ppermute | solution.py:58
  30.0 5.1 pack.1
  35.2 6.7 %collective-permute-done.3.refs_5_ = bf16[128,2176]{1,0:T(8,128)(2,1)S(1)} collective-permute-done((bf16[128,2176]{1,0:T(8,128)(2,1)S(1)}, bf16[128,2176]{1,0:T(8,128)(2,1)S(1)}, u32[]{:S(2)}, u32[]{:S(2)}) %collective-permute-start.3) | collective-permute-done | bytes 557088 | tf_op jit(solution)/shard_map/ppermute | solution.py:58
  45.2 10.9 %collective-permute-done.4.refs_4_ = bf16[128,2176]{1,0:T(8,128)(2,1)S(1)} collective-permute-done((bf16[128,2176]{1,0:T(8,128)(2,1)}, bf16[128,2176]{1,0:T(8,128)(2,1)S(1)}, u32[]{:S(2)}, u32[]{:S(2)}) %collective-permute-start.4) | collective-permute-done | bytes 557088 | tf_op jit(solution)/shard_map/ppermute | solution.py:58
  69.2 11.3 %attn_proj.1 = (bf16[1024,256]{1,0:T(8,128)(2,1)}, bf16[1024,256]{1,0:T(8,128)(2,1)}, bf16[1024,256]{1,0:T(8,128)(2,1)}, f32[1024,256]{1,0:T(8,128)}, f32[1024,256]{1,0:T(8,128)}, /*index=5*/bf16[1024,2048]{1,0:T(8,128)(2,1)}) custom-call(s32[8]{0:T(128)} %dynamic-slice_bitcast_fusion.1.refs_0_, bf16[64,2176]{1,0:T(8,128)(2,1)} %copy-done.42, ...), custom_call_target="tpu_custom_call" | custom-call | flops 6000000000 | bytes 1048576 | tf_op jit(solution)/shard_map/attn_proj/pallas_call | solution.py:312
  82.6 10.4 %attn_core.1 = (bf16[1024,256]{1,0:T(8,128)(2,1)}, f32[2,1024,1]{2,1,0:T(8,128)}, bf16[64,2048]{1,0:T(8,128)(2,1)}, bf16[64,2048]{1,0:T(8,128)(2,1)}, bf16[128,2...) custom-call(s32[8]{0:T(128)} %dynamic-slice_bitcast_fusion.1.refs_0_, ...), custom_call_target="tpu_custom_call" | custom-call | flops 6000000000 | bytes 1048576 | tf_op jit(solution)/shard_map/attn_core/pallas_call | solution.py:371
  95.4 4.6 collective-permute-done.12
  106.0 8.9 %collective-permute-done.17 = bf16[128,2048]{1,0:T(8,128)(2,1)S(1)} collective-permute-done((bf16[128,2048]{1,0:T(8,128)(2,1)S(1)}, bf16[128,2048]{1,0:T(8,128)(2,1)S(1)}, u32[]{:S(2)}, u32[]{:S(2)}) %collective-permute-start.17) | collective-permute-done | bytes 524320 | tf_op jit(solution)/shard_map/ppermute | solution.py:58
  118.9 9.0 %collective-permute-done.18 = bf16[128,2048]{1,0:T(8,128)(2,1)S(1)} collective-permute-done((bf16[128,2048]{1,0:T(8,128)(2,1)S(1)}, bf16[128,2048]{1,0:T(8,128)(2,1)S(1)}, u32[]{:S(2)}, u32[]{:S(2)}) %collective-permute-start.18) | collective-permute-done | bytes 524320 | tf_op jit(solution)/shard_map/ppermute | solution.py:58
  133.9 6.6 %collective-permute-done.19 = bf16[128,2048]{1,0:T(8,128)(2,1)S(1)} collective-permute-done((bf16[128,2048]{1,0:T(8,128)(2,1)S(1)}, bf16[128,2048]{1,0:T(8,128)(2,1)S(1)}, u32[]{:S(2)}, u32[]{:S(2)}) %collective-permute-start.19) | collective-permute-done | bytes 524320 | tf_op jit(solution)/shard_map/ppermute | solution.py:58
  149.3 11.4 %collective-permute-done.22.refs_0_.refs_6_ = bf16[128,2048]{1,0:T(8,128)(2,1)S(1)} collective-permute-done((bf16[128,2048]{1,0:T(8,128)(2,1)S(1)}, bf16[128,2048]{1,0:T(8,128)(2,1)S(1)}, u32[]{:S(2)}, u32[]{:S(2)}) %collective-permute-start.22) | collective-permute-done | bytes 524320 | tf_op jit(solution)/shard_map/ppermute | solution.py:58
  163.3 13.0 %moe_in.3.refs_7_ = bf16[384,4096]{1,0:T(8,128)(2,1)} custom-call(bf16[128,2048]{1,0:T(8,128)(2,1)} %copy-done.57, bf16[128,2048]{1,0:T(8,128)(2,1)} %copy-done.58, bf16[128,2048]{1,0:T(8,128)(2,1)} %copy-done.28, bf16[2048,4096]{1,0:T(8,128)(2,1)} %all-gather.5.cloned.1.call-done.refs_3_.refs_2_.refs_4_.refs_6_.refs_8_), custom_call_target="tpu_custom_call" | custom-call | flops 7008000000 | bytes 1048576 | tf_op jit(solution)/shard_map/moe_in/pallas_call | solution.py:599
  179.2 9.8 %moe_in.4.refs_6_ = bf16[256,4096]{1,0:T(8,128)(2,1)} custom-call(bf16[128,2048]{1,0:T(8,128)(2,1)} %collective-permute-done.23.refs_0_.refs_4_, bf16[128,2048]{1,0:T(8,128)(2,1)} %collective-permute-done.21.refs_1_.refs_5_, bf16[2048,4096]{1,0:T(8,128)(2,1)} %all-gather.5.cloned.1.call-done.refs_3_.refs_2_.refs_4_.refs_6_.refs_8_), custom_call_target="tpu_custom_call" | custom-call | flops 5472000000 | bytes 1048576 | tf_op jit(solution)/shard_map/moe_in/pallas_call | solution.py:599
  204.7 11.7 %moe_in.5.refs_5_ = bf16[384,4096]{1,0:T(8,128)(2,1)} custom-call(bf16[64,2048]{1,0:T(8,128)(2,1)} %copy-done.60, bf16[64,2048]{1,0:T(8,128)(2,1)} %copy-done.61, bf16[128,2048]{1,0:T(8,128)(2,1)} %copy-done.39, bf16[128,2048]{1,0:T(8,128)(2,1)} %copy-done.38, bf16[2048,4096]{1,0:T(8,128)(2,1)} %all-gather.5.cloned.1.call-done.refs_3_.refs_2_.refs_4_.refs_6_.refs_8_), custom_call_target="tpu_custom_call" | custom-call | flops 7008000000 | bytes 1048576 | tf_op jit(solution)/shard_map/moe_in/pallas_call | solution.py:599
  226.2 23.6 %moe_mid.2 = (bf16[64,2176]{1,0:T(8,128)(2,1)}, bf16[64,2176]{1,0:T(8,128)(2,1)}, bf16[128,2176]{1,0:T(8,128)(2,1)}, bf16[128,2176]{1,0:T(8,128)(2,1)}, bf16[64,...) custom-call(bf16[384,128]{1,0:T(8,128)(2,1)} %pad_slice_fusion.refs_, ...), custom_call_target="tpu_custom_call" | custom-call | flops 12816000000 | bytes 1048576 | tf_op jit(solution)/shard_map/moe_mid/pallas_call | solution.py:677
  252.6 5.5 %turn_rows.1.xt = bf16[2048,1024]{1,0:T(8,128)(2,1)} custom-call(bf16[64,2048]{1,0:T(8,128)(2,1)} %copy-done.60, bf16[64,2048]{1,0:T(8,128)(2,1)} %copy-done.61, bf16[128,2048]{1,0:T(8,128)(2,1)} %copy-done.39, bf16[128,2048]{1,0:T(8,128)(2,1)} %copy-done.38, bf16[128,2048]{1,0:T(8,128)(2,1)} %collective-permute-done.23.refs_0_.refs_4_, ...), custom_call_target="tpu_custom_call" | custom-call | flops 2400000000 | bytes 1048576 | tf_op jit(solution)/shard_map/turn_rows/pallas_call | solution.py:727
  263.5 34.5 %moe_mid.3 = (bf16[128,2176]{1,0:T(8,128)(2,1)}, bf16[128,2176]{1,0:T(8,128)(2,1)}, bf16[128,2176]{1,0:T(8,128)(2,1)}, bf16[128,2176]{1,0:T(8,128)(2,1)}, bf16[1...) custom-call(bf16[640,128]{1,0:T(8,128)(2,1)} %pad_slice_fusion.1.ref, ...), custom_call_target="tpu_custom_call" | custom-call | flops 18959998976 | bytes 1048576 | tf_op jit(solution)/shard_map/moe_mid/pallas_call | solution.py:677
  303.4 15.3 %out_grad.1 = bf16[16,128,2048]{2,1,0:T(8,128)(2,1)} custom-call(bf16[384,2048]{1,0:T(8,128)(2,1)} %get-tuple-element.201.refs_0_, bf16[640,2048]{1,0:T(8,128)(2,1)} %get-tuple-element.202.refs_1_, bf16[64,2048]{1,0:T(8,128)(2,1)} %copy-done.62, bf16[64,2048]{1,0:T(8,128)(2,1)} %copy-done.63, bf16[128,2048]{1,0:T(8,128)(2,1)} %collective-permute-done.29.refs_3_.refs_4_, ...), custom_call_target="tpu_custom_call" | custom-call | flops 7200000000 | bytes 1048576 | tf_op jit(solution)/shard_map/out_grad/pallas_call | solution.py:816
  321.4 11.9 %collective-permute-done.37 = bf16[128,2176]{1,0:T(8,128)(2,1)S(1)} collective-permute-done((bf16[128,2176]{1,0:T(8,128)(2,1)}, bf16[128,2176]{1,0:T(8,128)(2,1)S(1)}, u32[]{:S(2)}, u32[]{:S(2)}) %collective-permute-start.37) | collective-permute-done | bytes 557088 | tf_op jit(solution)/shard_map/ppermute | solution.py:58
  336.7 9.8 %in_grad.4 = (bf16[2,8,2,512,128]{4,3,2,1,0:T(8,128)(2,1)}, bf16[2,8,2,512,128]{4,3,2,1,0:T(8,128)(2,1)}) custom-call(s32[4]{0:T(128)} %dynamic-slice_bitcast_fusion.places, bf16[2048,1024]{1,0:T(8,128)(2,1)} %turn_rows.1.xt, bf16[384,4096]{1,0:T(8,128)(2,1)} %get-tuple-element.206.refs_0_, bf16[640,4096]{1,0:T(8,128)(2,1)} %get-tuple-element.207.refs_1_), custom_call_target="tpu_custom_call" | custom-call | flops 5400000000 | bytes 1048576 | tf_op jit(solution)/shard_map/in_grad/pallas_call | solution.py:777
  354.8 9.7 %in_grad.5 = (bf16[2,8,2,512,128]{4,3,2,1,0:T(8,128)(2,1)}, bf16[2,8,2,512,128]{4,3,2,1,0:T(8,128)(2,1)}) custom-call(s32[4]{0:T(128)} %dynamic-slice_bitcast_fusion.places, bf16[2048,1024]{1,0:T(8,128)(2,1)} %turn_rows.1.xt, bf16[384,4096]{1,0:T(8,128)(2,1)} %get-tuple-element.206.refs_0_, ...), custom_call_target="tpu_custom_call", output_to_operand_aliasing={{0}: (4, {}), {1}: (5, {})} | custom-call | flops 5400000000 | bytes 1048576 | tf_op jit(solution)/shard_map/in_grad/pallas_call | solution.py:777
  366.7 9.8 %in_grad.6 = (bf16[2,8,2,512,128]{4,3,2,1,0:T(8,128)(2,1)}, bf16[2,8,2,512,128]{4,3,2,1,0:T(8,128)(2,1)}) custom-call(s32[4]{0:T(128)} %dynamic-slice_bitcast_fusion.places, bf16[2048,1024]{1,0:T(8,128)(2,1)} %turn_rows.1.xt, bf16[384,4096]{1,0:T(8,128)(2,1)} %get-tuple-element.206.refs_0_, bf16[640,4096]{1,0:T(8,128)(2,1)} %get-tuple-element.207.refs_1_), custom_call_target="tpu_custom_call" | custom-call | flops 5400000000 | bytes 1048576 | tf_op jit(solution)/shard_map/in_grad/pallas_call | solution.py:777
  382.7 9.8 %in_grad.7 = (bf16[2,8,2,512,128]{4,3,2,1,0:T(8,128)(2,1)}, bf16[2,8,2,512,128]{4,3,2,1,0:T(8,128)(2,1)}) custom-call(s32[4]{0:T(128)} %dynamic-slice_bitcast_fusion.places, bf16[2048,1024]{1,0:T(8,128)(2,1)} %turn_rows.1.xt, bf16[384,4096]{1,0:T(8,128)(2,1)} %get-tuple-element.206.refs_0_, ...), custom_call_target="tpu_custom_call", output_to_operand_aliasing={{0}: (4, {}), {1}: (5, {})} | custom-call | flops 5400000000 | bytes 1048576 | tf_op jit(solution)/shard_map/in_grad/pallas_call | solution.py:777
  405.6 4.1 add_convert_fusion
  414.3 15.5 %attn_back.1 = (f32[1024,256]{1,0:T(8,128)}, f32[1024,256]{1,0:T(8,128)}, f32[1024,256]{1,0:T(8,128)}, bf16[1024,2048]{1,0:T(8,128)(2,1)}) custom-call(s32[8]{0:T(128)} %dynamic-slice_bitcast_fusion.1.refs_0_, bf16[64,2048]{1,0:T(8,128)(2,1)} %copy-done.64, bf16[64,2048]{1,0:T(8,128)(2,1)} %copy-done.65, bf16[128,2048]{1,0:T(8,128)(2,1)} %collective-permute-done.46.refs_3_, ...), custom_call_target="tpu_custom_call" | custom-call | flops 8400000000 | bytes 1048576 | tf_op jit(solution)/shard_map/attn_back/pallas_call | solution.py:432
  432.7 15.5 %proj_back.1 = (bf16[1024,768]{1,0:T(8,128)(2,1)}, f32[2,256]{1,0:T(2,128)}, f32[1,2048]{1,0:T(1,128)}, bf16[64,2048]{1,0:T(8,128)(2,1)}, bf16[64,2048]{1,0:T(8,...) custom-call(s32[8]{0:T(128)} %dynamic-slice_bitcast_fusion.1.refs_0_, ...), custom_call_target="tpu_custom_call" | custom-call | flops 7200000000 | bytes 1048576 | tf_op jit(solution)/shard_map/proj_back/pallas_call | solution.py:510
  454.4 4.4 collective-permute-done.57
  463.8 9.8 %attn_grad.1 = (bf16[2,3,512,256]{3,2,1,0:T(8,128)(2,1)}, bf16[2,3,512,256]{3,2,1,0:T(8,128)(2,1)}, bf16[2,256,512]{2,1,0:T(8,128)(2,1)}, bf16[2,256,512]{2,1,0:T(8,128)(2,1)}) custom-call(s32[4]{0:T(128)} %dynamic-slice_bitcast_fusion.places, bf16[1024,2048]{1,0:T(8,128)(2,1)} %get-tuple-element.242.refs_10_.xa.xb, ...), custom_call_target="tpu_custom_call" | custom-call | flops 3600000000 | bytes 1048576 | tf_op jit(solution)/shard_map/attn_grad/pallas_call | solution.py:549
  477.1 4.3 place.1
  484.8 5.4 finish.2.refs_0_
  517.8 6.2 %collective-permute-done.64 = bf16[128,2048]{1,0:T(8,128)(2,1)} collective-permute-done((bf16[128,2048]{1,0:T(8,128)(2,1)}, bf16[128,2048]{1,0:T(8,128)(2,1)}, u32[]{:S(2)}, u32[]{:S(2)}) %collective-permute-start.64) | collective-permute-done | bytes 524320 | tf_op jit(solution)/shard_map/ppermute | solution.py:58
  531.5 5.4 finish.3
  (449 shorter events, 206.2 us)
Async XLA Ops:
  7.2 58.8 %all-gather.9.cloned.1.call-start = ((), (), s32[]{:S(2)}) async-start(), calls=%async_computation.4 | async-start | bytes 5283840 | tf_op jit(solution)/shard_map/all_gather | solution.py:946
  12.0 151.3 %all-gather.5.cloned.1.call-start = ((), (), s32[]{:S(2)}) async-start(), calls=%async_computation.1 | async-start | bytes 20971520 | tf_op jit(solution)/shard_map/all_gather | solution.py:964
  12.3 15.7 %collective-permute-start.2 = (bf16[128,2176]{1,0:T(8,128)(2,1)S(1)}, bf16[128,2176]{1,0:T(8,128)(2,1)S(1)}, u32[]{:S(2)}, u32[]{:S(2)}) collective-permute-start(bf16[128,2176]{1,0:T(8,128)(2,1)S(1)} %fusion.12.refs_9_), channel_id=1, source_target_pairs={{0,1},{2,0},{4,2},{6,4},{7,6},{5,7},{3,5},{1,3},{8,9},{10,8},{12,1... | collective-permute-start | bytes 1671176 | tf_op jit(solution)/shard_map/ppermute | solution.py:58
  15.3 14.4 %collective-permute-start = (bf16[128,2176]{1,0:T(8,128)(2,1)S(1)}, bf16[128,2176]{1,0:T(8,128)(2,1)S(1)}, u32[]{:S(2)}, u32[]{:S(2)}) collective-permute-start(bf16[128,2176]{1,0:T(8,128)(2,1)S(1)} %fusion.12.refs_9_), channel_id=1, source_target_pairs={{0,2},{2,4},{4,6},{6,7},{7,5},{5,3},{3,1},{1,0},{8,10},{10,12},{12... | collective-permute-start | bytes 1671176 | tf_op jit(solution)/shard_map/ppermute | solution.py:58
  28.0 13.9 %collective-permute-start.3 = (bf16[128,2176]{1,0:T(8,128)(2,1)S(1)}, bf16[128,2176]{1,0:T(8,128)(2,1)S(1)}, u32[]{:S(2)}, u32[]{:S(2)}) collective-permute-start(bf16[128,2176]{1,0:T(8,128)(2,1)S(1)} %collective-permute-done.2.refs_7_), channel_id=1, source_target_pairs={{0,1},{2,0},{4,2},{6,4},{7,6},{5,7},{3,5},{1,3},{8,9},{10,8},{12,1... | collective-permute-start | bytes 1671176 | tf_op jit(solution)/shard_map/ppermute | solution.py:58
  43.1 177.5 %all-gather.7.cloned.1.call-start = ((), (), s32[]{:S(2)}) async-start(), calls=%async_computation.2 | async-start | bytes 10485760 | tf_op jit(solution)/shard_map/all_gather | solution.py:993
  63.9 16.6 %collective-permute-start.8 = (bf16[128,2048]{1,0:T(8,128)(2,1)S(1)}, bf16[128,2048]{1,0:T(8,128)(2,1)S(1)}, u32[]{:S(2)}, u32[]{:S(2)}) collective-permute-start(bf16[128,2048]{1,0:T(8,128)(2,1)S(1)} %copy-done.13), channel_id=1, source_target_pairs={{0,2},{2,4},{4,6},{6,7},{7,5},{5,3},{3,1},{1,0},{8,10},{10,12},{12... | collective-permute-start | bytes 1572872 | tf_op jit(solution)/shard_map/ppermute | solution.py:58
  65.5 15.0 %collective-permute-start.9 = (bf16[128,2048]{1,0:T(8,128)(2,1)S(1)}, bf16[128,2048]{1,0:T(8,128)(2,1)}, u32[]{:S(2)}, u32[]{:S(2)}) collective-permute-start(bf16[128,2048]{1,0:T(8,128)(2,1)S(1)} %copy-done.13), channel_id=1, source_target_pairs={{0,1},{2,0},{4,2},{6,4},{7,6},{5,7},{3,5},{1,3},{8,9},{10,8},{12,1... | collective-permute-start | bytes 1572872 | tf_op jit(solution)/shard_map/ppermute | solution.py:58
  102.9 374.1 %reduce-scatter.2.cloned.1.call-start = ((), (), s32[]{:S(2)}) async-start(), calls=%async_computation.3 | async-start | bytes 10485760 | tf_op jit(solution)/shard_map/reduce_scatter | solution.py:1036
  145.7 15.0 %collective-permute-start.22 = (bf16[128,2048]{1,0:T(8,128)(2,1)S(1)}, bf16[128,2048]{1,0:T(8,128)(2,1)S(1)}, u32[]{:S(2)}, u32[]{:S(2)}) collective-permute-start(bf16[128,2048]{1,0:T(8,128)(2,1)S(1)} %multiply_convert_fusion.refs_2_.refs_8_), channel_id=1, source_target_pairs={{0,1},{2,0},{4,2},{6,4},{7,6},{5,7},{3,5},{1,3},{8,9},{10,8},{12,1... | collective-permute-start | bytes 1572872 | tf_op jit(solution)/shard_map/ppermute | solution.py:58
  148.0 14.1 %collective-permute-start.20 = (bf16[128,2048]{1,0:T(8,128)(2,1)S(1)}, bf16[128,2048]{1,0:T(8,128)(2,1)S(1)}, u32[]{:S(2)}, u32[]{:S(2)}) collective-permute-start(bf16[128,2048]{1,0:T(8,128)(2,1)S(1)} %multiply_convert_fusion.refs_2_.refs_8_), channel_id=1, source_target_pairs={{0,2},{2,4},{4,6},{6,7},{7,5},{5,3},{3,1},{1,0},{8,10},{10,12},{12... | collective-permute-start | bytes 1572872 | tf_op jit(solution)/shard_map/ppermute | solution.py:58
  160.7 15.7 %collective-permute-start.23 = (bf16[128,2048]{1,0:T(8,128)(2,1)S(1)}, bf16[128,2048]{1,0:T(8,128)(2,1)}, u32[]{:S(2)}, u32[]{:S(2)}) collective-permute-start(bf16[128,2048]{1,0:T(8,128)(2,1)S(1)} %collective-permute-done.22.refs_0_.refs_6_), channel_id=1, source_target_pairs={{0,1},{2,0},{4,2},{6,4},{7,6},{5,7},{3,5},{1,3},{8,9},{10,8},{12,1... | collective-permute-start | bytes 1572872 | tf_op jit(solution)/shard_map/ppermute | solution.py:58
  162.1 14.3 %collective-permute-start.21 = (bf16[128,2048]{1,0:T(8,128)(2,1)S(1)}, bf16[128,2048]{1,0:T(8,128)(2,1)}, u32[]{:S(2)}, u32[]{:S(2)}) collective-permute-start(bf16[128,2048]{1,0:T(8,128)(2,1)S(1)} %collective-permute-done.20.refs_1_.refs_7_), channel_id=1, source_target_pairs={{0,2},{2,4},{4,6},{6,7},{7,5},{5,3},{3,1},{1,0},{8,10},{10,12},{12... | collective-permute-start | bytes 1572872 | tf_op jit(solution)/shard_map/ppermute | solution.py:58
  261.0 36.9 %collective-permute-start.34 = (bf16[192,2176]{1,0:T(8,128)(2,1)S(1)}, bf16[192,2176]{1,0:T(8,128)(2,1)S(1)}, u32[]{:S(2)}, u32[]{:S(2)}) collective-permute-start(bf16[192,2176]{1,0:T(8,128)(2,1)S(1)} %fusion.10), channel_id=1, source_target_pairs={{0,2},{2,4},{4,6},{6,7},{7,5},{5,3},{3,1},{1,0},{8,10},{10,12},{12... | collective-permute-start | bytes 2506760 | tf_op jit(solution)/shard_map/ppermute | solution.py:58
  262.5 37.5 %collective-permute-start.35 = (bf16[192,2176]{1,0:T(8,128)(2,1)S(1)}, bf16[192,2176]{1,0:T(8,128)(2,1)}, u32[]{:S(2)}, u32[]{:S(2)}) collective-permute-start(bf16[192,2176]{1,0:T(8,128)(2,1)S(1)} %fusion.11), channel_id=1, source_target_pairs={{0,1},{2,0},{4,2},{6,4},{7,6},{5,7},{3,5},{1,3},{8,9},{10,8},{12,1... | collective-permute-start | bytes 2506760 | tf_op jit(solution)/shard_map/ppermute | solution.py:58
  302.0 17.4 %collective-permute-start.36 = (bf16[128,2176]{1,0:T(8,128)(2,1)}, bf16[128,2176]{1,0:T(8,128)(2,1)}, u32[]{:S(2)}, u32[]{:S(2)}) collective-permute-start(bf16[128,2176]{1,0:T(8,128)(2,1)} %add_convert_fusion.6), channel_id=1, source_target_pairs={{0,2},{2,4},{4,6},{6,7},{7,5},{5,3},{3,1},{1,0},{8,10},{10,12},{12... | collective-permute-start | bytes 1671176 | tf_op jit(solution)/shard_map/ppermute | solution.py:58
  318.7 14.6 %collective-permute-start.37 = (bf16[128,2176]{1,0:T(8,128)(2,1)}, bf16[128,2176]{1,0:T(8,128)(2,1)S(1)}, u32[]{:S(2)}, u32[]{:S(2)}) collective-permute-start(bf16[128,2176]{1,0:T(8,128)(2,1)} %add_convert_fusion.5), channel_id=1, source_target_pairs={{0,1},{2,0},{4,2},{6,4},{7,6},{5,7},{3,5},{1,3},{8,9},{10,8},{12,1... | collective-permute-start | bytes 1671176 | tf_op jit(solution)/shard_map/ppermute | solution.py:58
  333.4 14.4 %collective-permute-start.38 = (bf16[128,2176]{1,0:T(8,128)(2,1)}, bf16[128,2176]{1,0:T(8,128)(2,1)S(1)}, u32[]{:S(2)}, u32[]{:S(2)}) collective-permute-start(bf16[128,2176]{1,0:T(8,128)(2,1)} %add_convert_fusion.4), channel_id=1, source_target_pairs={{0,2},{2,4},{4,6},{6,7},{7,5},{5,3},{3,1},{1,0},{8,10},{10,12},{12... | collective-permute-start | bytes 1671176 | tf_op jit(solution)/shard_map/ppermute | solution.py:58
  364.6 16.0 %collective-permute-start.42 = (bf16[128,2048]{1,0:T(8,128)(2,1)}, bf16[128,2048]{1,0:T(8,128)(2,1)S(1)}, u32[]{:S(2)}, u32[]{:S(2)}) collective-permute-start(bf16[128,2048]{1,0:T(8,128)(2,1)} %collective-permute-done.40.refs_8_), channel_id=1, source_target_pairs={{0,2},{2,4},{4,6},{6,7},{7,5},{5,3},{3,1},{1,0},{8,10},{10,12},{12... | collective-permute-start | bytes 1572872 | tf_op jit(solution)/shard_map/ppermute | solution.py:58
  365.7 14.9 %collective-permute-start.43 = (bf16[128,2048]{1,0:T(8,128)(2,1)}, bf16[128,2048]{1,0:T(8,128)(2,1)}, u32[]{:S(2)}, u32[]{:S(2)}) collective-permute-start(bf16[128,2048]{1,0:T(8,128)(2,1)} %collective-permute-done.41.refs_7_), channel_id=1, source_target_pairs={{0,1},{2,0},{4,2},{6,4},{7,6},{5,7},{3,5},{1,3},{8,9},{10,8},{12,1... | collective-permute-start | bytes 1572872 | tf_op jit(solution)/shard_map/ppermute | solution.py:58
  380.6 13.9 %collective-permute-start.45 = (bf16[128,2048]{1,0:T(8,128)(2,1)S(1)}, bf16[128,2048]{1,0:T(8,128)(2,1)}, u32[]{:S(2)}, u32[]{:S(2)}) collective-permute-start(bf16[128,2048]{1,0:T(8,128)(2,1)S(1)} %collective-permute-done.42.refs_6_), channel_id=1, source_target_pairs={{0,2},{2,4},{4,6},{6,7},{7,5},{5,3},{3,1},{1,0},{8,10},{10,12},{12... | collective-permute-start | bytes 1572872 | tf_op jit(solution)/shard_map/ppermute | solution.py:58
  399.3 51.0 %collective-permute-start.54 = (bf16[1,8,2,512,128]{4,3,2,1,0:T(8,128)(2,1)}, bf16[1,8,2,512,128]{4,3,2,1,0:T(8,128)(2,1)}, u32[]{:S(2)}, u32[]{:S(2)}) collective-permute-start(bf16[1,8,2,512,128]{4,3,2,1,0:T(8,128)(2,1)} %add_convert_fusion.1), channel_id=1, source_target_pairs={{0,16},{8,24},{16,0},{24,8},{1,17},{9,25},{17,1},{25,9},{2,18},{10... | collective-permute-start | bytes 6291464 | tf_op jit(solution)/shard_map/ppermute | solution.py:145
  412.0 17.7 %collective-permute-start.50 = (bf16[128,2048]{1,0:T(8,128)(2,1)}, bf16[128,2048]{1,0:T(8,128)(2,1)S(1)}, u32[]{:S(2)}, u32[]{:S(2)}) collective-permute-start(bf16[128,2048]{1,0:T(8,128)(2,1)} %add_convert_fusion.21), channel_id=1, source_target_pairs={{0,2},{2,4},{4,6},{6,7},{7,5},{5,3},{3,1},{1,0},{8,10},{10,12},{12... | collective-permute-start | bytes 1572872 | tf_op jit(solution)/shard_map/ppermute | solution.py:58
  412.4 18.0 %collective-permute-start.52 = (bf16[128,2048]{1,0:T(8,128)(2,1)}, bf16[128,2048]{1,0:T(8,128)(2,1)S(1)}, u32[]{:S(2)}, u32[]{:S(2)}) collective-permute-start(bf16[128,2048]{1,0:T(8,128)(2,1)} %add_convert_fusion.20), channel_id=1, source_target_pairs={{0,1},{2,0},{4,2},{6,4},{7,6},{5,7},{3,5},{1,3},{8,9},{10,8},{12,1... | collective-permute-start | bytes 1572872 | tf_op jit(solution)/shard_map/ppermute | solution.py:58
  429.9 20.4 %collective-permute-start.51 = (bf16[128,2048]{1,0:T(8,128)(2,1)S(1)}, bf16[128,2048]{1,0:T(8,128)(2,1)S(1)}, u32[]{:S(2)}, u32[]{:S(2)}) collective-permute-start(bf16[128,2048]{1,0:T(8,128)(2,1)S(1)} %add_convert_fusion.19), channel_id=1, source_target_pairs={{0,2},{2,4},{4,6},{6,7},{7,5},{5,3},{3,1},{1,0},{8,10},{10,12},{12... | collective-permute-start | bytes 1572872 | tf_op jit(solution)/shard_map/ppermute | solution.py:58
  430.9 19.4 %collective-permute-start.53 = (bf16[128,2048]{1,0:T(8,128)(2,1)S(1)}, bf16[128,2048]{1,0:T(8,128)(2,1)}, u32[]{:S(2)}, u32[]{:S(2)}) collective-permute-start(bf16[128,2048]{1,0:T(8,128)(2,1)S(1)} %add_convert_fusion.17), channel_id=1, source_target_pairs={{0,1},{2,0},{4,2},{6,4},{7,6},{5,7},{3,5},{1,3},{8,9},{10,8},{12,1... | collective-permute-start | bytes 1572872 | tf_op jit(solution)/shard_map/ppermute | solution.py:58
  452.5 56.9 %collective-permute-start.63 = (bf16[1,8,2,512,128]{4,3,2,1,0:T(8,128)(2,1)}, bf16[1,8,2,512,128]{4,3,2,1,0:T(8,128)(2,1)}, u32[]{:S(2)}, u32[]{:S(2)}) collective-permute-start(bf16[1,8,2,512,128]{4,3,2,1,0:T(8,128)(2,1)} %add_convert_fusion), channel_id=1, source_target_pairs={{0,16},{8,24},{16,0},{24,8},{1,17},{9,25},{17,1},{25,9},{2,18},{10... | collective-permute-start | bytes 6291464 | tf_op jit(solution)/shard_map/ppermute | solution.py:145
  484.3 15.6 %collective-permute-start.61 = (bf16[2,3,512,256]{3,2,1,0:T(8,128)(2,1)}, bf16[2,3,512,256]{3,2,1,0:T(8,128)(2,1)}, u32[]{:S(2)}, u32[]{:S(2)}) collective-permute-start(bf16[2,3,512,256]{3,2,1,0:T(8,128)(2,1)} %get-tuple-element.265), channel_id=1, source_target_pairs={{0,8},{8,0},{16,24},{24,16},{1,9},{9,1},{17,25},{25,17},{2,10},{10... | collective-permute-start | bytes 4718600 | tf_op jit(solution)/shard_map/ppermute | solution.py:145
  509.4 14.6 %collective-permute-start.64 = (bf16[128,2048]{1,0:T(8,128)(2,1)}, bf16[128,2048]{1,0:T(8,128)(2,1)}, u32[]{:S(2)}, u32[]{:S(2)}) collective-permute-start(bf16[128,2048]{1,0:T(8,128)(2,1)} %add_convert_fusion.11), channel_id=1, source_target_pairs={{0,2},{2,4},{4,6},{6,7},{7,5},{5,3},{3,1},{1,0},{8,10},{10,12},{12... | collective-permute-start | bytes 1572872 | tf_op jit(solution)/shard_map/ppermute | solution.py:58
  510.8 14.4 %collective-permute-start.65 = (bf16[128,2048]{1,0:T(8,128)(2,1)}, bf16[128,2048]{1,0:T(8,128)(2,1)}, u32[]{:S(2)}, u32[]{:S(2)}) collective-permute-start(bf16[128,2048]{1,0:T(8,128)(2,1)} %add_convert_fusion.10), channel_id=1, source_target_pairs={{0,1},{2,0},{4,2},{6,4},{7,6},{5,7},{3,5},{1,3},{8,9},{10,8},{12,1... | collective-permute-start | bytes 1572872 | tf_op jit(solution)/shard_map/ppermute | solution.py:58
  514.5 22.4 %collective-permute-start.69 = (bf16[1,256,512]{2,1,0:T(8,128)(2,1)S(1)}, bf16[1,256,512]{2,1,0:T(8,128)(2,1)}, u32[]{:S(2)}, u32[]{:S(2)}) collective-permute-start(bf16[1,256,512]{2,1,0:T(8,128)(2,1)S(1)} %add_convert_fusion.28), channel_id=1, source_target_pairs={{0,16},{8,24},{16,0},{24,8},{1,17},{9,25},{17,1},{25,9},{2,18},{10... | collective-permute-start | bytes 786440 | tf_op jit(solution)/shard_map/ppermute | solution.py:145
  515.8 24.2 %collective-permute-start.68 = (bf16[1,3,512,256]{3,2,1,0:T(8,128)(2,1)}, bf16[1,3,512,256]{3,2,1,0:T(8,128)(2,1)}, u32[]{:S(2)}, u32[]{:S(2)}) collective-permute-start(bf16[1,3,512,256]{3,2,1,0:T(8,128)(2,1)} %add_convert_fusion.2), channel_id=1, source_target_pairs={{0,16},{8,24},{16,0},{24,8},{1,17},{9,25},{17,1},{25,9},{2,18},{10... | collective-permute-start | bytes 2359304 | tf_op jit(solution)/shard_map/ppermute | solution.py:145
  (116 other events, 1175.3 us)
Sparse Core Ops, SparseCore 0:
  12.1 37.3 all-gather.8
  51.6 105.9 all-gather.4
  159.2 58.2 all-gather.6
  336.8 72.2 reduce-scatter.1

commit v6 on v5

--- a/solution.py
+++ b/solution.py
@@ -1034,7 +1034,7 @@
     dn_all = out_grad([hidden_far] + hidden[1:], d_pieces, experts)
     (ready,) = tie((dn_all,), third)
     dn_grad = lax.psum_scatter(ready, "dp", scatter_dimension=2, tiled=True)
-    fourth = d_normed.step(after=[dn_all])
+    fourth = d_normed.step()
 
     def gradient(c, after, whole=None):
         (turned,) = tie((mid_turned,), after)

time: 564 us -> 565 us (level)
  transfers between devices with their start and end apart: 79 -> 79, of which waited for: 42 -> 40; matrix products, arithmetic and copies ran while one was open for 11% -> 11% of each run, Pallas kernels for 38% -> 38%
where the time goes in v6:
time: 565 us; the launch traced here: 555 us
  Pallas kernels  235 us (42%)
  waiting for transfers between devices  142 us (25%)
  starting transfers between devices  83 us (15%)
  other arithmetic  53.5 us (9%)
  local copies, waits for them, and re-layouts  26.2 us (5%)
  between operations  15.3 us (3%)
    ppermute x62, waiting for transfers between devices, ring_step(): return lax.ppermute(value, 'tensor', pairs)  137 us
    ppermute x62, starting transfers between devices, ring_step(): return lax.ppermute(value, 'tensor', pairs)  72.4 us
    pallas_call x2, Pallas kernels, moe_mid(): pl.pallas_call(functools.partial(moe_mid_body, group, steps, len(gus), co...  58.1 us
    pallas_call x4, Pallas kernels, in_grad(): pl.pallas_call(functools.partial(in_grad_body, n, group, sets), grid=(num...  38.8 us
    pallas_call x3, Pallas kernels, moe_in(): pl.pallas_call(functools.partial(moe_in_body, count), grid=(columns // wi...  34.5 us
    pallas_call x1, Pallas kernels, proj_back(): pl.pallas_call(functools.partial(proj_back_body, count, steps), grid=(ste...  15.5 us
    pallas_call x1, Pallas kernels, attn_back(): pl.pallas_call(functools.partial(attn_back_body, count, min(256, length))...  15.5 us
    pallas_call x1, Pallas kernels, out_grad(): pl.pallas_call(functools.partial(out_grad_body, group, count, len(hws)),...  15.2 us
  transfers between devices with their start and end apart: 79, of which 40 were waited for; matrix products, arithmetic and copies ran while one was open for 11% of the time, Pallas kernels for 38%

profile of v6, /device:TPU:0, one launch (start us, length us, event | category | flops | bytes accessed | tf_op | source)
XLA Modules:
  0.0 554.9 jit_solution(15618074249047040878)
XLA Ops:
  15.4 12.6 %collective-permute-done.2.refs_7_ = bf16[128,2176]{1,0:T(8,128)(2,1)S(1)} collective-permute-done((bf16[128,2176]{1,0:T(8,128)(2,1)S(1)}, bf16[128,2176]{1,0:T(8,128)(2,1)S(1)}, u32[]{:S(2)}, u32[]{:S(2)}) %collective-permute-start.2) | collective-permute-done | bytes 557088 | tf_op jit(solution)/shard_map/ppermute | solution.py:58
  30.0 5.1 pack.1
  35.2 6.7 %collective-permute-done.3.refs_5_ = bf16[128,2176]{1,0:T(8,128)(2,1)S(1)} collective-permute-done((bf16[128,2176]{1,0:T(8,128)(2,1)S(1)}, bf16[128,2176]{1,0:T(8,128)(2,1)S(1)}, u32[]{:S(2)}, u32[]{:S(2)}) %collective-permute-start.3) | collective-permute-done | bytes 557088 | tf_op jit(solution)/shard_map/ppermute | solution.py:58
  45.2 10.9 %collective-permute-done.4.refs_4_ = bf16[128,2176]{1,0:T(8,128)(2,1)S(1)} collective-permute-done((bf16[128,2176]{1,0:T(8,128)(2,1)}, bf16[128,2176]{1,0:T(8,128)(2,1)S(1)}, u32[]{:S(2)}, u32[]{:S(2)}) %collective-permute-start.4) | collective-permute-done | bytes 557088 | tf_op jit(solution)/shard_map/ppermute | solution.py:58
  69.2 11.3 %attn_proj.1 = (bf16[1024,256]{1,0:T(8,128)(2,1)}, bf16[1024,256]{1,0:T(8,128)(2,1)}, bf16[1024,256]{1,0:T(8,128)(2,1)}, f32[1024,256]{1,0:T(8,128)}, f32[1024,256]{1,0:T(8,128)}, /*index=5*/bf16[1024,2048]{1,0:T(8,128)(2,1)}) custom-call(s32[8]{0:T(128)} %dynamic-slice_bitcast_fusion.1.refs_0_, bf16[64,2176]{1,0:T(8,128)(2,1)} %copy-done.44, ...), custom_call_target="tpu_custom_call" | custom-call | flops 6000000000 | bytes 1048576 | tf_op jit(solution)/shard_map/attn_proj/pallas_call | solution.py:312
  82.6 10.4 %attn_core.1 = (bf16[1024,256]{1,0:T(8,128)(2,1)}, f32[2,1024,1]{2,1,0:T(8,128)}, bf16[64,2048]{1,0:T(8,128)(2,1)}, bf16[64,2048]{1,0:T(8,128)(2,1)}, bf16[128,2...) custom-call(s32[8]{0:T(128)} %dynamic-slice_bitcast_fusion.1.refs_0_, ...), custom_call_target="tpu_custom_call" | custom-call | flops 6000000000 | bytes 1048576 | tf_op jit(solution)/shard_map/attn_core/pallas_call | solution.py:371
  95.4 4.6 collective-permute-done.12
  106.0 8.9 %collective-permute-done.17 = bf16[128,2048]{1,0:T(8,128)(2,1)S(1)} collective-permute-done((bf16[128,2048]{1,0:T(8,128)(2,1)S(1)}, bf16[128,2048]{1,0:T(8,128)(2,1)S(1)}, u32[]{:S(2)}, u32[]{:S(2)}) %collective-permute-start.17) | collective-permute-done | bytes 524320 | tf_op jit(solution)/shard_map/ppermute | solution.py:58
  118.9 9.0 %collective-permute-done.18 = bf16[128,2048]{1,0:T(8,128)(2,1)S(1)} collective-permute-done((bf16[128,2048]{1,0:T(8,128)(2,1)S(1)}, bf16[128,2048]{1,0:T(8,128)(2,1)S(1)}, u32[]{:S(2)}, u32[]{:S(2)}) %collective-permute-start.18) | collective-permute-done | bytes 524320 | tf_op jit(solution)/shard_map/ppermute | solution.py:58
  133.9 6.6 %collective-permute-done.19 = bf16[128,2048]{1,0:T(8,128)(2,1)S(1)} collective-permute-done((bf16[128,2048]{1,0:T(8,128)(2,1)S(1)}, bf16[128,2048]{1,0:T(8,128)(2,1)S(1)}, u32[]{:S(2)}, u32[]{:S(2)}) %collective-permute-start.19) | collective-permute-done | bytes 524320 | tf_op jit(solution)/shard_map/ppermute | solution.py:58
  149.3 11.4 %collective-permute-done.22.refs_0_.refs_6_ = bf16[128,2048]{1,0:T(8,128)(2,1)S(1)} collective-permute-done((bf16[128,2048]{1,0:T(8,128)(2,1)S(1)}, bf16[128,2048]{1,0:T(8,128)(2,1)S(1)}, u32[]{:S(2)}, u32[]{:S(2)}) %collective-permute-start.22) | collective-permute-done | bytes 524320 | tf_op jit(solution)/shard_map/ppermute | solution.py:58
  163.3 13.0 %moe_in.3.refs_7_ = bf16[384,4096]{1,0:T(8,128)(2,1)} custom-call(bf16[128,2048]{1,0:T(8,128)(2,1)} %copy-done.59, bf16[128,2048]{1,0:T(8,128)(2,1)} %copy-done.60, bf16[128,2048]{1,0:T(8,128)(2,1)} %copy-done.29, bf16[2048,4096]{1,0:T(8,128)(2,1)} %all-gather.5.cloned.1.call-done.refs_3_.refs_2_.refs_4_.refs_6_.refs_8_), custom_call_target="tpu_custom_call" | custom-call | flops 7008000000 | bytes 1048576 | tf_op jit(solution)/shard_map/moe_in/pallas_call | solution.py:599
  179.3 9.8 %moe_in.4.refs_6_ = bf16[256,4096]{1,0:T(8,128)(2,1)} custom-call(bf16[128,2048]{1,0:T(8,128)(2,1)} %collective-permute-done.23.refs_0_.refs_4_, bf16[128,2048]{1,0:T(8,128)(2,1)} %collective-permute-done.21.refs_1_.refs_5_, bf16[2048,4096]{1,0:T(8,128)(2,1)} %all-gather.5.cloned.1.call-done.refs_3_.refs_2_.refs_4_.refs_6_.refs_8_), custom_call_target="tpu_custom_call" | custom-call | flops 5472000000 | bytes 1048576 | tf_op jit(solution)/shard_map/moe_in/pallas_call | solution.py:599
  205.3 11.6 %moe_in.5.refs_5_ = bf16[384,4096]{1,0:T(8,128)(2,1)} custom-call(bf16[64,2048]{1,0:T(8,128)(2,1)} %copy-done.62, bf16[64,2048]{1,0:T(8,128)(2,1)} %copy-done.63, bf16[128,2048]{1,0:T(8,128)(2,1)} %copy-done.42, bf16[128,2048]{1,0:T(8,128)(2,1)} %copy-done.41, bf16[2048,4096]{1,0:T(8,128)(2,1)} %all-gather.5.cloned.1.call-done.refs_3_.refs_2_.refs_4_.refs_6_.refs_8_), custom_call_target="tpu_custom_call" | custom-call | flops 7008000000 | bytes 1048576 | tf_op jit(solution)/shard_map/moe_in/pallas_call | solution.py:599
  225.0 23.7 %moe_mid.2 = (bf16[64,2176]{1,0:T(8,128)(2,1)}, bf16[64,2176]{1,0:T(8,128)(2,1)}, bf16[128,2176]{1,0:T(8,128)(2,1)}, bf16[128,2176]{1,0:T(8,128)(2,1)}, bf16[64,...) custom-call(bf16[384,128]{1,0:T(8,128)(2,1)} %pad_slice_fusion.refs_, ...), custom_call_target="tpu_custom_call" | custom-call | flops 12816000000 | bytes 1048576 | tf_op jit(solution)/shard_map/moe_mid/pallas_call | solution.py:677
  251.5 5.5 turn_rows.1.xt
  262.6 34.5 %moe_mid.3 = (bf16[128,2176]{1,0:T(8,128)(2,1)}, bf16[128,2176]{1,0:T(8,128)(2,1)}, bf16[128,2176]{1,0:T(8,128)(2,1)}, bf16[128,2176]{1,0:T(8,128)(2,1)}, bf16[1...) custom-call(bf16[640,128]{1,0:T(8,128)(2,1)} %pad_slice_fusion.1.ref, ...), custom_call_target="tpu_custom_call" | custom-call | flops 18959998976 | bytes 1048576 | tf_op jit(solution)/shard_map/moe_mid/pallas_call | solution.py:677
  304.4 12.1 %collective-permute-done.36 = bf16[128,2176]{1,0:T(8,128)(2,1)} collective-permute-done((bf16[128,2176]{1,0:T(8,128)(2,1)}, bf16[128,2176]{1,0:T(8,128)(2,1)}, u32[]{:S(2)}, u32[]{:S(2)}) %collective-permute-start.36) | collective-permute-done | bytes 557088 | tf_op jit(solution)/shard_map/ppermute | solution.py:58
  321.6 15.2 %out_grad.1 = bf16[16,128,2048]{2,1,0:T(8,128)(2,1)} custom-call(bf16[384,2048]{1,0:T(8,128)(2,1)} %get-tuple-element.251.refs_0_, bf16[640,2048]{1,0:T(8,128)(2,1)} %get-tuple-element.252.refs_1_, bf16[64,2048]{1,0:T(8,128)(2,1)} %collective-permute-done.30.refs_1_.refs_2_, bf16[64,2048]{1,0:T(8,128)(2,1)} %collective-permute-done.31.refs_2_.refs_3_, ...), custom_call_target="tpu_custom_call" | custom-call | flops 7200000000 | bytes 1048576 | tf_op jit(solution)/shard_map/out_grad/pallas_call | solution.py:816
  336.8 9.7 %in_grad.4 = (bf16[2,8,2,512,128]{4,3,2,1,0:T(8,128)(2,1)}, bf16[2,8,2,512,128]{4,3,2,1,0:T(8,128)(2,1)}) custom-call(s32[4]{0:T(128)} %dynamic-slice_bitcast_fusion.places, bf16[2048,1024]{1,0:T(8,128)(2,1)} %turn_rows.1.xt, bf16[384,4096]{1,0:T(8,128)(2,1)} %get-tuple-element.199.refs_0_, bf16[640,4096]{1,0:T(8,128)(2,1)} %get-tuple-element.200.refs_1_), custom_call_target="tpu_custom_call" | custom-call | flops 5400000000 | bytes 1048576 | tf_op jit(solution)/shard_map/in_grad/pallas_call | solution.py:777
  354.6 9.6 %in_grad.5 = (bf16[2,8,2,512,128]{4,3,2,1,0:T(8,128)(2,1)}, bf16[2,8,2,512,128]{4,3,2,1,0:T(8,128)(2,1)}) custom-call(s32[4]{0:T(128)} %dynamic-slice_bitcast_fusion.places, bf16[2048,1024]{1,0:T(8,128)(2,1)} %turn_rows.1.xt, bf16[384,4096]{1,0:T(8,128)(2,1)} %get-tuple-element.199.refs_0_, ...), custom_call_target="tpu_custom_call", output_to_operand_aliasing={{0}: (4, {}), {1}: (5, {})} | custom-call | flops 5400000000 | bytes 1048576 | tf_op jit(solution)/shard_map/in_grad/pallas_call | solution.py:777
  366.4 9.7 %in_grad.6 = (bf16[2,8,2,512,128]{4,3,2,1,0:T(8,128)(2,1)}, bf16[2,8,2,512,128]{4,3,2,1,0:T(8,128)(2,1)}) custom-call(s32[4]{0:T(128)} %dynamic-slice_bitcast_fusion.places, bf16[2048,1024]{1,0:T(8,128)(2,1)} %turn_rows.1.xt, bf16[384,4096]{1,0:T(8,128)(2,1)} %get-tuple-element.199.refs_0_, bf16[640,4096]{1,0:T(8,128)(2,1)} %get-tuple-element.200.refs_1_), custom_call_target="tpu_custom_call" | custom-call | flops 5400000000 | bytes 1048576 | tf_op jit(solution)/shard_map/in_grad/pallas_call | solution.py:777
  382.3 9.7 %in_grad.7 = (bf16[2,8,2,512,128]{4,3,2,1,0:T(8,128)(2,1)}, bf16[2,8,2,512,128]{4,3,2,1,0:T(8,128)(2,1)}) custom-call(s32[4]{0:T(128)} %dynamic-slice_bitcast_fusion.places, bf16[2048,1024]{1,0:T(8,128)(2,1)} %turn_rows.1.xt, bf16[384,4096]{1,0:T(8,128)(2,1)} %get-tuple-element.199.refs_0_, ...), custom_call_target="tpu_custom_call", output_to_operand_aliasing={{0}: (4, {}), {1}: (5, {})} | custom-call | flops 5400000000 | bytes 1048576 | tf_op jit(solution)/shard_map/in_grad/pallas_call | solution.py:777
  404.2 4.1 add_convert_fusion
  414.0 15.5 %attn_back.1 = (f32[1024,256]{1,0:T(8,128)}, f32[1024,256]{1,0:T(8,128)}, f32[1024,256]{1,0:T(8,128)}, bf16[1024,2048]{1,0:T(8,128)(2,1)}) custom-call(s32[8]{0:T(128)} %dynamic-slice_bitcast_fusion.1.refs_0_, bf16[64,2048]{1,0:T(8,128)(2,1)} %copy-done.64, bf16[64,2048]{1,0:T(8,128)(2,1)} %copy-done.65, bf16[128,2048]{1,0:T(8,128)(2,1)} %collective-permute-done.46.refs_3_, ...), custom_call_target="tpu_custom_call" | custom-call | flops 8400000000 | bytes 1048576 | tf_op jit(solution)/shard_map/attn_back/pallas_call | solution.py:432
  432.0 15.5 %proj_back.1 = (bf16[1024,768]{1,0:T(8,128)(2,1)}, f32[2,256]{1,0:T(2,128)}, f32[1,2048]{1,0:T(1,128)}, bf16[64,2048]{1,0:T(8,128)(2,1)}, bf16[64,2048]{1,0:T(8,...) custom-call(s32[8]{0:T(128)} %dynamic-slice_bitcast_fusion.1.refs_0_, ...), custom_call_target="tpu_custom_call" | custom-call | flops 7200000000 | bytes 1048576 | tf_op jit(solution)/shard_map/proj_back/pallas_call | solution.py:510
  455.5 4.3 collective-permute-done.57
  464.9 9.8 %attn_grad.1 = (bf16[2,3,512,256]{3,2,1,0:T(8,128)(2,1)}, bf16[2,3,512,256]{3,2,1,0:T(8,128)(2,1)}, bf16[2,256,512]{2,1,0:T(8,128)(2,1)}, bf16[2,256,512]{2,1,0:T(8,128)(2,1)}) custom-call(s32[4]{0:T(128)} %dynamic-slice_bitcast_fusion.places, bf16[1024,2048]{1,0:T(8,128)(2,1)} %get-tuple-element.235.refs_10_.xa.xb, ...), custom_call_target="tpu_custom_call" | custom-call | flops 3600000000 | bytes 1048576 | tf_op jit(solution)/shard_map/attn_grad/pallas_call | solution.py:549
  478.2 4.3 place.1
  485.9 5.4 finish.2.refs_0_
  518.8 6.1 %collective-permute-done.64 = bf16[128,2048]{1,0:T(8,128)(2,1)} collective-permute-done((bf16[128,2048]{1,0:T(8,128)(2,1)}, bf16[128,2048]{1,0:T(8,128)(2,1)}, u32[]{:S(2)}, u32[]{:S(2)}) %collective-permute-start.64) | collective-permute-done | bytes 524320 | tf_op jit(solution)/shard_map/ppermute | solution.py:58
  532.3 5.4 finish.3
  (449 shorter events, 207.6 us)
Async XLA Ops:
  7.2 58.8 %all-gather.9.cloned.1.call-start = ((), (), s32[]{:S(2)}) async-start(), calls=%async_computation.4 | async-start | bytes 5283840 | tf_op jit(solution)/shard_map/all_gather | solution.py:946
  12.0 151.4 %all-gather.5.cloned.1.call-start = ((), (), s32[]{:S(2)}) async-start(), calls=%async_computation.1 | async-start | bytes 20971520 | tf_op jit(solution)/shard_map/all_gather | solution.py:964
  12.3 15.7 %collective-permute-start.2 = (bf16[128,2176]{1,0:T(8,128)(2,1)S(1)}, bf16[128,2176]{1,0:T(8,128)(2,1)S(1)}, u32[]{:S(2)}, u32[]{:S(2)}) collective-permute-start(bf16[128,2176]{1,0:T(8,128)(2,1)S(1)} %fusion.12.refs_9_), channel_id=1, source_target_pairs={{0,1},{2,0},{4,2},{6,4},{7,6},{5,7},{3,5},{1,3},{8,9},{10,8},{12,1... | collective-permute-start | bytes 1671176 | tf_op jit(solution)/shard_map/ppermute | solution.py:58
  15.3 14.4 %collective-permute-start = (bf16[128,2176]{1,0:T(8,128)(2,1)S(1)}, bf16[128,2176]{1,0:T(8,128)(2,1)S(1)}, u32[]{:S(2)}, u32[]{:S(2)}) collective-permute-start(bf16[128,2176]{1,0:T(8,128)(2,1)S(1)} %fusion.12.refs_9_), channel_id=1, source_target_pairs={{0,2},{2,4},{4,6},{6,7},{7,5},{5,3},{3,1},{1,0},{8,10},{10,12},{12... | collective-permute-start | bytes 1671176 | tf_op jit(solution)/shard_map/ppermute | solution.py:58
  43.1 176.9 %all-gather.7.cloned.1.call-start = ((), (), s32[]{:S(2)}) async-start(), calls=%async_computation.2 | async-start | bytes 10485760 | tf_op jit(solution)/shard_map/all_gather | solution.py:993
  63.9 16.6 %collective-permute-start.8 = (bf16[128,2048]{1,0:T(8,128)(2,1)S(1)}, bf16[128,2048]{1,0:T(8,128)(2,1)S(1)}, u32[]{:S(2)}, u32[]{:S(2)}) collective-permute-start(bf16[128,2048]{1,0:T(8,128)(2,1)S(1)} %copy-done.14), channel_id=1, source_target_pairs={{0,2},{2,4},{4,6},{6,7},{7,5},{5,3},{3,1},{1,0},{8,10},{10,12},{12... | collective-permute-start | bytes 1572872 | tf_op jit(solution)/shard_map/ppermute | solution.py:58
  65.5 15.0 %collective-permute-start.9 = (bf16[128,2048]{1,0:T(8,128)(2,1)S(1)}, bf16[128,2048]{1,0:T(8,128)(2,1)}, u32[]{:S(2)}, u32[]{:S(2)}) collective-permute-start(bf16[128,2048]{1,0:T(8,128)(2,1)S(1)} %copy-done.14), channel_id=1, source_target_pairs={{0,1},{2,0},{4,2},{6,4},{7,6},{5,7},{3,5},{1,3},{8,9},{10,8},{12,1... | collective-permute-start | bytes 1572872 | tf_op jit(solution)/shard_map/ppermute | solution.py:58
  102.9 375.3 %reduce-scatter.2.cloned.1.call-start = ((), (), s32[]{:S(2)}) async-start(), calls=%async_computation.3 | async-start | bytes 10485760 | tf_op jit(solution)/shard_map/reduce_scatter | solution.py:1036
  117.4 13.9 %collective-permute-start.14 = (bf16[128,2048]{1,0:T(8,128)(2,1)S(1)}, bf16[128,2048]{1,0:T(8,128)(2,1)S(1)}, u32[]{:S(2)}, u32[]{:S(2)}) collective-permute-start(bf16[128,2048]{1,0:T(8,128)(2,1)S(1)} %add_convert_fusion.26), channel_id=1, source_target_pairs={{0,2},{2,4},{4,6},{6,7},{7,5},{5,3},{3,1},{1,0},{8,10},{10,12},{12... | collective-permute-start | bytes 1572872 | tf_op jit(solution)/shard_map/ppermute | solution.py:58
  145.7 15.0 %collective-permute-start.22 = (bf16[128,2048]{1,0:T(8,128)(2,1)S(1)}, bf16[128,2048]{1,0:T(8,128)(2,1)S(1)}, u32[]{:S(2)}, u32[]{:S(2)}) collective-permute-start(bf16[128,2048]{1,0:T(8,128)(2,1)S(1)} %multiply_convert_fusion.refs_2_.refs_8_), channel_id=1, source_target_pairs={{0,1},{2,0},{4,2},{6,4},{7,6},{5,7},{3,5},{1,3},{8,9},{10,8},{12,1... | collective-permute-start | bytes 1572872 | tf_op jit(solution)/shard_map/ppermute | solution.py:58
  148.0 14.1 %collective-permute-start.20 = (bf16[128,2048]{1,0:T(8,128)(2,1)S(1)}, bf16[128,2048]{1,0:T(8,128)(2,1)S(1)}, u32[]{:S(2)}, u32[]{:S(2)}) collective-permute-start(bf16[128,2048]{1,0:T(8,128)(2,1)S(1)} %multiply_convert_fusion.refs_2_.refs_8_), channel_id=1, source_target_pairs={{0,2},{2,4},{4,6},{6,7},{7,5},{5,3},{3,1},{1,0},{8,10},{10,12},{12... | collective-permute-start | bytes 1572872 | tf_op jit(solution)/shard_map/ppermute | solution.py:58
  160.7 15.7 %collective-permute-start.23 = (bf16[128,2048]{1,0:T(8,128)(2,1)S(1)}, bf16[128,2048]{1,0:T(8,128)(2,1)}, u32[]{:S(2)}, u32[]{:S(2)}) collective-permute-start(bf16[128,2048]{1,0:T(8,128)(2,1)S(1)} %collective-permute-done.22.refs_0_.refs_6_), channel_id=1, source_target_pairs={{0,1},{2,0},{4,2},{6,4},{7,6},{5,7},{3,5},{1,3},{8,9},{10,8},{12,1... | collective-permute-start | bytes 1572872 | tf_op jit(solution)/shard_map/ppermute | solution.py:58
  162.1 14.3 %collective-permute-start.21 = (bf16[128,2048]{1,0:T(8,128)(2,1)S(1)}, bf16[128,2048]{1,0:T(8,128)(2,1)}, u32[]{:S(2)}, u32[]{:S(2)}) collective-permute-start(bf16[128,2048]{1,0:T(8,128)(2,1)S(1)} %collective-permute-done.20.refs_1_.refs_7_), channel_id=1, source_target_pairs={{0,2},{2,4},{4,6},{6,7},{7,5},{5,3},{3,1},{1,0},{8,10},{10,12},{12... | collective-permute-start | bytes 1572872 | tf_op jit(solution)/shard_map/ppermute | solution.py:58
  260.1 36.9 %collective-permute-start.34 = (bf16[192,2176]{1,0:T(8,128)(2,1)S(1)}, bf16[192,2176]{1,0:T(8,128)(2,1)S(1)}, u32[]{:S(2)}, u32[]{:S(2)}) collective-permute-start(bf16[192,2176]{1,0:T(8,128)(2,1)S(1)} %fusion.10), channel_id=1, source_target_pairs={{0,2},{2,4},{4,6},{6,7},{7,5},{5,3},{3,1},{1,0},{8,10},{10,12},{12... | collective-permute-start | bytes 2506760 | tf_op jit(solution)/shard_map/ppermute | solution.py:58
  261.6 37.6 %collective-permute-start.35 = (bf16[192,2176]{1,0:T(8,128)(2,1)S(1)}, bf16[192,2176]{1,0:T(8,128)(2,1)}, u32[]{:S(2)}, u32[]{:S(2)}) collective-permute-start(bf16[192,2176]{1,0:T(8,128)(2,1)S(1)} %fusion.11), channel_id=1, source_target_pairs={{0,1},{2,0},{4,2},{6,4},{7,6},{5,7},{3,5},{1,3},{8,9},{10,8},{12,1... | collective-permute-start | bytes 2506760 | tf_op jit(solution)/shard_map/ppermute | solution.py:58
  301.2 15.3 %collective-permute-start.36 = (bf16[128,2176]{1,0:T(8,128)(2,1)}, bf16[128,2176]{1,0:T(8,128)(2,1)}, u32[]{:S(2)}, u32[]{:S(2)}) collective-permute-start(bf16[128,2176]{1,0:T(8,128)(2,1)} %add_convert_fusion.6), channel_id=1, source_target_pairs={{0,2},{2,4},{4,6},{6,7},{7,5},{5,3},{3,1},{1,0},{8,10},{10,12},{12... | collective-permute-start | bytes 1671176 | tf_op jit(solution)/shard_map/ppermute | solution.py:58
  303.8 16.3 %collective-permute-start.38 = (bf16[128,2176]{1,0:T(8,128)(2,1)}, bf16[128,2176]{1,0:T(8,128)(2,1)S(1)}, u32[]{:S(2)}, u32[]{:S(2)}) collective-permute-start(bf16[128,2176]{1,0:T(8,128)(2,1)} %add_convert_fusion.5), channel_id=1, source_target_pairs={{0,1},{2,0},{4,2},{6,4},{7,6},{5,7},{3,5},{1,3},{8,9},{10,8},{12,1... | collective-permute-start | bytes 1671176 | tf_op jit(solution)/shard_map/ppermute | solution.py:58
  318.6 28.0 %collective-permute-start.37 = (bf16[128,2176]{1,0:T(8,128)(2,1)}, bf16[128,2176]{1,0:T(8,128)(2,1)S(1)}, u32[]{:S(2)}, u32[]{:S(2)}) collective-permute-start(bf16[128,2176]{1,0:T(8,128)(2,1)} %add_convert_fusion.4), channel_id=1, source_target_pairs={{0,2},{2,4},{4,6},{6,7},{7,5},{5,3},{3,1},{1,0},{8,10},{10,12},{12... | collective-permute-start | bytes 1671176 | tf_op jit(solution)/shard_map/ppermute | solution.py:58
  321.1 25.6 %collective-permute-start.39 = (bf16[128,2176]{1,0:T(8,128)(2,1)}, bf16[128,2176]{1,0:T(8,128)(2,1)S(1)}, u32[]{:S(2)}, u32[]{:S(2)}) collective-permute-start(bf16[128,2176]{1,0:T(8,128)(2,1)} %add_convert_fusion.3), channel_id=1, source_target_pairs={{0,1},{2,0},{4,2},{6,4},{7,6},{5,7},{3,5},{1,3},{8,9},{10,8},{12,1... | collective-permute-start | bytes 1671176 | tf_op jit(solution)/shard_map/ppermute | solution.py:58
  364.3 15.9 %collective-permute-start.42 = (bf16[128,2048]{1,0:T(8,128)(2,1)}, bf16[128,2048]{1,0:T(8,128)(2,1)S(1)}, u32[]{:S(2)}, u32[]{:S(2)}) collective-permute-start(bf16[128,2048]{1,0:T(8,128)(2,1)} %collective-permute-done.40.refs_8_), channel_id=1, source_target_pairs={{0,2},{2,4},{4,6},{6,7},{7,5},{5,3},{3,1},{1,0},{8,10},{10,12},{12... | collective-permute-start | bytes 1572872 | tf_op jit(solution)/shard_map/ppermute | solution.py:58
  366.0 14.3 %collective-permute-start.43 = (bf16[128,2048]{1,0:T(8,128)(2,1)}, bf16[128,2048]{1,0:T(8,128)(2,1)}, u32[]{:S(2)}, u32[]{:S(2)}) collective-permute-start(bf16[128,2048]{1,0:T(8,128)(2,1)} %collective-permute-done.41.refs_7_), channel_id=1, source_target_pairs={{0,1},{2,0},{4,2},{6,4},{7,6},{5,7},{3,5},{1,3},{8,9},{10,8},{12,1... | collective-permute-start | bytes 1572872 | tf_op jit(solution)/shard_map/ppermute | solution.py:58
  399.7 51.8 %collective-permute-start.54 = (bf16[1,8,2,512,128]{4,3,2,1,0:T(8,128)(2,1)}, bf16[1,8,2,512,128]{4,3,2,1,0:T(8,128)(2,1)}, u32[]{:S(2)}, u32[]{:S(2)}) collective-permute-start(bf16[1,8,2,512,128]{4,3,2,1,0:T(8,128)(2,1)} %add_convert_fusion.1), channel_id=1, source_target_pairs={{0,16},{8,24},{16,0},{24,8},{1,17},{9,25},{17,1},{25,9},{2,18},{10... | collective-permute-start | bytes 6291464 | tf_op jit(solution)/shard_map/ppermute | solution.py:145
  411.8 17.8 %collective-permute-start.50 = (bf16[128,2048]{1,0:T(8,128)(2,1)}, bf16[128,2048]{1,0:T(8,128)(2,1)S(1)}, u32[]{:S(2)}, u32[]{:S(2)}) collective-permute-start(bf16[128,2048]{1,0:T(8,128)(2,1)} %add_convert_fusion.21), channel_id=1, source_target_pairs={{0,2},{2,4},{4,6},{6,7},{7,5},{5,3},{3,1},{1,0},{8,10},{10,12},{12... | collective-permute-start | bytes 1572872 | tf_op jit(solution)/shard_map/ppermute | solution.py:58
  413.3 18.0 %collective-permute-start.52 = (bf16[128,2048]{1,0:T(8,128)(2,1)}, bf16[128,2048]{1,0:T(8,128)(2,1)S(1)}, u32[]{:S(2)}, u32[]{:S(2)}) collective-permute-start(bf16[128,2048]{1,0:T(8,128)(2,1)} %add_convert_fusion.20), channel_id=1, source_target_pairs={{0,1},{2,0},{4,2},{6,4},{7,6},{5,7},{3,5},{1,3},{8,9},{10,8},{12,1... | collective-permute-start | bytes 1572872 | tf_op jit(solution)/shard_map/ppermute | solution.py:58
  429.7 21.7 %collective-permute-start.51 = (bf16[128,2048]{1,0:T(8,128)(2,1)S(1)}, bf16[128,2048]{1,0:T(8,128)(2,1)S(1)}, u32[]{:S(2)}, u32[]{:S(2)}) collective-permute-start(bf16[128,2048]{1,0:T(8,128)(2,1)S(1)} %add_convert_fusion.19), channel_id=1, source_target_pairs={{0,2},{2,4},{4,6},{6,7},{7,5},{5,3},{3,1},{1,0},{8,10},{10,12},{12... | collective-permute-start | bytes 1572872 | tf_op jit(solution)/shard_map/ppermute | solution.py:58
  431.4 20.1 %collective-permute-start.53 = (bf16[128,2048]{1,0:T(8,128)(2,1)S(1)}, bf16[128,2048]{1,0:T(8,128)(2,1)}, u32[]{:S(2)}, u32[]{:S(2)}) collective-permute-start(bf16[128,2048]{1,0:T(8,128)(2,1)S(1)} %add_convert_fusion.17), channel_id=1, source_target_pairs={{0,1},{2,0},{4,2},{6,4},{7,6},{5,7},{3,5},{1,3},{8,9},{10,8},{12,1... | collective-permute-start | bytes 1572872 | tf_op jit(solution)/shard_map/ppermute | solution.py:58
  453.6 56.6 %collective-permute-start.63 = (bf16[1,8,2,512,128]{4,3,2,1,0:T(8,128)(2,1)}, bf16[1,8,2,512,128]{4,3,2,1,0:T(8,128)(2,1)}, u32[]{:S(2)}, u32[]{:S(2)}) collective-permute-start(bf16[1,8,2,512,128]{4,3,2,1,0:T(8,128)(2,1)} %add_convert_fusion), channel_id=1, source_target_pairs={{0,16},{8,24},{16,0},{24,8},{1,17},{9,25},{17,1},{25,9},{2,18},{10... | collective-permute-start | bytes 6291464 | tf_op jit(solution)/shard_map/ppermute | solution.py:145
  485.4 15.3 %collective-permute-start.61 = (bf16[2,3,512,256]{3,2,1,0:T(8,128)(2,1)}, bf16[2,3,512,256]{3,2,1,0:T(8,128)(2,1)}, u32[]{:S(2)}, u32[]{:S(2)}) collective-permute-start(bf16[2,3,512,256]{3,2,1,0:T(8,128)(2,1)} %get-tuple-element.261), channel_id=1, source_target_pairs={{0,8},{8,0},{16,24},{24,16},{1,9},{9,1},{17,25},{25,17},{2,10},{10... | collective-permute-start | bytes 4718600 | tf_op jit(solution)/shard_map/ppermute | solution.py:145
  510.2 14.6 %collective-permute-start.64 = (bf16[128,2048]{1,0:T(8,128)(2,1)}, bf16[128,2048]{1,0:T(8,128)(2,1)}, u32[]{:S(2)}, u32[]{:S(2)}) collective-permute-start(bf16[128,2048]{1,0:T(8,128)(2,1)} %add_convert_fusion.11), channel_id=1, source_target_pairs={{0,2},{2,4},{4,6},{6,7},{7,5},{5,3},{3,1},{1,0},{8,10},{10,12},{12... | collective-permute-start | bytes 1572872 | tf_op jit(solution)/shard_map/ppermute | solution.py:58
  511.6 14.4 %collective-permute-start.65 = (bf16[128,2048]{1,0:T(8,128)(2,1)}, bf16[128,2048]{1,0:T(8,128)(2,1)}, u32[]{:S(2)}, u32[]{:S(2)}) collective-permute-start(bf16[128,2048]{1,0:T(8,128)(2,1)} %add_convert_fusion.10), channel_id=1, source_target_pairs={{0,1},{2,0},{4,2},{6,4},{7,6},{5,7},{3,5},{1,3},{8,9},{10,8},{12,1... | collective-permute-start | bytes 1572872 | tf_op jit(solution)/shard_map/ppermute | solution.py:58
  515.4 22.3 %collective-permute-start.69 = (bf16[1,256,512]{2,1,0:T(8,128)(2,1)S(1)}, bf16[1,256,512]{2,1,0:T(8,128)(2,1)}, u32[]{:S(2)}, u32[]{:S(2)}) collective-permute-start(bf16[1,256,512]{2,1,0:T(8,128)(2,1)S(1)} %add_convert_fusion.28), channel_id=1, source_target_pairs={{0,16},{8,24},{16,0},{24,8},{1,17},{9,25},{17,1},{25,9},{2,18},{10... | collective-permute-start | bytes 786440 | tf_op jit(solution)/shard_map/ppermute | solution.py:145
  516.6 24.4 %collective-permute-start.68 = (bf16[1,3,512,256]{3,2,1,0:T(8,128)(2,1)}, bf16[1,3,512,256]{3,2,1,0:T(8,128)(2,1)}, u32[]{:S(2)}, u32[]{:S(2)}) collective-permute-start(bf16[1,3,512,256]{3,2,1,0:T(8,128)(2,1)} %add_convert_fusion.2), channel_id=1, source_target_pairs={{0,16},{8,24},{16,0},{24,8},{1,17},{9,25},{17,1},{25,9},{2,18},{10... | collective-permute-start | bytes 2359304 | tf_op jit(solution)/shard_map/ppermute | solution.py:145
  (116 other events, 1188.6 us)
Sparse Core Ops, SparseCore 0:
  12.1 37.3 all-gather.8
  51.6 105.9 all-gather.4
  159.2 58.2 all-gather.6
  336.9 74.2 reduce-scatter.1
